TPU v7x, 32 devices: a whole 2x2x4 slice. The times are simulated.
32 devices in a mesh: row: 4 (over z), col: 8 (over y, x, core).
Axes of the slice: x: 2, y: 2, z: 4, core: 2. Of those that a mesh axis runs over, the one named last changes fastest.
Arguments:
- token_ids: int32 [32, 1024], P(('row', 'col')), may hold values from 0 to 32783
- segment_ids: int32 [32, 1024], P(('row', 'col')), may hold values from 0 to 7, never falling along the last dimension, each value on 1 to 512 neighbouring positions
- loss_positions: int32 [32, 64], P(('row', 'col')), may hold values from 0 to 1023
- loss_targets: int32 [32, 64], P(('row', 'col')), may hold values from 0 to 32783
- loss_valid: int32 [32, 64], P(('row', 'col')), may hold values 0 or 1
- block_owner: int32 [48], replicated, may hold values from 0 to 47, each once
- step_count: int32 [1], replicated, may hold values from 1 to 20
- block_weights: float32 [48, 1024, 256], P('col', 'row'), may hold values from -0.1875 to 0.1875
- block_first: float32 [48, 1024, 256], P('col', 'row'), may hold values from -0.00015258789 to 0.00015258789
- block_second: float32 [48, 1024, 256], P('col', 'row'), may hold values from 1e-11 to 1e-09
- left_basis: float32 [48, 1024, 1024], P('col', 'row'), may hold values from -0.1875 to 0.1875
- right_basis: float32 [48, 256, 256], P('col'), may hold values from -0.375 to 0.375
- table: float32 [32784, 1024], P('col', 'row'), may hold values from -0.6875 to 0.6875
- table_first: float32 [32784, 1024], P('col', 'row'), may hold values from -0.00015258789 to 0.00015258789
- table_second: float32 [32784, 1024], P('col', 'row'), may hold values from 1e-11 to 1e-09
- vector_params: float32 [38216], replicated, may hold values from -7 to 3, as said below
- vector_first: float32 [38216], replicated, may hold values from -0.0014648438 to 0.0014648438
- vector_second: float32 [38216], replicated, may hold values from 1e-09 to 1e-07
Outputs:
- mean_loss: float32 [], replicated
- grad_norm: float32 [], replicated
- new_blocks: float32 [48, 1024, 256], P('col', 'row')
- new_block_first: float32 [48, 1024, 256], P('col', 'row')
- new_block_second: float32 [48, 1024, 256], P('col', 'row')
- new_table: float32 [32784, 1024], P('col', 'row')
- new_table_first: float32 [32784, 1024], P('col', 'row')
- new_table_second: float32 [32784, 1024], P('col', 'row')
- new_vectors: float32 [38216], replicated
- new_vector_first: float32 [38216], replicated
- new_vector_second: float32 [38216], replicated
Inputs may be any that keep to these rules, and one draw needn't show every extreme that they name: `segment_ids`: in each sequence the document number starts at 0, never falls and steps by one; each of the 8 documents holds 1 to 512 positions, one exactly 512. `block_owner`: A permutation of the slots. `vector_params`: Time-step biases are softplus inverses of values in 0.001 to 0.1; decay logarithms lie in 0 to log 16; gains lie in 0.5 to 1.5.
All inputs are finite; a program needn't handle non-finite values. No bound on the sum of `loss_valid` on one device may be relied on, other than what follows from the above.
Results may differ from a plain program's by a relative error of at most 0.013.
The roundings to bfloat16 on the way count: a program that leaves them out, or rounds other values in their place, can miss the bound.
Values may be sent and summed in bfloat16 or wider, within the bound.
A program may use at most 384 MiB of HBM per device.

v0:
```python
import jax
import jax.numpy as jnp
from jax import lax
from jax.sharding import PartitionSpec as P

D = 1024
HEADS = 8
KV_HEADS = 2
HEAD_DIM = 64
SSM_HEADS = 24
SSM_HEAD_DIM = 64
STATE = 128
CONV = 4
FF = 2048
BLOCK_COLS = 256
SSM_INNER = 1536
XBC_WIDTH = 1792
SPAN = 256
QBLOCK = 512


highest = lax.Precision.HIGHEST
rope_base = 100000000000.0
clip_limit = 1.0
learn_rate = 0.01
vector_rate = 0.08
weight_decay = 0.1
soap_first = 0.95
soap_second = 0.95
adam_first = 0.9
adam_second = 0.95
adam_eps = 1e-08


def merged(value, axis, combine):
    everything = jax.tree.map(lambda part: lax.all_gather(part, axis), value)
    leading = jax.tree.map(lambda part: part[0], everything)

    def step(k, so_far):
        return combine(so_far, jax.tree.map(lambda part: part[k], everything))

    return lax.fori_loop(1, lax.axis_size(axis), step, leading)


def rms_gain(values, gain_vec):
    inv_scale = lax.rsqrt(jnp.mean(values * values, axis=-1, keepdims=True) + 1e-05)
    return values * inv_scale * gain_vec


def swiglu(gate_val, up_val):
    return jax.nn.silu(gate_val) * up_val


def unpack(flattened):
    piece_sizes = [
        CONV * XBC_WIDTH,
        XBC_WIDTH,
        SSM_HEADS,
        SSM_HEADS,
        SSM_HEADS,
        SSM_INNER,
        3 * D,
        D * SSM_HEADS,
    ]
    pieces = []
    offset = 0
    for length in piece_sizes:
        pieces.append(flattened[offset : offset + length])
        offset = offset + length
    return pieces


def rope_table(length):
    half_dim = HEAD_DIM // 2
    frequency = rope_base ** (-jnp.arange(half_dim, dtype=jnp.float32) * 2.0 / HEAD_DIM)
    angles = jnp.arange(length, dtype=jnp.float32)[:, None] * frequency[None, :]
    return (jnp.cos(angles), jnp.sin(angles))


def rotate(values, cosine, sine_table):
    half_dim = values.shape[-1] // 2
    first_half = values[..., :half_dim]
    second_half = values[..., half_dim:]
    cos_wide = cosine[:, None, :]
    sin_wide = sine_table[:, None, :]
    return jnp.concatenate(
        [
            first_half * cos_wide - second_half * sin_wide,
            second_half * cos_wide + first_half * sin_wide,
        ],
        axis=-1,
    )


def attention_core(packed, segment):
    length = packed.shape[0]
    groups = HEADS // KV_HEADS
    queries = packed[:, : HEADS * HEAD_DIM].reshape(length, HEADS, HEAD_DIM)
    keys_all = packed[:, HEADS * HEAD_DIM : (HEADS + KV_HEADS) * HEAD_DIM].reshape(
        length, KV_HEADS, HEAD_DIM
    )
    values_all = packed[:, (HEADS + KV_HEADS) * HEAD_DIM :].reshape(length, KV_HEADS, HEAD_DIM)
    cosine, sine_table = rope_table(length)
    queries = rotate(queries, cosine, sine_table) * HEAD_DIM ** (-0.5)
    keys_all = rotate(keys_all, cosine, sine_table)
    nblocks = length // QBLOCK
    queries = queries.reshape(nblocks, QBLOCK, KV_HEADS, groups, HEAD_DIM)
    doc_blocks = segment.reshape(nblocks, QBLOCK)
    starts = jnp.arange(nblocks, dtype=jnp.int32) * QBLOCK
    positions = jnp.arange(length, dtype=jnp.int32)

    def one_block(inputs):
        query_block, doc_block, start_row = inputs
        scores = jnp.einsum("qkgd,skd->kgqs", query_block, keys_all, precision=highest)
        row_pos = start_row + jnp.arange(QBLOCK, dtype=jnp.int32)
        allowed = (doc_block[:, None] == segment[None, :]) & (
            row_pos[:, None] >= positions[None, :]
        )
        scores = jnp.where(allowed, scores, -1e30)
        row_top = jnp.max(scores, axis=-1, keepdims=True)
        weights = jnp.where(allowed, jnp.exp(scores - row_top), 0.0)
        row_total = jnp.sum(weights, axis=-1, keepdims=True)
        return jnp.einsum("kgqs,skd->qkgd", weights / row_total, values_all, precision=highest)

    blocks = lax.map(jax.checkpoint(one_block), (queries, doc_blocks, starts))
    return blocks.reshape(length, HEADS * HEAD_DIM)


def ssd_scan(heads_in, step_size, decay_rate, input_map, output_map, segment):
    length = heads_in.shape[0]
    nspans = length // SPAN

    def span_step(carry_in, inputs):
        carry_state, carry_doc = carry_in
        heads_block, step_block, input_block, output_block, doc_block = inputs
        cum_decay = jnp.cumsum(step_block * decay_rate[None, :], axis=0)
        causal = jnp.arange(SPAN)[:, None] >= jnp.arange(SPAN)[None, :]
        same_doc = ((doc_block[:, None] == doc_block[None, :]) & causal)[:, :, None]
        cum_gaps = cum_decay[:, None, :] - cum_decay[None, :, :]
        decay_mat = jnp.where(same_doc, jnp.exp(jnp.where(same_doc, cum_gaps, 0.0)), 0.0)
        inner_bc = jnp.einsum("tn,sn->ts", output_block, input_block, precision=highest)
        mixing = decay_mat * (inner_bc[:, :, None] * step_block[None, :, :])
        result = jnp.einsum("tsh,shp->thp", mixing, heads_block, precision=highest)
        carried = (doc_block == carry_doc).astype(jnp.float32)[:, None] * jnp.exp(cum_decay)
        result = result + carried[:, :, None] * jnp.einsum(
            "tn,hpn->thp", output_block, carry_state, precision=highest
        )
        last_doc = doc_block[SPAN - 1]
        tail_weight = (
            jnp.where(
                (doc_block == last_doc)[:, None],
                jnp.exp(cum_decay[SPAN - 1][None, :] - cum_decay),
                0.0,
            )
            * step_block
        )
        keep_old = (carry_doc == last_doc).astype(jnp.float32) * jnp.exp(cum_decay[SPAN - 1])
        fresh_state = jnp.einsum(
            "sh,shp,sn->hpn", tail_weight, heads_block, input_block, precision=highest
        )
        return ((keep_old[:, None, None] * carry_state + fresh_state, last_doc), result)

    initial = (jnp.zeros((SSM_HEADS, SSM_HEAD_DIM, STATE), jnp.float32), jnp.array(-1, jnp.int32))
    spanned = (
        heads_in.reshape(nspans, SPAN, SSM_HEADS, SSM_HEAD_DIM),
        step_size.reshape(nspans, SPAN, SSM_HEADS),
        input_map.reshape(nspans, SPAN, STATE),
        output_map.reshape(nspans, SPAN, STATE),
        segment.reshape(nspans, SPAN),
    )
    _, outputs = lax.scan(jax.checkpoint(span_step), initial, spanned)
    return outputs.reshape(length, SSM_HEADS, SSM_HEAD_DIM)


def mixer_core(
    projected,
    time_raw,
    conv_weight,
    conv_bias,
    time_bias,
    decay_log,
    skip_gain,
    mixer_gain,
    segment,
):
    length = projected.shape[0]
    gate_part = projected[:, :SSM_INNER]
    conv_in = projected[:, SSM_INNER:]
    kernel = conv_weight.reshape(CONV, XBC_WIDTH)
    conv_sum = jnp.zeros_like(conv_in) + conv_bias[None, :]
    for offset in range(CONV):
        shift_by = CONV - 1 - offset
        shifted = jnp.pad(conv_in, ((shift_by, 0), (0, 0)))[:length]
        doc_shift = jnp.pad(segment, (shift_by, 0), constant_values=-1)[:length]
        same_doc = (doc_shift == segment).astype(jnp.float32)[:, None]
        conv_sum = conv_sum + kernel[offset][None, :] * shifted * same_doc
    activated = jax.nn.silu(conv_sum)
    heads_in = activated[:, :SSM_INNER].reshape(length, SSM_HEADS, SSM_HEAD_DIM)
    input_map = activated[:, SSM_INNER : SSM_INNER + STATE]
    output_map = activated[:, SSM_INNER + STATE :]
    step_size = jax.nn.softplus(time_raw + time_bias[None, :])
    decay_rate = -jnp.exp(decay_log)
    output = ssd_scan(heads_in, step_size, decay_rate, input_map, output_map, segment)
    output = output + skip_gain[None, :, None] * heads_in
    gated = output.reshape(length, SSM_INNER) * jax.nn.silu(gate_part)
    return rms_gain(gated, mixer_gain)


def project(left_rows, blocks):
    return jnp.einsum("td,kdb->tkb", left_rows, blocks, preferred_element_type=jnp.float32).reshape(
        left_rows.shape[0], -1
    )


def project_back(right_cols, blocks):
    shaped = right_cols.reshape(right_cols.shape[0], blocks.shape[0], blocks.shape[2])
    return jnp.einsum("tkb,kdb->td", shaped, blocks, preferred_element_type=jnp.float32)


def weight_grad(left_rows, right_cols):
    shaped = right_cols.reshape(right_cols.shape[0], -1, BLOCK_COLS)
    return jnp.einsum("td,tkb->kdb", left_rows, shaped, preferred_element_type=jnp.float32)


def combine_softmax(former, latter):
    row_top = jnp.maximum(former[0], latter[0])
    row_total = former[1] * jnp.exp(former[0] - row_top) + latter[1] * jnp.exp(latter[0] - row_top)
    return (row_top, row_total, former[2] + latter[2])


def adam_step(weights, grads, first, second, steps_done, decay, rate):
    first_new = adam_first * first + (1.0 - adam_first) * grads
    second_new = adam_second * second + (1.0 - adam_second) * grads * grads
    direction = (
        first_new
        / (1.0 - adam_first**steps_done)
        / (jnp.sqrt(second_new / (1.0 - adam_second**steps_done)) + adam_eps)
    )
    return (weights - rate * (direction + decay * weights), first_new, second_new)


def body(
    token_ids,
    segment_ids,
    loss_positions,
    loss_targets,
    loss_valid,
    block_owner,
    step_count,
    block_weights,
    block_first,
    block_second,
    left_basis,
    right_basis,
    table,
    table_first,
    table_second,
    vector_params,
    vector_first,
    vector_second,
):
    col_index = lax.axis_index("col")
    tokens = token_ids[0]
    segment = segment_ids[0]
    length = tokens.shape[0]
    in_cols = 2 * SSM_INNER + 2 * STATE
    first_end = (in_cols + (HEADS + 2 * KV_HEADS) * HEAD_DIM) // BLOCK_COLS
    second_end = first_end + (SSM_INNER + HEADS * HEAD_DIM) // BLOCK_COLS
    third_end = second_end + 2 * FF // BLOCK_COLS
    table_low = table.astype(jnp.bfloat16)
    blocks_cols, table_cols = (
        lax.all_gather(block_weights.astype(jnp.bfloat16), "col", axis=0, tiled=True),
        lax.all_gather(table_low, "col", axis=0, tiled=True),
    )
    blocks_all, table_rows, tokens_rows = (
        lax.all_gather(blocks_cols, "row", axis=1, tiled=True),
        lax.all_gather(table_low, "row", axis=1, tiled=True),
        lax.all_gather(token_ids, "row", axis=0, tiled=True),
    )
    logical = jnp.take(blocks_all, block_owner, axis=0)
    in_blocks = logical[:first_end]
    branch_blocks = logical[first_end:second_end]
    gate_blocks = logical[second_end:third_end]
    down_blocks = logical[third_end:]
    token_list = tokens_rows.reshape(-1)
    looked_up = jnp.take(table_cols, token_list, axis=0)
    embedded = lax.all_to_all(looked_up, "row", split_axis=0, concat_axis=1, tiled=True)
    conv_weight, conv_bias, time_bias, decay_log, skip_gain, mixer_gain, norm_gains, time_proj = (
        unpack(vector_params)
    )
    gain_rows = norm_gains.reshape(3, D)
    time_low = time_proj.reshape(D, SSM_HEADS).astype(jnp.bfloat16)
    embed_wide = embedded.astype(jnp.float32)
    normed_wide, first_norm_back = jax.vjp(rms_gain, embed_wide, gain_rows[0])
    normed = normed_wide.astype(jnp.bfloat16)
    both_proj = project(normed, in_blocks)
    projected = both_proj[:, :in_cols]
    packed = both_proj[:, in_cols:]
    time_raw = jnp.dot(normed, time_low, preferred_element_type=jnp.float32)

    def mixer_local(
        projected_in, time_in, conv_in, bias_in, time_bias_in, decay_in, skip_in, gain_in
    ):
        return mixer_core(
            projected_in,
            time_in,
            conv_in,
            bias_in,
            time_bias_in,
            decay_in,
            skip_in,
            gain_in,
            segment,
        )

    mixer_out, mixer_back = jax.vjp(
        mixer_local,
        projected,
        time_raw,
        conv_weight,
        conv_bias,
        time_bias,
        decay_log,
        skip_gain,
        mixer_gain,
    )

    def attention_local(packed_in):
        return attention_core(packed_in, segment)

    context, attention_back = jax.vjp(attention_local, packed)
    branch_in = jnp.concatenate([mixer_out, context], axis=1).astype(jnp.bfloat16)
    hidden_one = embed_wide + project_back(branch_in, branch_blocks)
    second_wide, second_norm_back = jax.vjp(rms_gain, hidden_one, gain_rows[1])
    normed_two = second_wide.astype(jnp.bfloat16)
    gate_up = project(normed_two, gate_blocks)
    activated, swiglu_back = jax.vjp(swiglu, gate_up[:, :FF], gate_up[:, FF:])
    act_low = activated.astype(jnp.bfloat16)
    hidden_two = hidden_one + project_back(act_low, down_blocks)
    final_wide, final_norm_back = jax.vjp(rms_gain, hidden_two, gain_rows[2])
    final_out = final_wide.astype(jnp.bfloat16)
    positions = loss_positions[0]
    count_rows = positions.shape[0]
    picked_rows = jnp.take(final_out, positions, axis=0)
    rows_all, targets_all, valid_all = (
        lax.all_gather(picked_rows, "col", axis=0, tiled=True),
        lax.all_gather(loss_targets[0], "col", axis=0, tiled=True),
        lax.all_gather(loss_valid[0], "col", axis=0, tiled=True),
    )
    logits = jnp.einsum("rd,vd->rv", rows_all, table_rows, preferred_element_type=jnp.float32)
    shard_rows = table_rows.shape[0]
    local_target = targets_all - col_index * shard_rows
    onehot = jnp.arange(shard_rows, dtype=jnp.int32)[None, :] == local_target[:, None]
    row_top = jnp.max(logits, axis=1)
    row_total = jnp.sum(jnp.exp(logits - row_top[:, None]), axis=1)
    target_logit = jnp.sum(jnp.where(onehot, logits, 0.0), axis=1)
    top_all, total_all, target_all = merged(
        (row_top, row_total, target_logit), "col", combine_softmax
    )
    log_total = top_all + jnp.log(total_all)
    valid_wide = valid_all.astype(jnp.float32)
    own_loss = lax.dynamic_slice_in_dim(
        (log_total - target_all) * valid_wide, col_index * count_rows, count_rows
    )
    own_valid = lax.dynamic_slice_in_dim(valid_wide, col_index * count_rows, count_rows)
    loss_sum, valid_count = lax.psum((jnp.sum(own_loss), jnp.sum(own_valid)), ("row", "col"))
    mean_loss = loss_sum / valid_count
    logit_grad = (
        (jnp.exp(logits - log_total[:, None]) - onehot.astype(jnp.float32))
        * (valid_wide / valid_count)[:, None]
    ).astype(jnp.bfloat16)
    rows_grad = lax.psum_scatter(
        jnp.einsum("rv,vd->rd", logit_grad, table_rows, preferred_element_type=jnp.float32),
        "col",
        scatter_dimension=0,
        tiled=True,
    )
    table_loss_grad = jnp.einsum(
        "rv,rd->vd", logit_grad, rows_all, preferred_element_type=jnp.float32
    )
    final_grad = jnp.zeros((length, D), jnp.float32).at[positions].add(rows_grad)
    hidden_two_grad, gain_final_grad = final_norm_back(final_grad)
    down_in = hidden_two_grad.astype(jnp.bfloat16)
    act_grad = project(down_in, down_blocks)
    grad_down = weight_grad(down_in, act_low)
    gate_grad, up_grad = swiglu_back(act_grad)
    gate_up_grad = jnp.concatenate([gate_grad, up_grad], axis=1).astype(jnp.bfloat16)
    grad_gate_up = weight_grad(normed_two, gate_up_grad)
    normed_two_grad = project_back(gate_up_grad, gate_blocks)
    hidden_one_part, gain_ff_grad = second_norm_back(normed_two_grad)
    hidden_one_grad = hidden_two_grad + hidden_one_part
    branch_grad_low = hidden_one_grad.astype(jnp.bfloat16)
    branch_out_grad = project(branch_grad_low, branch_blocks)
    grad_branch = weight_grad(branch_grad_low, branch_in)
    mixer_grads = mixer_back(branch_out_grad[:, :SSM_INNER])
    (packed_grad,) = attention_back(branch_out_grad[:, SSM_INNER:])
    in_grad_low = jnp.concatenate([mixer_grads[0], packed_grad], axis=1).astype(jnp.bfloat16)
    time_grad_low = mixer_grads[1].astype(jnp.bfloat16)
    grad_in = weight_grad(normed, in_grad_low)
    grad_time = jnp.einsum("td,th->dh", normed, time_grad_low, preferred_element_type=jnp.float32)
    normed_grad = project_back(in_grad_low, in_blocks) + jnp.einsum(
        "th,dh->td", time_grad_low, time_low, preferred_element_type=jnp.float32
    )
    embed_part, gain_in_grad = first_norm_back(normed_grad)
    embed_grad = (hidden_one_grad + embed_part).astype(jnp.bfloat16)
    embed_grad_rows = lax.all_to_all(embed_grad, "row", split_axis=1, concat_axis=0, tiled=True)
    grads_tokens, tokens_all = (
        lax.all_gather(embed_grad_rows, "col", axis=0, tiled=True),
        lax.all_gather(token_list, "col", axis=0, tiled=True),
    )
    local_tokens = tokens_all - col_index * shard_rows
    inside = (local_tokens >= 0) & (local_tokens < shard_rows)
    segment_index = jnp.where(inside, local_tokens, shard_rows)
    table_input_grad = jax.ops.segment_sum(
        grads_tokens.astype(jnp.float32), segment_index, num_segments=shard_rows + 1
    )[:shard_rows]
    grad_logical = jnp.concatenate([grad_in, grad_branch, grad_gate_up, grad_down], axis=0)
    nblocks = block_owner.shape[0]
    inverse = (
        jnp.zeros((nblocks,), jnp.int32).at[block_owner].set(jnp.arange(nblocks, dtype=jnp.int32))
    )
    grad_slots = jnp.take(grad_logical, inverse, axis=0)
    grad_owned = lax.psum_scatter(grad_slots, "col", scatter_dimension=0, tiled=True)
    grad_mine, table_loss_mine = (
        lax.psum_scatter(grad_owned, "row", scatter_dimension=1, tiled=True),
        lax.psum_scatter(table_loss_grad, "row", scatter_dimension=1, tiled=True),
    )
    table_grad = table_loss_mine + table_input_grad
    vector_grad = jnp.concatenate(
        [
            mixer_grads[2],
            mixer_grads[3],
            mixer_grads[4],
            mixer_grads[5],
            mixer_grads[6],
            mixer_grads[7],
            gain_in_grad,
            gain_ff_grad,
            gain_final_grad,
            grad_time.reshape(-1),
        ]
    )
    square_part = jnp.sum(grad_mine * grad_mine) + jnp.sum(table_grad * table_grad)
    vector_total, square_total = lax.psum((vector_grad, square_part), ("row", "col"))
    grad_norm = jnp.sqrt(square_total + jnp.sum(vector_total * vector_total))
    clip_scale = jnp.minimum(1.0, clip_limit / (grad_norm + 1e-06))
    steps_done = step_count[0].astype(jnp.float32)
    grad_whole = lax.all_gather(grad_mine, "row", axis=1, tiled=True) * clip_scale
    rotated = jnp.einsum("sid,sdb->sib", left_basis, grad_whole, precision=highest)
    rotated = jnp.einsum("sib,sbc->sic", rotated, right_basis, precision=highest)
    first_new = soap_first * block_first + (1.0 - soap_first) * rotated
    second_new = soap_second * block_second + (1.0 - soap_second) * rotated * rotated
    direction = (
        first_new
        / (1.0 - soap_first**steps_done)
        / (jnp.sqrt(second_new / (1.0 - soap_second**steps_done)) + adam_eps)
    )
    turned = jnp.einsum("sic,sbc->sib", direction, right_basis, precision=highest)
    partial_update = jnp.einsum("sid,sib->sdb", left_basis, turned, precision=highest)
    update = lax.psum_scatter(partial_update, "row", scatter_dimension=1, tiled=True)
    new_blocks = block_weights - learn_rate * (update + weight_decay * block_weights)
    new_table, table_first_new, table_second_new = adam_step(
        table,
        table_grad * clip_scale,
        table_first,
        table_second,
        steps_done,
        weight_decay,
        learn_rate,
    )
    new_vectors, vector_first_new, vector_second_new = adam_step(
        vector_params,
        vector_total * clip_scale,
        vector_first,
        vector_second,
        steps_done,
        0.0,
        vector_rate,
    )
    return (
        mean_loss,
        grad_norm,
        new_blocks,
        first_new,
        second_new,
        new_table,
        table_first_new,
        table_second_new,
        new_vectors,
        vector_first_new,
        vector_second_new,
    )


def solution(mesh):
    placed = (
        P(("row", "col"), None),
        P(("row", "col"), None),
        P(("row", "col"), None),
        P(("row", "col"), None),
        P(("row", "col"), None),
        P(),
        P(),
        P("col", "row", None),
        P("col", "row", None),
        P("col", "row", None),
        P("col", "row", None),
        P("col", None, None),
        P("col", "row"),
        P("col", "row"),
        P("col", "row"),
        P(),
        P(),
        P(),
    )
    return jax.shard_map(
        body,
        mesh=mesh,
        in_specs=placed,
        out_specs=(
            P(),
            P(),
            P("col", "row", None),
            P("col", "row", None),
            P("col", "row", None),
            P("col", "row"),
            P("col", "row"),
            P("col", "row"),
            P(),
            P(),
            P(),
        ),
        check_vma=False,
    )
```

profile of v0, /device:TPU:0, one launch (start us, length us, event | category | flops | bytes accessed | tf_op | source)
XLA Modules:
  0.0 3418.7 jit_solution(12527470356338616038)
XLA Ops:
  13.6 45.1 %all-gather.18.cloned.1.call-done = bf16[48,256,256]{2,1,0:T(8,128)(2,1)} async-done(((bf16[6,256,256]{2,1,0:T(8,128)(2,1)}), bf16[48,256,256]{2,1,0:T(8,128)(2,1)}) %all-gather.18.cloned.1.call-update) | async-done | bytes 6291472 | tf_op jit(solution)/shard_map/all_gather | solution.py:272
  72.6 78.6 %all-gather.30.cloned.1.call-done = bf16[8,4098,256]{2,1,0:T(8,128)(2,1)} async-done(((bf16[1,4098,256]{2,1,0:T(8,128)(2,1)}), bf16[8,4098,256]{2,1,0:T(8,128)(2,1)}) %all-gather.30.cloned.1.call-update) | async-done | bytes 16785424 | tf_op jit(solution)/shard_map/all_gather | solution.py:273
  171.7 25.3 gather_fusion
  221.9 86.1 %all-to-all-done = bf16[4,1024,256]{1,2,0:T(8,128)(2,1)} async-done(((bf16[4,1024,256]{1,2,0:T(8,128)(2,1)}), bf16[4,1024,256]{1,2,0:T(8,128)(2,1)}, u32[]{:S(2)}, u32[]{:S(2)}) %all-to-all-start) | async-done | bytes 2097184 | tf_op jit(solution)/shard_map/all_to_all | solution.py:287
  315.3 307.6 %all-gather.20.cloned.1.call-done = bf16[48,1024,256]{2,1,0:T(8,128)(2,1)} async-done(((bf16[48,256,256]{2,1,0:T(8,128)(2,1)}), bf16[48,1024,256]{2,1,0:T(8,128)(2,1)}) %all-gather.20.cloned.1.call-update) | async-done | bytes 25165840 | tf_op jit(solution)/shard_map/all_gather | solution.py:276
  744.5 100.2 %while.98 = (s32[]{:T(128)}, f32[24,64,128]{2,1,0:T(8,128)S(1)}, s32[]{:T(128)}, f32[4,256,24,64]{1,3,2,0:T(8,128)}, f32[4,24,64,128]{3,2,1,0:T(8,128)}, /*index...) while((s32[]{:T(128)}, f32[24,64,128]{2,1,0:T(8,128)S(1)}, ...), condition=%wide.region_4.5_spmd.clone, body=%wide.region_1.4_spmd.clone.sunk | while | flops 2527630336 | bytes 13432215 | solution.py:171
  865.8 123.7 %while.97 = (s32[]{:T(128)}, bf16[2,512,2,4,64]{1,4,3,2,0:T(8,128)(2,1)}, s32[2,512]{1,0:T(2,128)S(1)}, s32[1,1024]{1,0:T(1,128)S(1)}, s32[2]{0:T(128)S(1)}, /*i...) while((s32[]{:T(128)}, ...), condition=%wide.region_9.10_spmd.clone, body=%wide.region_6.9_spmd.clone.sunk | while | flops 6469191168 | bytes 73448592 | solution.py:125
  1098.5 37.2 %psum.29 = f32[]{:T(128)} all-reduce(f32[]{:T(128)} %dynamic-slice_reduce_fusion), channel_id=1, replica_groups=mesh['row'=4,'col'=8] {'row','col'}, use_global_device_ids=true, to_apply=%region_20.21 | all-reduce | flops 1 | bytes 8 | tf_op jit(solution)/shard_map/psum | solution.py:366
  1191.4 39.0 %reduce-scatter.6.cloned.1.call-done = f32[64,1024]{1,0:T(8,128)} async-done(((f32[512,1024]{1,0:T(8,128)}), f32[64,1024]{1,0:T(8,128)}) %reduce-scatter.6.cloned.1.call-update) | async-done | bytes 262160 | tf_op jit(solution)/shard_map/reduce_scatter | solution.py:372
  1403.0 252.8 %while.99 = (s32[]{:T(128)}, f32[24]{0:T(128)}, f32[24,64,128]{2,1,0:T(8,128)}, f32[4,256,24,64]{1,3,2,0:T(8,128)}, f32[4,256,24]{1,0,2:T(4,128)}, /*index=5*/f3...) while((s32[]{:T(128)}, f32[24]{0:T(128)}, ...), condition=%wide.region_40.41_spmd.clone, body=%wide.region_27.40_spmd.clone.sunk | while | flops 5775729664 | bytes 57208524 | solution.py:171
  1717.8 326.6 %while.100 = (s32[]{:T(128)}, f32[1024,2,64]{0,2,1:T(8,128)}, f32[1024,2,64]{0,2,1:T(8,128)}, f32[2,512,2,4,64]{1,0,4,3,2:T(2,128)}, f32[2,512,2,4,64]{1,4,3,2,0...) while((s32[]{:T(128)}, f32[1024,2,64]{0,2,1:T(8,128)}, ...), condition=%wide.region_47.48_spmd.clone, body=%wide.region_41.47_spmd.clone.sunk | while | flops 16260792320 | bytes 351193472 | solution.py:125
  1904.2 23.5 multiply_reduce_fusion.31
  2095.6 29.4 pad_maximum_fusion
  2125.0 34.0 gather_fusion.3
  2159.0 36.5 %broadcast_select_fusion.2 = f32[48,1024,256]{1,2,0:T(8,128)} fusion(f32[48,1024,256]{1,2,0:T(8,128)} %gather_fusion.3, pred[48]{0:T(512)(128)(4,1)S(1)} %copy-done.126), kind=kLoop, calls=%fused_computation.233 | loop fusion | flops 12582912 | bytes 100663344 | tf_op jit(solution)/shard_map/jit(_take)/select_n | solution.py:422
  2195.7 285.9 %reduce-scatter.8.cloned.1.call-done = f32[6,1024,256]{1,2,0:T(8,128)} async-done(((f32[48,1024,256]{1,2,0:T(8,128)}), f32[6,1024,256]{1,2,0:T(8,128)}) %reduce-scatter.8.cloned.1.call-update) | async-done | bytes 6291472 | tf_op jit(solution)/shard_map/reduce_scatter | solution.py:423
  2517.0 109.8 %all_to_all.29 = bf16[1024,4,256]{0,2,1:T(8,128)(2,1)} all-to-all(bf16[1024,4,256]{0,2,1:T(8,128)(2,1)S(1)} %bitcast.755), channel_id=1, replica_groups=mesh['row'=4,'col'=8] {'row'}, dimensions={1} | all-to-all | bytes 4194304 | tf_op jit(solution)/shard_map/all_to_all | solution.py:406
  2658.9 72.6 %all-gather.26.cloned.1.call-done = bf16[32768,256]{1,0:T(8,128)(2,1)} async-done(((bf16[4096,256]{1,0:T(8,128)(2,1)}), bf16[32768,256]{1,0:T(8,128)(2,1)}) %all-gather.26.cloned.1.call-update) | async-done | bytes 16777232 | tf_op jit(solution)/shard_map/all_gather | solution.py:408
  2731.5 210.6 %scatter_custom_fusion.2 = f32[4099,256]{1,0:T(8,128)} fusion(s32[32768]{0:T(1024)S(1)} %and_select_fusion, bf16[32768,256]{1,0:T(8,128)(2,1)} %all-gather.26.cloned.1.call-done, f32[]{:T(128)} %constant.378.clone.1), kind=kCustom, calls=%fused_computation.231 | custom fusion | flops 16777216 | bytes 20974596 | tf_op jit(solution)/shard_map/scatter-add | solution.py:414
  2942.0 71.6 %reduce-scatter.12.cloned.1.call-done = f32[4098,256]{1,0:T(8,128)} async-done(((f32[4098,1024]{1,0:T(8,128)}), f32[4098,256]{1,0:T(8,128)}) %reduce-scatter.12.cloned.1.call-update) | async-done | bytes 4196368 | tf_op jit(solution)/shard_map/reduce_scatter | solution.py:426
  3021.1 122.2 %all-reduce.33.cloned.1.call-done = f32[38216]{0:T(1024)} async-done(((f32[38216]{0:T(1024)}), f32[38216]{0:T(1024)}) %all-reduce.33.cloned.1.call-update) | async-done | bytes 152880 | tf_op jit(solution)/shard_map/psum | solution.py:444
  3144.9 51.0 %all-reduce.30 = (f32[]{:T(128)}, f32[]{:T(128)}) all-reduce(f32[]{:T(128)} %dynamic-slice_reduce_fusion.1, f32[]{:T(128)S(6)} %add.482), channel_id=1, replica_groups=mesh['row'=4,'col'=8] {'row','col'}, use_global_device_ids=true, to_apply=%region_18.19 | all-reduce | flops 2 | bytes 16 | tf_op jit(solution)/shard_map/psum | solution.py:366
  3197.2 66.0 %all-gather.28.cloned.1.call-done = f32[6,1024,256]{1,2,0:T(8,128)} async-done(((f32[6,256,256]{1,2,0:T(8,128)}), f32[6,1024,256]{1,2,0:T(8,128)}) %all-gather.28.cloned.1.call-update) | async-done | bytes 6291472 | tf_op jit(solution)/shard_map/all_gather | solution.py:448
  3314.0 89.6 %reduce-scatter.14.cloned.1.call-done = f32[6,256,256]{1,2,0:T(8,128)} async-done(((f32[6,1024,256]{1,2,0:T(8,128)}), f32[6,256,256]{1,2,0:T(8,128)}) %reduce-scatter.14.cloned.1.call-update) | async-done | bytes 1572880 | tf_op jit(solution)/shard_map/reduce_scatter | solution.py:460
  (989 shorter events, 1551.8 us)
Async XLA Ops:
  7.2 3273.7 %copy-start = (f32[6,256,256]{2,1,0:T(8,128)S(1)}, f32[6,256,256]{2,1,0:T(8,128)}, u32[]{:S(2)}) copy-start(f32[6,256,256]{2,1,0:T(8,128)} %param.39) | copy-start | bytes 4718596
  7.2 51.5 %all-gather.18.cloned.1.call-start = ((), (), s32[]{:S(2)}) async-start(), calls=%async_computation.7 | async-start | bytes 7077888 | tf_op jit(solution)/shard_map/all_gather | solution.py:272
  9.8 141.5 %all-gather.30.cloned.1.call-start = ((), (), s32[]{:S(2)}) async-start(), calls=%async_computation.19 | async-start | bytes 18911232 | tf_op jit(solution)/shard_map/all_gather | solution.py:273
  13.5 609.4 %all-gather.20.cloned.1.call-start = ((), (), s32[]{:S(2)}) async-start(), calls=%async_computation.8 | async-start | bytes 31457280 | tf_op jit(solution)/shard_map/all_gather | solution.py:276
  204.0 104.0 %all-to-all-start = ((bf16[4,1024,256]{1,2,0:T(8,128)(2,1)}), bf16[4,1024,256]{1,2,0:T(8,128)(2,1)}, u32[]{:S(2)}, u32[]{:S(2)}) async-start(bf16[4,1024,256]{1,2,0:T(8,128)(2,1)} %broadcast_select_fusion.4), calls=%async_computation | async-start | bytes 4194304 | tf_op jit(solution)/shard_map/all_to_all | solution.py:287
  208.7 927.1 %all-gather.24.cloned.1.call-start = ((), (), s32[]{:S(2)}) async-start(), calls=%async_computation.10 | async-start | bytes 10506240 | tf_op jit(solution)/shard_map/all_gather | solution.py:277
  212.5 923.3 %all-gather.22.cloned.1.call-start = ((), (), s32[]{:S(2)}) async-start(), calls=%async_computation.9 | async-start | bytes 1179648 | tf_op jit(solution)/shard_map/all_gather | solution.py:346
  215.0 427.3 %copy-start.37 = (bf16[1024,24]{1,0:T(8,128)(2,1)}, bf16[1024,24]{1,0:T(8,128)(2,1)S(1)}, u32[]{:S(2)}) copy-start(bf16[1024,24]{1,0:T(8,128)(2,1)S(1)} %convert_element_type.169) | copy-start | bytes 147460
  220.6 482.6 %copy-start.89 = (f32[1024]{0:T(1024)}, f32[1024]{0:T(1024)S(1)}, u32[]{:S(2)}) copy-start(f32[1024]{0:T(1024)S(1)} %get-tuple-element.1754) | copy-start | bytes 12292
  220.6 482.6 %copy-start.91 = (f32[1024]{0:T(1024)}, f32[1024]{0:T(1024)S(1)}, u32[]{:S(2)}) copy-start(f32[1024]{0:T(1024)S(1)} %get-tuple-element.1755) | copy-start | bytes 12292
  220.6 482.6 %copy-start.93 = (f32[1024]{0:T(1024)}, f32[1024]{0:T(1024)S(1)}, u32[]{:S(2)}) copy-start(f32[1024]{0:T(1024)S(1)} %get-tuple-element.1756) | copy-start | bytes 12292
  220.6 482.6 %copy-start.78 = (f32[1792]{0:T(1024)}, f32[1792]{0:T(1024)S(1)}, u32[]{:S(2)}) copy-start(f32[1792]{0:T(1024)S(1)} %get-tuple-element.1750) | copy-start | bytes 21508
  220.6 482.6 %copy-start.80 = (f32[1792]{0:T(1024)}, f32[1792]{0:T(1024)S(1)}, u32[]{:S(2)}) copy-start(f32[1792]{0:T(1024)S(1)} %get-tuple-element.1751) | copy-start | bytes 21508
  220.6 482.6 %copy-start.82 = (f32[1792]{0:T(1024)}, f32[1792]{0:T(1024)S(1)}, u32[]{:S(2)}) copy-start(f32[1792]{0:T(1024)S(1)} %get-tuple-element.1752) | copy-start | bytes 21508
  220.6 482.6 %copy-start.84 = (f32[1792]{0:T(1024)}, f32[1792]{0:T(1024)S(1)}, u32[]{:S(2)}) copy-start(f32[1792]{0:T(1024)S(1)} %get-tuple-element.1753) | copy-start | bytes 21508
  1088.5 141.8 %reduce-scatter.6.cloned.1.call-start = ((), (), s32[]{:S(2)}) async-start(), calls=%async_computation.11 | async-start | bytes 2359296 | tf_op jit(solution)/shard_map/reduce_scatter | solution.py:372
  1189.3 1292.3 %reduce-scatter.8.cloned.1.call-start = ((), (), s32[]{:S(2)}) async-start(), calls=%async_computation.12 | async-start | bytes 56623104 | tf_op jit(solution)/shard_map/reduce_scatter | solution.py:423
  1717.8 326.6 %copy-start.36 = (f32[1024,32]{0,1:T(8,128)S(1)}, f32[1024,32]{0,1:T(8,128)}, u32[]{:S(2)}) copy-start(f32[1024,32]{0,1:T(8,128)} %get-tuple-element.1759) | copy-start | bytes 393220
  2195.6 451.4 %reduce-scatter.10.cloned.1.call-start = ((), (), s32[]{:S(2)}) async-start(), calls=%async_computation.13 | async-start | bytes 7864320 | tf_op jit(solution)/shard_map/reduce_scatter | solution.py:425
  2481.6 249.8 %all-gather.26.cloned.1.call-start = ((), (), s32[]{:S(2)}) async-start(), calls=%async_computation.15 | async-start | bytes 18874368 | tf_op jit(solution)/shard_map/all_gather | solution.py:408
  2630.8 382.8 %reduce-scatter.12.cloned.1.call-start = ((), (), s32[]{:S(2)}) async-start(), calls=%async_computation.14 | async-start | bytes 21012480 | tf_op jit(solution)/shard_map/reduce_scatter | solution.py:426
  2643.0 500.3 %all-reduce.33.cloned.1.call-start = ((), (), s32[]{:S(2)}) async-start(), calls=%async_computation.16 | async-start | bytes 311296 | tf_op jit(solution)/shard_map/psum | solution.py:444
  2646.9 616.3 %all-gather.28.cloned.1.call-start = ((), (), s32[]{:S(2)}) async-start(), calls=%async_computation.17 | async-start | bytes 7864320 | tf_op jit(solution)/shard_map/all_gather | solution.py:448
  2647.5 756.1 %reduce-scatter.14.cloned.1.call-start = ((), (), s32[]{:S(2)}) async-start(), calls=%async_computation.18 | async-start | bytes 7864320 | tf_op jit(solution)/shard_map/reduce_scatter | solution.py:460
  (199 other events, 4433.5 us)
Sparse Core Ops, SparseCore 0:
  10.5 48.2 all-gather.17
  61.2 89.9 all-gather.29
  152.8 470.0 all-gather.19
  624.3 147.5 all-gather.23
  1088.6 21.4 all-gather.21
  1189.4 40.8 reduce-scatter.5
  2195.7 285.8 reduce-scatter.7
  2483.9 144.4 reduce-scatter.9
  2630.9 100.5 all-gather.25
  2733.7 279.8 reduce-scatter.11
  3020.7 122.6 all-reduce.32
  3144.8 118.3 all-gather.27
  3294.6 108.9 reduce-scatter.13
where the time goes:
time: 3440 us; the launch traced here: 3420 us
  waiting for transfers between devices  1270 us (37%)
  matrix products  691 us (20%)
  other arithmetic  685 us (20%)
  local copies, waits for them, and re-layouts  461 us (13%)
  blocking collectives  255 us (7%)
    all_gather x1, waiting for transfers between devices, body(): lax.all_gather(blocks_cols, 'row', axis=1, tiled=True)  308 us
    reduce_scatter x1, waiting for transfers between devices, body(): lax.psum_scatter(grad_slots, 'col', scatter_dimension=0, tiled=True)  286 us
    scatter-add x1, other arithmetic, body(): jax.ops.segment_sum(grads_tokens.astype(jnp.float32), segment_index, num_...  211 us
    dot_general x8, matrix products, one_block(): jnp.einsum('qkgd,skd->kgqs', query_block, keys_all, precision=highest)  135 us
    dot_general x6, matrix products, one_block(): jnp.einsum('kgqs,skd->qkgd', weights / row_total, values_all, precision=h...  127 us
    psum x1, waiting for transfers between devices, body(): lax.psum((vector_grad, square_part), ('row', 'col'))  122 us
    dot_general x12, matrix products, span_step(): result = jnp.einsum('tsh,shp->thp', mixing, heads_block, precision=highest)  114 us
    all_to_all x1, blocking collectives, body(): lax.all_to_all(embed_grad, 'row', split_axis=1, concat_axis=0, tiled=True)  110 us
  transfers between devices with their start and end apart: 14, of which 11 were waited for; matrix products, arithmetic and copies ran while one was open for 24% of the time, Pallas kernels for 0%

commit v1 on v0

v1 whole, which is shorter than its diff:
```python
import functools

import jax
import jax.numpy as jnp
from jax import lax
from jax.experimental import pallas as pl
from jax.experimental.pallas import tpu as pltpu
from jax.sharding import PartitionSpec as P

D = 1024
HEADS = 8
KV_HEADS = 2
HEAD_DIM = 64
SSM_HEADS = 24
SSM_HEAD_DIM = 64
STATE = 128
CONV = 4
FF = 2048
BLOCK_COLS = 256
SSM_INNER = 1536
XBC_WIDTH = 1792
CHUNK = 128
QROWS = 256
LANES = 128
PAD_ROWS = 16

BF16 = jnp.bfloat16
F32 = jnp.float32
MESH = pl.DeviceIdType.MESH
highest = lax.Precision.HIGHEST
rope_base = 100000000000.0
clip_limit = 1.0
learn_rate = 0.01
vector_rate = 0.08
weight_decay = 0.1
soap_first = 0.95
soap_second = 0.95
adam_first = 0.9
adam_second = 0.95
adam_eps = 1e-08
vmem_bytes = 56 * 1024 * 1024


def params(**more):
    return pltpu.CompilerParams(vmem_limit_bytes=vmem_bytes, **more)


def cost(flops, nbytes, exps=0):
    return pl.CostEstimate(flops=int(flops), bytes_accessed=int(nbytes), transcendentals=int(exps))


def rms_gain(values, gain_vec):
    inv_scale = lax.rsqrt(jnp.mean(values * values, axis=-1, keepdims=True) + 1e-05)
    return values * inv_scale * gain_vec


def swiglu(gate_val, up_val):
    return jax.nn.silu(gate_val) * up_val


def unpack(flattened):
    piece_sizes = [
        CONV * XBC_WIDTH,
        XBC_WIDTH,
        SSM_HEADS,
        SSM_HEADS,
        SSM_HEADS,
        SSM_INNER,
        3 * D,
        D * SSM_HEADS,
    ]
    pieces = []
    offset = 0
    for length in piece_sizes:
        pieces.append(flattened[offset : offset + length])
        offset = offset + length
    return pieces


def dot_nt(left, right):
    return lax.dot_general(left, right, (((1,), (1,)), ((), ())), preferred_element_type=F32)


def dot_tn(left, right):
    return lax.dot_general(left, right, (((0,), (0,)), ((), ())), preferred_element_type=F32)


def dot_nn(left, right):
    return jnp.dot(left, right, preferred_element_type=F32)


def project_kernel(own_ref, x_ref, w_ref, o_ref):
    o_ref[...] = dot_nn(x_ref[...], w_ref[...].reshape(D, BLOCK_COLS))


def project(rows_in, gathered, owner, first, count):
    rows, _, depth, _ = gathered.shape
    length = rows_in.shape[0]
    return pl.pallas_call(
        project_kernel,
        grid_spec=pltpu.PrefetchScalarGridSpec(
            num_scalar_prefetch=1,
            grid=(count,),
            in_specs=[
                pl.BlockSpec((length, D), lambda k, own: (0, 0)),
                pl.BlockSpec(
                    (rows, 1, depth, BLOCK_COLS), lambda k, own: (0, own[first + k], 0, 0)
                ),
            ],
            out_specs=pl.BlockSpec((length, BLOCK_COLS), lambda k, own: (0, k)),
        ),
        out_shape=jax.ShapeDtypeStruct((length, count * BLOCK_COLS), F32),
        compiler_params=params(),
        cost_estimate=cost(
            2 * length * D * BLOCK_COLS * count, count * BLOCK_COLS * (2 * D + 4 * length)
        ),
    )(owner, rows_in, gathered)


def back_kernel(own_ref, c_ref, w_ref, base_ref, o_ref):
    @pl.when(pl.program_id(0) == 0)
    def _():
        o_ref[...] = base_ref[...]

    o_ref[...] += dot_nt(c_ref[...], w_ref[...].reshape(D, BLOCK_COLS))


def project_back(cols_in, gathered, owner, first, count, base):
    rows, _, depth, _ = gathered.shape
    length = cols_in.shape[0]
    return pl.pallas_call(
        back_kernel,
        grid_spec=pltpu.PrefetchScalarGridSpec(
            num_scalar_prefetch=1,
            grid=(count,),
            in_specs=[
                pl.BlockSpec((length, BLOCK_COLS), lambda k, own: (0, k)),
                pl.BlockSpec(
                    (rows, 1, depth, BLOCK_COLS), lambda k, own: (0, own[first + k], 0, 0)
                ),
                pl.BlockSpec((length, D), lambda k, own: (0, 0)),
            ],
            out_specs=pl.BlockSpec((length, D), lambda k, own: (0, 0)),
        ),
        out_shape=jax.ShapeDtypeStruct((length, D), F32),
        compiler_params=params(),
        cost_estimate=cost(
            2 * length * D * BLOCK_COLS * count, count * BLOCK_COLS * (2 * D + 2 * length)
        ),
    )(owner, cols_in, gathered, base)


def wgrad_kernel(own_ref, l_ref, r_ref, *rest):
    o_ref, turned = rest[-2], rest[-1]

    @pl.when(pl.program_id(0) == 0)
    def _():
        turned[...] = l_ref[...].T

    grad = dot_nn(turned[...], r_ref[...])
    o_ref[...] = grad.astype(BF16).reshape(o_ref.shape)


def weight_grad(left_rows, right_cols, owner, first, like, into):
    rows, nslots, depth, _ = like
    length = left_rows.shape[0]
    count = right_cols.shape[1] // BLOCK_COLS
    in_specs = [
        pl.BlockSpec((length, D), lambda k, own: (0, 0)),
        pl.BlockSpec((length, BLOCK_COLS), lambda k, own: (0, k)),
    ]
    operands = [owner, left_rows, right_cols]
    aliases = {}
    if into is not None:
        in_specs.append(pl.BlockSpec(memory_space=pl.ANY))
        operands.append(into)
        aliases = {3: 0}
    return pl.pallas_call(
        wgrad_kernel,
        grid_spec=pltpu.PrefetchScalarGridSpec(
            num_scalar_prefetch=1,
            grid=(count,),
            in_specs=in_specs,
            out_specs=pl.BlockSpec(
                (rows, 1, depth, BLOCK_COLS), lambda k, own: (0, own[first + k], 0, 0)
            ),
            scratch_shapes=[pltpu.VMEM((D, length), BF16)],
        ),
        out_shape=jax.ShapeDtypeStruct(like, BF16),
        input_output_aliases=aliases,
        compiler_params=params(),
        cost_estimate=cost(
            2 * length * D * BLOCK_COLS * count, count * BLOCK_COLS * (2 * D + 2 * length)
        ),
    )(*operands)


def rope_tables(length):
    half_dim = HEAD_DIM // 2
    frequency = rope_base ** (-jnp.arange(half_dim, dtype=F32) * 2.0 / HEAD_DIM)
    angles = jnp.arange(length, dtype=F32)[:, None] * frequency[None, :]
    cosine, sine = jnp.cos(angles), jnp.sin(angles)
    wide_cos = jnp.concatenate([cosine] * 4, axis=1)
    wide_sin = jnp.concatenate([-sine, sine, -sine, sine], axis=1)
    return wide_cos, wide_sin


def lane_iota():
    return lax.broadcasted_iota(jnp.int32, (1, LANES), 1)


def swap_halves(values):
    low_half = (lane_iota() % HEAD_DIM) < HEAD_DIM // 2
    return jnp.where(
        low_half,
        pltpu.roll(values, LANES - HEAD_DIM // 2, 1),
        pltpu.roll(values, HEAD_DIM // 2, 1),
    )


def turn(values, cosine, sine):
    return values * cosine + swap_halves(values) * sine


def turn_back(values, cosine, sine):
    return values * cosine - swap_halves(values) * sine


def doubled(values, group):
    moved = pltpu.roll(values, HEAD_DIM, 1)
    keep = (lane_iota() < HEAD_DIM) == (group == 0)
    return jnp.where(keep, values, moved)


def attention_mask(segc_ref, segr_ref, low_row, low_col, wide):
    doc_rows = segc_ref[low_row : low_row + QROWS, :]
    doc_cols = segr_ref[:, low_col : low_col + wide]
    row_pos = low_row + lax.broadcasted_iota(jnp.int32, (QROWS, wide), 0)
    col_pos = low_col + lax.broadcasted_iota(jnp.int32, (QROWS, wide), 1)
    return (doc_rows == doc_cols) & (row_pos >= col_pos)


def attention_probs(query, key, allowed):
    scores = jnp.where(allowed, dot_nt(query, key), -1e30)
    row_top = jnp.max(scores, axis=-1, keepdims=True)
    weights = jnp.exp(scores - row_top)
    return weights, jnp.sum(weights, axis=-1, keepdims=True)


def halves(values):
    high = values.astype(BF16).astype(F32)
    return high, values - high


def fold(values):
    return values + pltpu.roll(values, HEAD_DIM, 1)


def head_operands(values):
    low = lane_iota() < HEAD_DIM
    high, rest = halves(values)
    high_moved, rest_moved = pltpu.roll(high, HEAD_DIM, 1), pltpu.roll(rest, HEAD_DIM, 1)
    head_a = [jnp.where(low, high, rest_moved), jnp.where(low, high, 0.0)]
    head_b = [jnp.where(low, high_moved, rest), jnp.where(low, high_moved, 0.0)]
    return [jnp.concatenate(h, axis=1).astype(BF16) for h in (head_a, head_b)]


def group_operands(values):
    low = lane_iota() < HEAD_DIM
    high, rest = halves(values)
    inner = jnp.concatenate([high, rest], axis=1).astype(BF16)
    return inner, jnp.where(low, high, rest).astype(BF16)


def attn_fwd_kernel(q_ref, k_ref, v_ref, segc_ref, segr_ref, cos_ref, sin_ref, o_ref):
    group = pl.program_id(0) // 2
    low = lane_iota() < HEAD_DIM
    cosine, sine = cos_ref[...], sin_ref[...]
    length = cosine.shape[0]
    query_h = head_operands(turn(q_ref[...], cosine, sine) * HEAD_DIM ** (-0.5))
    key, _ = group_operands(doubled(turn(k_ref[...], cosine, sine), group))
    _, value = group_operands(doubled(v_ref[...], group))
    for block in range(length // QROWS):
        low_row = block * QROWS
        low_col = max(0, low_row - 2 * QROWS)
        wide = low_row + QROWS - low_col
        rows, cols = slice(low_row, low_row + QROWS), slice(low_col, low_col + wide)
        allowed = attention_mask(segc_ref, segr_ref, low_row, low_col, wide)
        outs = []
        for h in range(2):
            weights, total = attention_probs(query_h[h][rows], key[cols], allowed)
            weights_high, weights_rest = split(weights)
            mixed = dot_nn(weights_high, value[cols]) + dot_nn(weights_rest, value[cols])
            outs.append(fold(mixed) / total)
        o_ref[rows, :] = jnp.where(low, outs[0], outs[1]).astype(BF16)


def attn_bwd_kernel(
    q_ref, k_ref, v_ref, segc_ref, segr_ref, cos_ref, sin_ref, g_ref, dq_ref, dkv_ref, dk_s, dv_s
):
    step = pl.program_id(0)
    group = step // 2
    low = lane_iota() < HEAD_DIM
    cosine, sine = cos_ref[...], sin_ref[...]
    length = cosine.shape[0]

    @pl.when(step == 0)
    def _():
        dk_s[...] = jnp.zeros_like(dk_s)
        dv_s[...] = jnp.zeros_like(dv_s)

    scale = HEAD_DIM ** (-0.5)
    query_h = head_operands(turn(q_ref[...], cosine, sine) * scale)
    grad_h = head_operands(g_ref[...])
    key, key_out = group_operands(doubled(turn(k_ref[...], cosine, sine), group))
    value, _ = group_operands(doubled(v_ref[...], group))
    for block in range(length // QROWS):
        low_row = block * QROWS
        low_col = max(0, low_row - 2 * QROWS)
        wide = low_row + QROWS - low_col
        rows, cols = slice(low_row, low_row + QROWS), slice(low_col, low_col + wide)
        allowed = attention_mask(segc_ref, segr_ref, low_row, low_col, wide)
        dqs, ps, dss = [], [], []
        for h in range(2):
            weights, total = attention_probs(query_h[h][rows], key[cols], allowed)
            probs = weights * (1.0 / total)
            dprobs = dot_nt(grad_h[h][rows], value[cols])
            delta = jnp.sum(probs * dprobs, axis=-1, keepdims=True)
            dscores = split(probs * (dprobs - delta))
            dqs.append(fold(dot_nn(dscores[0], key_out[cols]) + dot_nn(dscores[1], key_out[cols])))
            ps.append(probs.astype(BF16))
            dss.append(dscores[0])
        both_p = jnp.concatenate(ps, axis=0)
        both_d = jnp.concatenate(dss, axis=0)
        both_g = jnp.concatenate([grad_h[h][rows, :LANES] for h in range(2)], axis=0)
        both_q = jnp.concatenate([query_h[h][rows, :LANES] for h in range(2)], axis=0)
        dv_s[group, cols, :] += dot_tn(both_p, both_g)
        dk_s[group, cols, :] += dot_tn(both_d, both_q)
        dq = jnp.where(low, dqs[0], dqs[1]) * scale
        dq_ref[rows, :] = turn_back(dq, cosine[rows], sine[rows]).astype(BF16)

    @pl.when(step == pl.num_programs(0) - 1)
    def _():
        dk = jnp.where(low, fold(dk_s[0]), fold(dk_s[1]))
        dv = jnp.where(low, fold(dv_s[0]), fold(dv_s[1]))
        dkv_ref[:, :LANES] = turn_back(dk, cosine, sine).astype(BF16)
        dkv_ref[:, LANES:] = dv.astype(BF16)


def attention_specs(length, base):
    return [
        pl.BlockSpec((length, LANES), lambda p: (0, base + p)),
        pl.BlockSpec((length, LANES), lambda p: (0, base + 4)),
        pl.BlockSpec((length, LANES), lambda p: (0, base + 5)),
        pl.BlockSpec((length, 1), lambda p: (0, 0)),
        pl.BlockSpec((1, length), lambda p: (0, 0)),
        pl.BlockSpec((length, LANES), lambda p: (0, 0)),
        pl.BlockSpec((length, LANES), lambda p: (0, 0)),
    ]


def attention_forward(both_proj, segc, segr, cosine, sine):
    length = both_proj.shape[0]
    base = (SSM_INNER + XBC_WIDTH) // LANES
    pairs = HEADS // 2
    return pl.pallas_call(
        attn_fwd_kernel,
        grid=(pairs,),
        in_specs=attention_specs(length, base),
        out_specs=pl.BlockSpec((length, LANES), lambda p: (0, p)),
        out_shape=jax.ShapeDtypeStruct((length, HEADS * HEAD_DIM), BF16),
        compiler_params=params(),
        cost_estimate=cost(4 * HEADS * length * length * HEAD_DIM, 6 * length * D, HEADS * length * length // 2),
    )(both_proj, both_proj, both_proj, segc, segr, cosine, sine)


def attention_backward(both_proj, segc, segr, cosine, sine, grads, grad_base):
    length = both_proj.shape[0]
    base = (SSM_INNER + XBC_WIDTH) // LANES
    pairs = HEADS // 2
    return pl.pallas_call(
        attn_bwd_kernel,
        grid=(pairs,),
        in_specs=attention_specs(length, base)
        + [pl.BlockSpec((length, LANES), lambda p: (0, grad_base + p))],
        out_specs=[
            pl.BlockSpec((length, LANES), lambda p: (0, p)),
            pl.BlockSpec((length, 2 * LANES), lambda p: (0, 0)),
        ],
        out_shape=[
            jax.ShapeDtypeStruct((length, HEADS * HEAD_DIM), BF16),
            jax.ShapeDtypeStruct((length, 2 * LANES), BF16),
        ],
        scratch_shapes=[pltpu.VMEM((2, length, LANES), F32)] * 2,
        compiler_params=params(),
        cost_estimate=cost(10 * HEADS * length * length * HEAD_DIM, 10 * length * D, HEADS * length * length // 2),
    )(both_proj, both_proj, both_proj, segc, segr, cosine, sine, grads)


def chunk_masks(segc_ref, segr_ref, last_ref, chunk):
    doc_rows, doc_cols = segc_ref[...], segr_ref[...]
    row_pos = lax.broadcasted_iota(jnp.int32, (CHUNK, CHUNK), 0)
    col_pos = lax.broadcasted_iota(jnp.int32, (CHUNK, CHUNK), 1)
    same = (doc_rows == doc_cols) & (row_pos >= col_pos)
    madd = jnp.where(same, 0.0, -1e30)
    last = last_ref[chunk]
    previous = jnp.where(chunk > 0, last_ref[jnp.maximum(chunk - 1, 0)], -1)
    carried = jnp.where(doc_rows == previous, 1.0, 0.0)
    tail = jnp.where(doc_rows == last, 1.0, 0.0)
    keep = jnp.where(last == previous, 1.0, 0.0)
    return madd, carried, tail, keep


def spread(low, columns, a):
    return jnp.where(low, columns[:, a : a + 1], columns[:, a + 1 : a + 2])


def split(values):
    high = values.astype(BF16)
    return high, (values - high.astype(F32)).astype(BF16)


def wide_split(values):
    return jnp.concatenate(split(values), axis=1)


def both_sides(values):
    return values[:, :LANES] + values[:, LANES:]


def ssm_fwd_kernel(
    last_ref, xbc_ref, dt_ref, cum_ref, cumt_ref, skip_ref, segc_ref, segr_ref,
    y_ref, s_ref, state,
):
    chunk = pl.program_id(0)

    @pl.when(chunk == 0)
    def _():
        state[...] = jnp.zeros_like(state)

    s_ref[...] = state[...].reshape(s_ref.shape)
    low = lane_iota() < SSM_HEAD_DIM
    madd, carried, tail, keep = chunk_masks(segc_ref, segr_ref, last_ref, chunk)
    dt, cum, cumt = dt_ref[...], cum_ref[...], cumt_ref[...]
    last_cum = cum[CHUNK - 1 : CHUNK, :]
    ecum = jnp.exp(cum) * carried
    tails = jnp.exp(last_cum - cum) * tail
    keeps = jnp.exp(last_cum) * keep
    into = xbc_ref[:, SSM_INNER : SSM_INNER + STATE]
    into_t = into.T
    into_high, into_rest = split(into_t)
    out_high, out_rest = split(xbc_ref[:, SSM_INNER + STATE :])
    out_both = jnp.concatenate([out_high, out_rest], axis=1)
    into_both = jnp.concatenate([into_high, into_rest], axis=1)
    gram = dot_nn(out_both, jnp.concatenate([into_high, into_high], axis=0)) + dot_nn(
        out_high, into_rest
    )
    for p in range(SSM_HEADS // 2):
        a, cols = 2 * p, slice(p * LANES, (p + 1) * LANES)
        heads = xbc_ref[:, cols]
        scaled = heads * spread(low, dt, a)
        decay_a = jnp.exp(cum[:, a : a + 1] - cumt[a : a + 1, :] + madd)
        decay_b = jnp.exp(cum[:, a + 1 : a + 2] - cumt[a + 1 : a + 2, :] + madd)
        mixing = wide_split(jnp.concatenate([decay_a * gram, decay_b * gram], axis=1))
        stacked_wide = wide_split(
            jnp.concatenate([jnp.where(low, scaled, 0.0), jnp.where(low, 0.0, scaled)], axis=0)
        )
        old = state[:, cols]
        old_wide = wide_split(old)
        carry_in = both_sides(dot_nn(out_both, jnp.concatenate([old_wide, old_wide], axis=0)))
        y_ref[:, cols] = (
            both_sides(dot_nn(mixing, jnp.concatenate([stacked_wide, stacked_wide], axis=0)))
            + spread(low, ecum, a) * carry_in
            + spread(low, skip_ref[...], a) * heads
        )
        tail_in = wide_split(scaled * spread(low, tails, a))
        fresh = both_sides(dot_nn(into_both, jnp.concatenate([tail_in, tail_in], axis=0)))
        state[:, cols] = spread(low, keeps, a) * old + fresh


def ssm_bwd_kernel(
    last_ref, xbc_ref, dt_ref, cum_ref, cumt_ref, skip_ref, segc_ref, segr_ref, s_ref, n_ref,
    y_ref, g_ref, dxbc_ref, sums_ref, ends_ref, dstate,
):
    chunk = pl.num_programs(0) - 1 - pl.program_id(0)

    @pl.when(pl.program_id(0) == 0)
    def _():
        dstate[...] = jnp.zeros_like(dstate)

    low = lane_iota() < SSM_HEAD_DIM
    madd, carried, tail, keep = chunk_masks(segc_ref, segr_ref, last_ref, chunk)
    dt, cum, cumt = dt_ref[...], cum_ref[...], cumt_ref[...]
    last_cum = cum[CHUNK - 1 : CHUNK, :]
    ecum = jnp.exp(cum) * carried
    tails = jnp.exp(last_cum - cum) * tail
    keeps = jnp.exp(last_cum) * keep
    into, into_rest = split(xbc_ref[:, SSM_INNER : SSM_INNER + STATE])
    outof, outof_rest = split(xbc_ref[:, SSM_INNER + STATE :])
    outof_t = outof.T
    into_both = jnp.concatenate([into, into_rest], axis=1)
    gram = dot_nt(
        jnp.concatenate([outof, outof_rest], axis=1), jnp.concatenate([into, into], axis=1)
    ) + dot_nt(outof, into_rest)
    dgram = jnp.zeros((CHUNK, CHUNK), F32)
    d_into = jnp.zeros((CHUNK, STATE), F32)
    d_outof = jnp.zeros((CHUNK, STATE), F32)
    sum_y = jnp.zeros((CHUNK, LANES), F32)
    sum_x = jnp.zeros((CHUNK, LANES), F32)
    sum_k = jnp.zeros((CHUNK, LANES), F32)
    ends = jnp.zeros((8, LANES), F32)
    lane_pos = lax.broadcasted_iota(jnp.int32, (LANES, LANES), 0) // SSM_HEAD_DIM
    head_pos = lax.broadcasted_iota(jnp.int32, (LANES, LANES), 1)

    def by_head(values, pick):
        high = values.astype(BF16)
        rest = (values - high.astype(F32)).astype(BF16)
        return dot_nn(jnp.concatenate([high, rest], axis=1), pick)

    for p in range(SSM_HEADS // 2):
        a, cols = 2 * p, slice(p * LANES, (p + 1) * LANES)
        pick = jnp.where(lane_pos + a == head_pos, 1.0, 0.0).astype(BF16)
        pick = jnp.concatenate([pick, pick], axis=0)
        heads, grad = xbc_ref[:, cols], g_ref[:, cols]
        dt_wide = spread(low, dt, a)
        skip_wide = spread(low, skip_ref[...], a)
        tail_wide = spread(low, tails, a)
        keep_wide = spread(low, keeps, a)
        scaled = heads * dt_wide
        scaled_low = scaled.astype(BF16)
        decay_a = jnp.exp(cum[:, a : a + 1] - cumt[a : a + 1, :] + madd)
        decay_b = jnp.exp(cum[:, a + 1 : a + 2] - cumt[a + 1 : a + 2, :] + madd)
        grads = wide_split(
            jnp.concatenate([jnp.where(low, grad, 0.0), jnp.where(low, 0.0, grad)], axis=0)
        )
        dmix = dot_nt(grads, jnp.concatenate([scaled_low, scaled_low], axis=1))
        dgram += decay_a * dmix[:CHUNK] + decay_b * dmix[CHUNK:]
        mixing = split(jnp.concatenate([decay_a * gram, decay_b * gram], axis=0))
        d_new = dstate[:, cols]
        d_new_wide = wide_split(d_new)
        d_new_low = d_new_wide[:, :LANES]
        d_inner = dot_tn(jnp.concatenate(mixing, axis=0), jnp.concatenate([grads, grads], axis=0))
        d_scaled = both_sides(d_inner) + tail_wide * both_sides(
            dot_nn(into_both, jnp.concatenate([d_new_wide, d_new_wide], axis=0))
        )
        old = s_ref[0, :, cols]
        d_carry = (spread(low, ecum, a) * grad).astype(BF16)
        d_outof += dot_nt(d_carry, old.astype(BF16))
        d_into += dot_nt((scaled * tail_wide).astype(BF16), d_new_low)
        ends += jnp.sum((d_new * n_ref[0, :, cols]).reshape(STATE // 8, 8, LANES), axis=0) @ pick[
            :LANES
        ].astype(F32)
        dstate[:, cols] = keep_wide * d_new + dot_nn(outof_t, d_carry)
        dxbc_ref[:, cols] = d_scaled * dt_wide + skip_wide * grad
        both = grad * heads
        sum_y += by_head(grad * y_ref[:, cols] - skip_wide * both - scaled * d_scaled, pick)
        sum_x += by_head(heads * d_scaled, pick)
        sum_k += by_head(both, pick)
    dgram_low = dgram.astype(BF16)
    dxbc_ref[:, SSM_INNER : SSM_INNER + STATE] = d_into + dot_tn(dgram_low, outof)
    dxbc_ref[:, SSM_INNER + STATE :] = d_outof + dot_nn(dgram_low, into)
    sums_ref[:, :LANES] = sum_y
    sums_ref[:, LANES : 2 * LANES] = sum_x
    sums_ref[:, 2 * LANES :] = sum_k
    ends_ref[...] = ends.reshape(ends_ref.shape)


def ssm_forward(last, xbc, dt, cum, cumt, skip, segc, segr):
    length = xbc.shape[0]
    chunks = length // CHUNK
    here = lambda c, last: (c, 0)
    across = lambda c, last: (0, c)
    return pl.pallas_call(
        ssm_fwd_kernel,
        grid_spec=pltpu.PrefetchScalarGridSpec(
            num_scalar_prefetch=1,
            grid=(chunks,),
            in_specs=[
                pl.BlockSpec((CHUNK, XBC_WIDTH), here),
                pl.BlockSpec((CHUNK, SSM_HEADS), here),
                pl.BlockSpec((CHUNK, SSM_HEADS), here),
                pl.BlockSpec((SSM_HEADS, CHUNK), across),
                pl.BlockSpec((1, SSM_HEADS), lambda c, last: (0, 0)),
                pl.BlockSpec((CHUNK, 1), here),
                pl.BlockSpec((1, CHUNK), across),
            ],
            out_specs=[
                pl.BlockSpec((CHUNK, SSM_INNER), here),
                pl.BlockSpec((1, STATE, SSM_INNER), lambda c, last: (c, 0, 0)),
            ],
            scratch_shapes=[pltpu.VMEM((STATE, SSM_INNER), F32)],
        ),
        out_shape=[
            jax.ShapeDtypeStruct((length, SSM_INNER), F32),
            jax.ShapeDtypeStruct((chunks, STATE, SSM_INNER), F32),
        ],
        compiler_params=params(),
        cost_estimate=cost(
            8 * length * SSM_INNER * STATE, 24 * length * SSM_INNER, length * CHUNK * SSM_HEADS
        ),
    )(last, xbc, dt, cum, cumt, skip, segc, segr)


def ssm_backward(last, xbc, dt, cum, cumt, skip, segc, segr, states, outputs, grads):
    length = xbc.shape[0]
    chunks = length // CHUNK
    end = chunks - 1
    here = lambda i, last: (end - i, 0)
    across = lambda i, last: (0, end - i)
    return pl.pallas_call(
        ssm_bwd_kernel,
        grid_spec=pltpu.PrefetchScalarGridSpec(
            num_scalar_prefetch=1,
            grid=(chunks,),
            in_specs=[
                pl.BlockSpec((CHUNK, XBC_WIDTH), here),
                pl.BlockSpec((CHUNK, SSM_HEADS), here),
                pl.BlockSpec((CHUNK, SSM_HEADS), here),
                pl.BlockSpec((SSM_HEADS, CHUNK), across),
                pl.BlockSpec((1, SSM_HEADS), lambda i, last: (0, 0)),
                pl.BlockSpec((CHUNK, 1), here),
                pl.BlockSpec((1, CHUNK), across),
                pl.BlockSpec((1, STATE, SSM_INNER), lambda i, last: (end - i, 0, 0)),
                pl.BlockSpec(
                    (1, STATE, SSM_INNER), lambda i, last: (jnp.minimum(end - i + 1, end), 0, 0)
                ),
                pl.BlockSpec((CHUNK, SSM_INNER), here),
                pl.BlockSpec((CHUNK, SSM_INNER), here),
            ],
            out_specs=[
                pl.BlockSpec((CHUNK, XBC_WIDTH), here),
                pl.BlockSpec((CHUNK, 3 * LANES), here),
                pl.BlockSpec((1, 8, LANES), lambda i, last: (end - i, 0, 0)),
            ],
            scratch_shapes=[pltpu.VMEM((STATE, SSM_INNER), F32)],
        ),
        out_shape=[
            jax.ShapeDtypeStruct((length, XBC_WIDTH), F32),
            jax.ShapeDtypeStruct((length, 3 * LANES), F32),
            jax.ShapeDtypeStruct((chunks, 8, LANES), F32),
        ],
        compiler_params=params(),
        cost_estimate=cost(
            24 * length * SSM_INNER * STATE, 40 * length * SSM_INNER, length * CHUNK * SSM_HEADS
        ),
    )(last, xbc, dt, cum, cumt, skip, segc, segr, states, states, outputs, grads)


def conv_act(conv_in, conv_weight, conv_bias, segment):
    length = conv_in.shape[0]
    kernel = conv_weight.reshape(CONV, XBC_WIDTH)
    conv_sum = jnp.zeros_like(conv_in) + conv_bias[None, :]
    for offset in range(CONV):
        shift_by = CONV - 1 - offset
        shifted = jnp.pad(conv_in, ((shift_by, 0), (0, 0)))[:length]
        doc_shift = jnp.pad(segment, (shift_by, 0), constant_values=-1)[:length]
        same_doc = (doc_shift == segment).astype(F32)[:, None]
        conv_sum = conv_sum + kernel[offset][None, :] * shifted * same_doc
    return jax.nn.silu(conv_sum)


def gated_norm(output, gate_part, mixer_gain):
    return rms_gain(output * jax.nn.silu(gate_part), mixer_gain)


def rows_kernel(lo_ref, hi_ref, ids_ref, g_ref, o_ref, wide):
    step = pl.program_id(0)

    @pl.when(step == 0)
    def _():
        o_ref[...] = jnp.zeros_like(o_ref)

    group = g_ref.shape[0]
    wide[...] = g_ref[...].astype(F32)
    low, high = lo_ref[step], hi_ref[step]

    def one(j):
        o_ref[pl.ds(ids_ref[step * group + j], 1), :] += wide[pl.ds(j, 1), :]

    def eight(k, carry):
        for u in range(8):
            one(low + 8 * k + u)
        return carry

    def rest(j, carry):
        one(j)
        return carry

    eights = (high - low) // 8
    lax.fori_loop(0, eights, eight, 0)
    lax.fori_loop(low + 8 * eights, high, rest, 0)


def rows_by_token(local_ids, grads, shard_rows, group):
    count, width = grads.shape
    lists = local_ids.reshape(-1, group)
    low = jnp.sum((lists < 0).astype(jnp.int32), axis=1)
    high = jnp.sum((lists < shard_rows).astype(jnp.int32), axis=1)
    return pl.pallas_call(
        rows_kernel,
        grid_spec=pltpu.PrefetchScalarGridSpec(
            num_scalar_prefetch=3,
            grid=(count // group,),
            in_specs=[pl.BlockSpec((group, width), lambda i, lo, hi, ids: (i, 0))],
            out_specs=pl.BlockSpec((shard_rows, width), lambda i, lo, hi, ids: (0, 0)),
            scratch_shapes=[pltpu.VMEM((group, width), F32)],
        ),
        out_shape=jax.ShapeDtypeStruct((shard_rows, width), F32),
        compiler_params=params(),
        cost_estimate=cost(count * width * LANES, count * width * 2),
    )(low, high, local_ids, grads)


def split_nn(left, right):
    left_high, left_rest = split(left)
    right_high, right_rest = split(right)
    return dot_nn(left_high, right_high) + dot_nn(left_rest, right_high) + dot_nn(left_high, right_rest)


def rotate_kernel(l_ref, g_ref, r_ref, o_ref):
    grad = g_ref[...].reshape(D, BLOCK_COLS)
    left_high, left_rest = split(l_ref[0])
    part = dot_nn(left_high, grad) + dot_nn(left_rest, grad)
    o_ref[0] = split_nn(part, r_ref[0])


def rotate_blocks(left_basis, grad_whole, right_basis):
    slots, depth, _ = left_basis.shape
    rows = grad_whole.shape[0]
    return pl.pallas_call(
        rotate_kernel,
        grid=(slots,),
        in_specs=[
            pl.BlockSpec((1, depth, D), lambda k: (k, 0, 0)),
            pl.BlockSpec((rows, 1, depth, BLOCK_COLS), lambda k: (0, k, 0, 0)),
            pl.BlockSpec((1, BLOCK_COLS, BLOCK_COLS), lambda k: (k, 0, 0)),
        ],
        out_specs=pl.BlockSpec((1, depth, BLOCK_COLS), lambda k: (k, 0, 0)),
        out_shape=jax.ShapeDtypeStruct((slots, depth, BLOCK_COLS), F32),
        compiler_params=params(),
        cost_estimate=cost(6 * slots * depth * D * BLOCK_COLS, slots * depth * D * 5),
    )(left_basis, grad_whole, right_basis)


def step_kernel(scale_ref, rot_ref, m_ref, v_ref, l_ref, r_ref, mo_ref, vo_ref, u_ref):
    rotated = rot_ref[0] * scale_ref[0]
    first_new = soap_first * m_ref[0] + (1.0 - soap_first) * rotated
    second_new = soap_second * v_ref[0] + (1.0 - soap_second) * rotated * rotated
    mo_ref[0], vo_ref[0] = first_new, second_new
    direction = (first_new / scale_ref[1]) / (jnp.sqrt(second_new / scale_ref[2]) + adam_eps)
    turned = split_nn(direction, r_ref[0].T).astype(BF16)
    left_high, left_rest = split(l_ref[0])
    update = dot_nn(left_high.T, turned) + dot_nn(left_rest.T, turned)
    u_ref[0] = update.astype(BF16)


def step_blocks(scales, rotated, block_first, block_second, left_basis, right_basis):
    slots, depth, _ = left_basis.shape
    own = pl.BlockSpec((1, depth, BLOCK_COLS), lambda k: (k, 0, 0))
    small = jax.ShapeDtypeStruct((slots, depth, BLOCK_COLS), F32)
    return pl.pallas_call(
        step_kernel,
        grid=(slots,),
        in_specs=[
            pl.BlockSpec(memory_space=pltpu.SMEM),
            own,
            own,
            own,
            pl.BlockSpec((1, depth, D), lambda k: (k, 0, 0)),
            pl.BlockSpec((1, BLOCK_COLS, BLOCK_COLS), lambda k: (k, 0, 0)),
        ],
        out_specs=[own, own, pl.BlockSpec((1, D, BLOCK_COLS), lambda k: (k, 0, 0))],
        out_shape=[small, small, jax.ShapeDtypeStruct((slots, D, BLOCK_COLS), BF16)],
        compiler_params=params(),
        cost_estimate=cost(6 * slots * depth * D * BLOCK_COLS, slots * depth * D * 7),
    )(scales, rotated, block_first, block_second, left_basis, right_basis)


def total_kernel(rows, cols, x_ref, o_ref, inbox, send_sem, recv_sem):
    row, col = lax.axis_index("row"), lax.axis_index("col")
    partners = []
    bit = 1
    while bit < cols:
        partners.append((row, col + bit - 2 * bit * (col // bit % 2)))
        bit = bit * 2
    bit = 1
    while bit < rows:
        partners.append((row + bit - 2 * bit * (row // bit % 2), col))
        bit = bit * 2
    barrier = pltpu.get_barrier_semaphore()
    for partner in partners:
        pl.semaphore_signal(barrier, inc=1, device_id=partner, device_id_type=MESH)
    pl.semaphore_wait(barrier, len(partners))
    o_ref[...] = x_ref[...]
    for step, partner in enumerate(partners):
        copy = pltpu.make_async_remote_copy(
            src_ref=o_ref,
            dst_ref=inbox.at[step],
            send_sem=send_sem.at[step],
            recv_sem=recv_sem.at[step],
            device_id=partner,
            device_id_type=MESH,
        )
        copy.start()
        copy.wait()
        o_ref[...] += inbox[step]


def total_over_all(values, rows, cols, collective_id):
    steps = (rows - 1).bit_length() + (cols - 1).bit_length()
    return pl.pallas_call(
        functools.partial(total_kernel, rows, cols),
        in_specs=[pl.BlockSpec(memory_space=pltpu.VMEM)],
        out_specs=pl.BlockSpec(memory_space=pltpu.VMEM),
        out_shape=jax.ShapeDtypeStruct(values.shape, F32),
        scratch_shapes=[
            pltpu.VMEM((steps,) + values.shape, F32),
            pltpu.SemaphoreType.DMA((steps,)),
            pltpu.SemaphoreType.DMA((steps,)),
        ],
        compiler_params=params(collective_id=collective_id, has_side_effects=True),
        cost_estimate=cost(steps * values.size, steps * values.size * 4),
    )(values)


def ring_bits(rows, cols):
    bits = []
    for axis, extent in ((0, rows), (1, cols)):
        bit = extent // 2
        while bit >= 1:
            bits.append((axis, bit))
            bit = bit // 2
    return bits


def scatter_orders(rows, cols):
    bits = ring_bits(rows, cols)
    row_bits = [b for b in reversed(bits) if b[0] == 0]
    col_bits = [b for b in reversed(bits) if b[0] == 1]
    return col_bits + row_bits, col_bits[:1] + col_bits[1:][::-1] + row_bits


def tail_kernel(rows, cols, slots, g_ref, p_ref, v_ref, whole_ref, tok_ref, vec_ref, own, *rest):
    bits = ring_bits(rows, cols)
    stages = len(bits)
    row_bits = [b for b in bits if b[0] == 0]
    col_bits = [b for b in bits if b[0] == 1]
    boxes, rest = rest[:stages], rest[stages:]
    vec_box, vec_sum, send_sem, recv_sem, own_sem = rest[:5]
    join_send, join_recv, tok_send, tok_recv, tok_own, vec_send, vec_recv = rest[5:]
    place = (lax.axis_index("row"), lax.axis_index("col"))
    half = whole_ref.shape[-2] // 2
    orders = scatter_orders(rows, cols)

    def side(which):
        axis, bit = which
        return place[axis] // bit % 2

    def partner(which):
        axis, bit = which
        moved = place[axis] + bit - 2 * bit * side(which)
        return (moved, place[1]) if axis == 0 else (place[0], moved)

    def remote(src, dst, send, recv, which):
        return pltpu.make_async_remote_copy(
            src_ref=src,
            dst_ref=dst,
            send_sem=send,
            recv_sem=recv,
            device_id=partner(which),
            device_id_type=MESH,
        )

    barrier = pltpu.get_barrier_semaphore()
    for which in bits:
        pl.semaphore_signal(barrier, inc=1, device_id=partner(which), device_id_type=MESH)
    pl.semaphore_wait(barrier, stages)
    units = [(slot, h) for slot in range(slots) for h in range(2)]

    def pick(ref, before, which, side_of, after):
        at = before.index(which)
        return ref.at[(slice(None),) * at + (side_of,) + (slice(None),) * (len(before) - at - 1) + after]

    def part(slot, h, side_of):
        return pick(g_ref, bits, orders[h][0], side_of, (slot, slice(h * half, (h + 1) * half)))

    def cut(stage, u, side_of):
        order = orders[units[u][1]]
        left = [b for b in bits if b not in order[: stage + 1]]
        return pick(boxes[stage].at[u], left, order[stage + 1], side_of, ())

    def send(stage, u):
        slot, h = units[u]
        which = orders[h][stage]
        other = 1 - side(which)
        return remote(
            part(slot, h, other) if stage == 0 else cut(stage - 1, u, other),
            boxes[stage].at[u],
            send_sem.at[stage, u],
            recv_sem.at[stage, u],
            which,
        )

    def keep(u):
        slot, h = units[u]
        return pltpu.make_async_copy(part(slot, h, side(orders[h][0])), own.at[u], own_sem.at[u])

    def joined(ref, order, of_bits, stage, after):
        at = tuple(slice(None) if b in order[:stage] else side(b) for b in of_bits)
        return ref.at[at + after]

    def join(stage, u):
        slot, h = units[u]
        region = joined(whole_ref, row_bits, row_bits, stage, (slot, slice(h * half, (h + 1) * half)))
        return remote(region, region, join_send.at[stage, u], join_recv.at[stage, u], row_bits[stage])

    def tok(stage, h):
        order = (orders[h][1 : len(col_bits)] + orders[h][:1])
        region = joined(tok_ref, order, col_bits, stage, (h,))
        return remote(
            p_ref.at[h] if stage == 0 else region, region, tok_send.at[stage, h],
            tok_recv.at[stage, h], order[stage],
        )

    def tok_keep():
        region = joined(tok_ref, [], col_bits, 0, ())
        return pltpu.make_async_copy(p_ref, region, tok_own)

    def vec(stage):
        return remote(
            vec_sum.at[stage], vec_box.at[stage], vec_send.at[stage], vec_recv.at[stage], bits[stage]
        )

    sent = []

    def start(copy):
        copy.start()
        sent.append(copy)
        return copy

    flying = {}
    vec_sum[0] = v_ref[...]
    flying["vec", 0] = start(vec(0))
    for u in range(len(units)):
        flying[0, u] = start(send(0, u))
        keep(u).start()
        if u == 1:
            tok_keep().start()
            for h in range(2):
                flying["tok", 0, h] = start(tok(0, h))
    steps = slots + stages + len(row_bits) - 1
    tok_at = [(k + 1) * steps // (len(col_bits) + 1) for k in range(len(col_bits))]
    for t in range(steps):
        if t < stages:
            flying["vec", t].wait_recv()
            if t + 1 < stages:
                vec_sum[t + 1] = vec_sum[t] + vec_box[t]
                flying["vec", t + 1] = start(vec(t + 1))
            else:
                vec_ref[...] = vec_sum[t] + vec_box[t]
        for k, at in enumerate(tok_at):
            if at == t:
                if k == 0:
                    tok_keep().wait()
                for h in range(2):
                    flying["tok", k, h].wait_recv()
                    if k + 1 < len(col_bits):
                        flying["tok", k + 1, h] = start(tok(k + 1, h))
        for stage in reversed(range(stages + len(row_bits))):
            slot = t - stage
            if not 0 <= slot < slots:
                continue
            for h in range(2):
                u = 2 * slot + h
                if stage >= stages:
                    flying["join", stage - stages, u].wait_recv()
                    if stage - stages + 1 < len(row_bits):
                        flying["join", stage - stages + 1, u] = start(join(stage - stages + 1, u))
                    continue
                flying[stage, u].wait_recv()
                box = boxes[stage].at[u]
                if stage == 0:
                    keep(u).wait()
                    held = own.at[u]
                else:
                    held = cut(stage - 1, u, side(orders[h][stage]))
                if stage == stages - 1:
                    total = held[...].astype(F32) + box[...].astype(F32)
                    mine = joined(
                        whole_ref, [], row_bits, 0, (slot, slice(h * half, (h + 1) * half))
                    )
                    mine[...] = total.astype(BF16)
                    flying["join", 0, u] = start(join(0, u))
                    continue
                extents = box.shape[:-2]

                def add(k, carry, box=box, held=held, extents=extents):
                    at = []
                    for extent in reversed(extents):
                        at.append(k % extent)
                        k = k // extent
                    at = tuple(reversed(at))
                    box[at] = (held[at].astype(F32) + box[at].astype(F32)).astype(BF16)
                    return carry

                lax.fori_loop(0, 2 ** len(extents), add, 0)
                flying[stage + 1, u] = start(send(stage + 1, u))
    for copy in sent:
        copy.wait_send()


def tail_exchange(grads, pieces, vectors, rows, cols, collective_id):
    _, nslots, depth, _ = grads.shape
    slots = nslots // cols
    bits = ring_bits(rows, cols)
    stages = len(bits)
    row_stages, col_stages = (rows - 1).bit_length(), (cols - 1).bit_length()
    units, half = 2 * slots, depth // 2
    count, width = pieces.shape
    boxes = [
        pltpu.VMEM((units,) + (2,) * (stages - s - 1) + (half, BLOCK_COLS), BF16)
        for s in range(stages)
    ]
    vec_shape = (stages,) + vectors.shape
    whole, tokens, total = pl.pallas_call(
        functools.partial(tail_kernel, rows, cols, slots),
        in_specs=[
            pl.BlockSpec(memory_space=pl.ANY),
            pl.BlockSpec(memory_space=pl.ANY),
            pl.BlockSpec(memory_space=pltpu.VMEM),
        ],
        out_specs=[
            pl.BlockSpec(memory_space=pltpu.VMEM),
            pl.BlockSpec(memory_space=pl.ANY),
            pl.BlockSpec(memory_space=pltpu.VMEM),
        ],
        out_shape=[
            jax.ShapeDtypeStruct((2,) * row_stages + (slots, depth, BLOCK_COLS), BF16),
            jax.ShapeDtypeStruct((2,) * col_stages + (2, count // 2, width), BF16),
            jax.ShapeDtypeStruct(vectors.shape, F32),
        ],
        scratch_shapes=[pltpu.VMEM(boxes[0].shape, BF16)]
        + boxes
        + [
            pltpu.VMEM(vec_shape, F32),
            pltpu.VMEM(vec_shape, F32),
            pltpu.SemaphoreType.DMA((stages, units)),
            pltpu.SemaphoreType.DMA((stages, units)),
            pltpu.SemaphoreType.DMA((units,)),
            pltpu.SemaphoreType.DMA((row_stages, units)),
            pltpu.SemaphoreType.DMA((row_stages, units)),
            pltpu.SemaphoreType.DMA((col_stages, 2)),
            pltpu.SemaphoreType.DMA((col_stages, 2)),
            pltpu.SemaphoreType.DMA,
            pltpu.SemaphoreType.DMA((stages,)),
            pltpu.SemaphoreType.DMA((stages,)),
        ],
        compiler_params=params(collective_id=collective_id, has_side_effects=True),
        cost_estimate=cost(rows * nslots * depth * BLOCK_COLS, rows * nslots * depth * BLOCK_COLS * 6),
    )(
        grads.reshape((2,) * stages + (slots, depth, BLOCK_COLS)),
        pieces.reshape(2, count // 2, width),
        vectors,
    )
    return whole.reshape(rows, slots, depth, BLOCK_COLS), tokens.reshape(cols * count, width), total


def exchange_rows(values, rows):
    row = lax.axis_index("row")
    width = values.shape[1] // rows
    arrived = []
    for k in range(rows):
        part = lax.dynamic_slice_in_dim(values, (row + k) % rows * width, width, 1)
        if k > 0:
            part = lax.ppermute(part, "row", [(r, (r + k) % rows) for r in range(rows)])
        arrived.append(part)
    return jnp.concatenate(arrived, axis=0)


def adam_step(weights, grads, first, second, steps_done, decay, rate):
    first_new = adam_first * first + (1.0 - adam_first) * grads
    second_new = adam_second * second + (1.0 - adam_second) * grads * grads
    direction = (
        first_new
        / (1.0 - adam_first**steps_done)
        / (jnp.sqrt(second_new / (1.0 - adam_second**steps_done)) + adam_eps)
    )
    return (weights - rate * (direction + decay * weights), first_new, second_new)


def body(
    rows,
    cols,
    token_ids,
    segment_ids,
    loss_positions,
    loss_targets,
    loss_valid,
    block_owner,
    step_count,
    block_weights,
    block_first,
    block_second,
    left_basis,
    right_basis,
    table,
    table_first,
    table_second,
    vector_params,
    vector_first,
    vector_second,
):
    col_index = lax.axis_index("col")
    tokens = token_ids[0]
    segment = segment_ids[0]
    length = tokens.shape[0]
    in_cols = 2 * SSM_INNER + 2 * STATE
    in_blocks = (in_cols + (HEADS + 2 * KV_HEADS) * HEAD_DIM) // BLOCK_COLS
    branch_blocks = (SSM_INNER + HEADS * HEAD_DIM) // BLOCK_COLS
    gate_blocks = 2 * FF // BLOCK_COLS
    down_blocks = FF // BLOCK_COLS
    branch_at = in_blocks
    gate_at = branch_at + branch_blocks
    down_at = gate_at + gate_blocks
    nblocks = block_owner.shape[0]
    depth = block_weights.shape[1]
    shard_rows = table.shape[0]

    row_index = lax.axis_index("row")
    devices = rows * cols
    count_rows = loss_positions.shape[1]
    table_low = table.astype(BF16)
    shard_padded = -(-shard_rows // PAD_ROWS) * PAD_ROWS
    padded = jnp.pad(table_low, ((0, shard_padded - shard_rows), (0, 0)))
    table_cols = lax.all_gather(padded, "col", axis=0, tiled=True)
    order = jnp.argsort(tokens)
    sent = jnp.concatenate(
        [tokens, jnp.sort(tokens), loss_targets[0], loss_valid[0]]
    ).reshape(1, -1)
    ints = lax.all_gather(sent, ("row", "col"), axis=0, tiled=True).reshape(rows, cols, -1)
    gathered = lax.all_gather(
        block_weights.astype(BF16), ("row", "col"), axis=0, tiled=True
    ).reshape(rows, nblocks, depth, BLOCK_COLS)
    table_rows = lax.all_gather(padded, "row", axis=1, tiled=True)
    token_list = lax.dynamic_index_in_dim(ints, col_index, 1, False)[:, :length].reshape(-1)
    owners = token_list // shard_rows
    looked_up = jnp.take(
        table_cols, token_list + owners * (shard_padded - shard_rows), axis=0, mode="clip"
    )
    embedded = lax.all_to_all(looked_up, "row", split_axis=0, concat_axis=1, tiled=True)
    sorted_ints = ints[:, :, length : 2 * length]
    sorted_all = jnp.stack(
        [
            lax.dynamic_index_in_dim(sorted_ints, (row_index - k) % rows, 0, False)
            for k in range(rows)
        ],
        axis=1,
    ).reshape(-1)
    labels_all = lax.dynamic_index_in_dim(ints, row_index, 0, False)[:, 2 * length :]
    targets_all = labels_all[:, :count_rows].reshape(-1)
    valid_all = labels_all[:, count_rows:].reshape(-1)
    valid_count = jnp.sum(ints[:, :, 2 * length + count_rows :]).astype(F32)

    conv_weight, conv_bias, time_bias, decay_log, skip_gain, mixer_gain, norm_gains, time_proj = (
        unpack(vector_params)
    )
    gain_rows = norm_gains.reshape(3, D)
    time_low = time_proj.reshape(D, SSM_HEADS).astype(BF16)
    segc, segr = segment[:, None], segment[None, :]
    chunks = length // CHUNK
    last_docs = segment.reshape(chunks, CHUNK)[:, CHUNK - 1]
    cosine, sine = rope_tables(length)

    embed_wide = embedded.astype(F32)
    normed_wide, first_norm_back = jax.vjp(rms_gain, embed_wide, gain_rows[0])
    normed = normed_wide.astype(BF16)
    both_proj = project(normed, gathered, block_owner, 0, in_blocks)
    time_raw = jnp.dot(normed, time_low, preferred_element_type=F32)

    def steps_of(time_in, bias_in, decay_in):
        step_size = jax.nn.softplus(time_in + bias_in[None, :])
        return step_size, step_size * -jnp.exp(decay_in)[None, :]

    (step_size, decays), steps_back = jax.vjp(steps_of, time_raw, time_bias, decay_log)
    earlier = jnp.tril(jnp.ones((CHUNK, CHUNK), F32))
    decays_cut = decays.reshape(chunks, CHUNK, SSM_HEADS)
    cum = jnp.einsum("ts,csh->cth", earlier, decays_cut, precision=highest).reshape(
        length, SSM_HEADS
    )
    cumt = cum.T
    act_xbc, conv_back = jax.vjp(
        lambda u, w, b: conv_act(u, w, b, segment),
        both_proj[:, SSM_INNER:in_cols],
        conv_weight,
        conv_bias,
    )
    skip_row = skip_gain[None, :]
    scan_in = (last_docs, act_xbc, step_size, cum, cumt, skip_row, segc, segr)
    scan_out, states = ssm_forward(*scan_in)
    mixer_wide, gated_back = jax.vjp(gated_norm, scan_out, both_proj[:, :SSM_INNER], mixer_gain)
    context = attention_forward(both_proj, segc, segr, cosine, sine)
    branch_in = jnp.concatenate([mixer_wide.astype(BF16), context], axis=1)
    hidden_one = project_back(branch_in, gathered, block_owner, branch_at, branch_blocks, embed_wide)
    second_wide, second_norm_back = jax.vjp(rms_gain, hidden_one, gain_rows[1])
    normed_two = second_wide.astype(BF16)
    gate_up = project(normed_two, gathered, block_owner, gate_at, gate_blocks)
    activated, swiglu_back = jax.vjp(swiglu, gate_up[:, :FF], gate_up[:, FF:])
    act_low = activated.astype(BF16)
    hidden_two = project_back(act_low, gathered, block_owner, down_at, down_blocks, hidden_one)
    final_wide, final_norm_back = jax.vjp(rms_gain, hidden_two, gain_rows[2])
    final_out = final_wide.astype(BF16)
    positions = loss_positions[0]
    chosen = (positions[:, None] == jnp.arange(length, dtype=jnp.int32)[None, :]).astype(BF16)
    picked_rows = jnp.dot(chosen, final_out, preferred_element_type=F32).astype(BF16)
    rows_all = lax.all_gather(picked_rows, "col", axis=0, tiled=True)

    logits = jnp.einsum("rd,vd->rv", rows_all, table_rows, preferred_element_type=F32)
    local_target = targets_all - col_index * shard_rows
    places = jnp.arange(shard_padded, dtype=jnp.int32)[None, :]
    onehot = (places == local_target[:, None]) & (places < shard_rows)
    logits = jnp.where(places < shard_rows, logits, -1e30)
    row_top = jnp.max(logits, axis=1)
    row_total = jnp.sum(jnp.exp(logits - row_top[:, None]), axis=1)
    target_logit = jnp.sum(jnp.where(onehot, logits, 0.0), axis=1)
    parts = lax.all_gather(jnp.stack([row_top, row_total, target_logit]), "col", axis=0)
    top_all = jnp.max(parts[:, 0], axis=0)
    total_all = jnp.sum(parts[:, 1] * jnp.exp(parts[:, 0] - top_all[None, :]), axis=0)
    target_all = jnp.sum(parts[:, 2], axis=0)
    log_total = top_all + jnp.log(total_all)
    valid_wide = valid_all.astype(F32)
    own_loss = lax.dynamic_slice_in_dim(
        (log_total - target_all) * valid_wide, col_index * count_rows, count_rows
    )
    logit_grad = (
        (jnp.exp(logits - log_total[:, None]) - onehot.astype(F32))
        * (valid_wide / valid_count)[:, None]
    ).astype(BF16)
    rows_grad = lax.psum_scatter(
        jnp.einsum("rv,vd->rd", logit_grad, table_rows, preferred_element_type=F32),
        "col",
        scatter_dimension=0,
        tiled=True,
    )
    table_loss_grad = jnp.einsum("rv,rd->vd", logit_grad, rows_all, preferred_element_type=F32)
    table_loss_low, rows_grad = lax.optimization_barrier((table_loss_grad.astype(BF16), rows_grad))
    table_loss_mine = lax.psum_scatter(table_loss_low, "row", scatter_dimension=1, tiled=True)
    final_grad = jnp.zeros((length, D), F32).at[positions].add(rows_grad)
    hidden_two_grad, gain_final_grad = final_norm_back(final_grad)
    down_in = hidden_two_grad.astype(BF16)
    act_grad = project(down_in, gathered, block_owner, down_at, down_blocks)
    like = (rows, nblocks, depth, BLOCK_COLS)
    gate_grad, up_grad = swiglu_back(act_grad)
    gate_up_grad = jnp.concatenate([gate_grad, up_grad], axis=1).astype(BF16)
    no_base = jnp.zeros((length, D), F32)
    normed_two_grad = project_back(
        gate_up_grad, gathered, block_owner, gate_at, gate_blocks, no_base
    )
    hidden_one_part, gain_ff_grad = second_norm_back(normed_two_grad)
    hidden_one_grad = hidden_two_grad + hidden_one_part
    branch_grad_low = hidden_one_grad.astype(BF16)
    branch_out_grad = project(branch_grad_low, gathered, block_owner, branch_at, branch_blocks)

    dq, dkv = attention_backward(
        both_proj, segc, segr, cosine, sine, branch_out_grad, SSM_INNER // LANES
    )
    scan_grad, gate_part_grad, mixer_gain_grad = gated_back(branch_out_grad[:, :SSM_INNER])
    xbc_grad, sums, ends = ssm_backward(*scan_in, states, scan_out, scan_grad)
    sum_y, sum_x, sum_k = (
        sums[:, i * LANES : i * LANES + SSM_HEADS] for i in range(3)
    )
    skip_grad = jnp.sum(sum_k, axis=0)
    cum_grad = sum_y.reshape(chunks, CHUNK, SSM_HEADS)
    decays_grad = jnp.einsum("ts,cth->csh", earlier, cum_grad, precision=highest)
    decays_grad = decays_grad + jnp.sum(ends, axis=1)[:, None, :SSM_HEADS]
    time_grad, time_bias_grad, decay_log_grad = steps_back(
        (sum_x, decays_grad.reshape(length, SSM_HEADS))
    )
    conv_in_grad, conv_weight_grad, conv_bias_grad = conv_back(xbc_grad)
    in_grad_low = jnp.concatenate(
        [gate_part_grad.astype(BF16), conv_in_grad.astype(BF16), dq, dkv], axis=1
    )
    in_grad_low, table_loss_mine = lax.optimization_barrier((in_grad_low, table_loss_mine))
    time_grad_low = time_grad.astype(BF16)
    grad_time = jnp.einsum("td,th->dh", normed, time_grad_low, preferred_element_type=F32)
    time_part = jnp.einsum("th,dh->td", time_grad_low, time_low, preferred_element_type=F32)
    normed_grad = project_back(in_grad_low, gathered, block_owner, 0, in_blocks, time_part)
    embed_part, gain_in_grad = first_norm_back(normed_grad)
    embed_grad = (hidden_one_grad + embed_part).astype(BF16)
    placed = (order[:, None] == jnp.arange(length, dtype=jnp.int32)[None, :]).astype(BF16)
    embed_sorted = jnp.dot(placed, embed_grad, preferred_element_type=F32).astype(BF16)
    embed_sorted, down_in, normed_two, branch_grad_low, normed = lax.optimization_barrier(
        (embed_sorted, down_in, normed_two, branch_grad_low, normed)
    )
    pieces = exchange_rows(embed_sorted, rows)
    grad_slots = weight_grad(down_in, act_low, block_owner, down_at, like, None)
    grad_slots = weight_grad(normed_two, gate_up_grad, block_owner, gate_at, like, grad_slots)
    grad_slots = weight_grad(branch_grad_low, branch_in, block_owner, branch_at, like, grad_slots)
    grad_slots = weight_grad(normed, in_grad_low, block_owner, 0, like, grad_slots)
    grad_slots, pieces = lax.optimization_barrier((grad_slots, pieces))
    vector_grad = jnp.concatenate(
        [
            conv_weight_grad,
            conv_bias_grad,
            time_bias_grad,
            decay_log_grad,
            skip_grad,
            mixer_gain_grad,
            gain_in_grad,
            gain_ff_grad,
            gain_final_grad,
            grad_time.reshape(-1),
            jnp.sum(own_loss)[None],
        ]
    )
    nvec = vector_params.shape[0]
    packed_len = -(-(nvec + 1) // (8 * LANES)) * 8 * LANES
    to_sum = jnp.pad(vector_grad, (0, packed_len - nvec - 1)).reshape(-1, LANES)
    grad_whole, grads_tokens, summed = tail_exchange(grad_slots, pieces, to_sum, rows, cols, 1)
    summed = summed.reshape(-1)
    vector_total, loss_sum = summed[:nvec], summed[nvec]
    local_tokens = sorted_all - col_index * shard_rows
    table_input_grad = rows_by_token(local_tokens, grads_tokens, shard_rows, length)
    table_grad = table_loss_mine[:shard_rows].astype(F32) + table_input_grad
    grad_mine_wide = lax.dynamic_index_in_dim(grad_whole, row_index, 0, False).astype(F32)
    square_part = jnp.sum(grad_mine_wide * grad_mine_wide) + jnp.sum(table_grad * table_grad)
    square_total = total_over_all(jnp.full((8, LANES), square_part), rows, cols, 0)[0, 0]
    rotated = rotate_blocks(left_basis, grad_whole, right_basis)
    mean_loss = loss_sum / valid_count
    grad_norm = jnp.sqrt(square_total + jnp.sum(vector_total * vector_total))
    clip_scale = jnp.minimum(1.0, clip_limit / (grad_norm + 1e-06))
    steps_done = step_count[0].astype(F32)
    scales = jnp.stack(
        [clip_scale, 1.0 - soap_first**steps_done, 1.0 - soap_second**steps_done]
    )
    first_new, second_new, partial_update = step_blocks(
        scales, rotated, block_first, block_second, left_basis, right_basis
    )
    update = lax.psum_scatter(
        partial_update, "row", scatter_dimension=1, tiled=True
    ).astype(F32)
    new_blocks = block_weights - learn_rate * (update + weight_decay * block_weights)
    new_table, table_first_new, table_second_new = adam_step(
        table,
        table_grad * clip_scale,
        table_first,
        table_second,
        steps_done,
        weight_decay,
        learn_rate,
    )
    new_vectors, vector_first_new, vector_second_new = adam_step(
        vector_params,
        vector_total * clip_scale,
        vector_first,
        vector_second,
        steps_done,
        0.0,
        vector_rate,
    )
    return (
        mean_loss,
        grad_norm,
        new_blocks,
        first_new,
        second_new,
        new_table,
        table_first_new,
        table_second_new,
        new_vectors,
        vector_first_new,
        vector_second_new,
    )


def solution(mesh):
    rows, cols = mesh.shape["row"], mesh.shape["col"]
    placed = (
        P(("row", "col"), None),
        P(("row", "col"), None),
        P(("row", "col"), None),
        P(("row", "col"), None),
        P(("row", "col"), None),
        P(),
        P(),
        P("col", "row", None),
        P("col", "row", None),
        P("col", "row", None),
        P("col", "row", None),
        P("col", None, None),
        P("col", "row"),
        P("col", "row"),
        P("col", "row"),
        P(),
        P(),
        P(),
    )
    return jax.shard_map(
        functools.partial(body, rows, cols),
        mesh=mesh,
        in_specs=placed,
        out_specs=(
            P(),
            P(),
            P("col", "row", None),
            P("col", "row", None),
            P("col", "row", None),
            P("col", "row"),
            P("col", "row"),
            P("col", "row"),
            P(),
            P(),
            P(),
        ),
        check_vma=False,
    )
```

time: 3440 us -> 1270 us (0.37)
  waiting for transfers between devices: 1270 us -> 272 us
  matrix products: 691 us -> 42.7 us
  Pallas kernels: 0 us -> 618 us
  other arithmetic: 685 us -> 181 us
  local copies, waits for them, and re-layouts: 461 us -> 61.7 us
  blocking collectives: 255 us -> 54.1 us
    dot_general x92 -> x10, matrix products: 691 us -> 42.7 us  [the longest x1 11 us: body(): jnp.einsum('rv,rd->vd', logit_grad, rows_all, preferred_element_type=F32)]
    pallas_call x0 -> x21, Pallas kernels: none -> 618 us  [the longest x1 221 us: tail_exchange(): pl.pallas_call(functools.partial(tail_kernel, rows, cols, slots), in_spec...]
    all_gather x7 -> x4, waiting for transfers between devices: 570 us -> 124 us  [the longest x1 60 us: body(): lax.all_gather(block_weights.astype(BF16), ('row', 'col'), axis=0, tiled=...]
    reduce_scatter x3 -> x1, waiting for transfers between devices: 358 us -> 0.01 us  [body(): lax.psum_scatter(table_loss_low, 'row', scatter_dimension=1, tiled=True)]
    scatter-add x2 -> x1, other arithmetic: 214 us -> 3.68 us  [body(): final_grad = jnp.zeros((length, D), F32).at[positions].add(rows_grad)]
    psum x1 -> x0, waiting for transfers between devices: 122 us -> none  [body(): lax.psum((vector_grad, square_part), ('row', 'col'))]
    all_to_all x1 -> x0, blocking collectives: 110 us -> none  [body(): lax.all_to_all(embed_grad, 'row', split_axis=1, concat_axis=0, tiled=True)]
    select_n x11 -> x1, other arithmetic: 95.1 us -> 0.01 us  [body(): final_grad = jnp.zeros((length, D), F32).at[positions].add(rows_grad)]
  transfers between devices with their start and end apart: 14 -> 11, of which waited for: 11 -> 6; matrix products, arithmetic and copies ran while one was open for 24% -> 18% of each run, Pallas kernels for 0% -> 23%
where the time goes in v1:
time: 1270 us; the launch traced here: 1260 us
  Pallas kernels  618 us (49%)
  waiting for transfers between devices  272 us (21%)
  other arithmetic  181 us (14%)
  local copies, waits for them, and re-layouts  61.7 us (5%)
  blocking collectives  54.1 us (4%)
  matrix products  42.7 us (3%)
  between operations  22.6 us (2%)
    pallas_call x1, Pallas kernels, tail_exchange(): pl.pallas_call(functools.partial(tail_kernel, rows, cols, slots), in_spec...  221 us
    all_to_all x1, waiting for transfers between devices, body(): lax.all_to_all(looked_up, 'row', split_axis=0, concat_axis=1, tiled=True)  75.7 us
    pallas_call x4, Pallas kernels, project_back(): pl.pallas_call(back_kernel, grid_spec=pltpu.PrefetchScalarGridSpec(num_sc...  70.2 us
    pallas_call x4, Pallas kernels, project(): pl.pallas_call(project_kernel, grid_spec=pltpu.PrefetchScalarGridSpec(num...  64.6 us
    pallas_call x4, Pallas kernels, weight_grad(): pl.pallas_call(wgrad_kernel, grid_spec=pltpu.PrefetchScalarGridSpec(num_s...  61.6 us
    all_gather x1, waiting for transfers between devices, body(): lax.all_gather(block_weights.astype(BF16), ('row', 'col'), axis=0, tiled=...  60 us
    all_gather x1, blocking collectives, body(): lax.all_gather(sent, ('row', 'col'), axis=0, tiled=True)  44.6 us
    reduce_scatter x1, waiting for transfers between devices, body(): lax.psum_scatter(partial_update, 'row', scatter_dimension=1, tiled=True)  44.5 us
  transfers between devices with their start and end apart: 11, of which 6 were waited for; matrix products, arithmetic and copies ran while one was open for 18% of the time, Pallas kernels for 23%

profile of v1, /device:TPU:0, one launch (start us, length us, event | category | flops | bytes accessed | tf_op | source)
XLA Modules:
  0.0 1261.4 jit_solution(12416546765109128534)
XLA Ops:
  17.2 44.6 %all-gather.2 = s32[32,1,2176]{2,1,0:T(1,128)S(1)} all-gather(s32[1,1,2176]{2,1,0:T(1,128)S(1)} %reshape.408), channel_id=2, replica_groups=mesh['row'=4,'col'=8] {'row','col'}, dimensions={0}, use_global_device_ids=true | all-gather | bytes 287232 | tf_op jit(solution)/shard_map/all_gather | solution.py:1140
  62.0 44.1 %all-gather.9.cloned.1.call-done = bf16[32896,256]{1,0:T(8,128)(2,1)} async-done(((bf16[4112,256]{1,0:T(8,128)(2,1)}), bf16[32896,256]{1,0:T(8,128)(2,1)}) %all-gather.9.cloned.1.call-update) | async-done | bytes 16842768 | tf_op jit(solution)/shard_map/all_gather | solution.py:1135
  106.1 23.9 %gather_fusion = bf16[4096,256]{1,0:T(8,128)(2,1)} fusion(bf16[32896,256]{1,0:T(8,128)(2,1)} %all-gather.9.cloned.1.call-done, s32[4096]{0:T(1024)S(1)} %broadcast_clamp_fusion), kind=kCustom, calls=%fused_computation | custom fusion | bytes 4210688 | tf_op jit(solution)/shard_map/jit(_take)/gather | solution.py:1147
  142.4 75.7 %all-to-all-done = bf16[4,1024,256]{2,1,0:T(8,128)(2,1)} async-done(((bf16[4,1024,256]{2,1,0:T(8,128)(2,1)}), bf16[4,1024,256]{2,1,0:T(8,128)(2,1)}, u32[]{:S(2)}, u32[]{:S(2)}) %all-to-all-start) | async-done | bytes 2097184 | tf_op jit(solution)/shard_map/all_to_all | solution.py:1150
  239.3 60.0 %all-gather.11.cloned.1.call-done = bf16[192,256,256]{2,1,0:T(8,128)(2,1)} async-done(((bf16[6,256,256]{2,1,0:T(8,128)(2,1)}), bf16[192,256,256]{2,1,0:T(8,128)(2,1)}) %all-gather.11.cloned.1.call-update) | async-done | bytes 25165840 | tf_op jit(solution)/shard_map/all_gather | solution.py:1141
  299.3 20.4 %shard_map.257.q_ref.k_ref.v_ref = f32[1024,4096]{1,0:T(8,128)} custom-call(s32[48]{0:T(128)} %own_ref.23, bf16[1024,1024]{1,0:T(8,128)(2,1)} %multiply_convert_fusion.7.x_ref.l_ref, bf16[4,48,256,256]{3,2,1,0:T(8,128)(2,1)} %bitcast.112), custom_call_target="tpu_custom_call" | custom-call | flops 8589934592 | bytes 25165824 | tf_op jit(solution)/shard_map/pallas_call | solution.py:99
  332.3 21.3 %shard_map.258 = (f32[1024,1536]{1,0:T(8,128)}, f32[8,128,1536]{2,1,0:T(8,128)}) custom-call(s32[8]{0:T(128)} %bitcast.158, f32[1024,1792]{1,0:T(8,128)} %get-tuple-element.100.xbc_ref, f32[1024,24]{1,0:T(8,128)} %get-tuple-element.117.dt_ref, f32[1024,24]{1,0:T(8,128)} %copy.93.cum_ref, f32[24,1024]{1,0:T(8,128)} %bitcast.136, ...), custom_call_target="tpu_custom_call" | custom-call | flops 1610612736 | bytes 37748736 | tf_op jit(solution)/shard_map/pallas_call | solution.py:573
  353.6 24.6 %shard_map.259 = bf16[1024,512]{1,0:T(8,128)(2,1)} custom-call(f32[1024,4096]{1,0:T(8,128)} %shard_map.257.q_ref.k_ref.v_ref, f32[1024,4096]{1,0:T(8,128)} %shard_map.257.q_ref.k_ref.v_ref, f32[1024,4096]{1,0:T(8,128)} %shard_map.257.q_ref.k_ref.v_ref, s32[1024,1]{1,0:T(8,128)} %copy.94.segc_ref, s32[1,1024]{1,0:T(1,128)} %segr_ref.7, ...), custom_call_target="tpu_custom_call" | custom-call | flops 2147483648 | bytes 6291456 | tf_op jit(solution)/shard_map/pallas_call | solution.py:366
  388.8 13.2 %shard_map.260.base_ref = f32[1024,1024]{1,0:T(8,128)} custom-call(s32[48]{0:T(128)} %own_ref.23, bf16[1024,2048]{1,0:T(8,128)(2,1)} %pad_maximum_fusion.2.c_ref.r_ref, bf16[4,48,256,256]{3,2,1,0:T(8,128)(2,1)} %bitcast.113, f32[1024,1024]{1,0:T(8,128)} %copy.107.base_ref), custom_call_target="tpu_custom_call" | custom-call | flops 4294967296 | bytes 8388608 | tf_op jit(solution)/shard_map/pallas_call | solution.py:131
  407.3 20.2 %shard_map.261 = f32[1024,4096]{1,0:T(8,128)} custom-call(s32[48]{0:T(128)} %own_ref.23, bf16[1024,1024]{1,0:T(8,128)(2,1)} %multiply_convert_fusion.5.x_ref.l_ref, bf16[4,48,256,256]{3,2,1,0:T(8,128)(2,1)} %bitcast.114), custom_call_target="tpu_custom_call" | custom-call | flops 8589934592 | bytes 25165824 | tf_op jit(solution)/shard_map/pallas_call | solution.py:99
  436.2 13.4 %shard_map.262 = f32[1024,1024]{1,0:T(8,128)} custom-call(s32[48]{0:T(128)} %own_ref.23, bf16[1024,2048]{1,0:T(8,128)(2,1)} %multiply_convert_fusion.2.c_ref.r_ref, bf16[4,48,256,256]{3,2,1,0:T(8,128)(2,1)} %bitcast.115, f32[1024,1024]{1,0:T(8,128)} %shard_map.260.base_ref), custom_call_target="tpu_custom_call" | custom-call | flops 4294967296 | bytes 8388608 | tf_op jit(solution)/shard_map/pallas_call | solution.py:131
  456.1 20.3 %all-gather.13.cloned.1.call-done = bf16[512,1024]{1,0:T(8,128)(2,1)} async-done(((bf16[64,1024]{1,0:T(8,128)(2,1)}), bf16[512,1024]{1,0:T(8,128)(2,1)}) %all-gather.13.cloned.1.call-update) | async-done | bytes 1048592 | tf_op jit(solution)/shard_map/all_gather | solution.py:1215
  519.6 26.3 %reduce-scatter.4.cloned.1.call-done = f32[64,1024]{1,0:T(8,128)} async-done(((f32[512,1024]{1,0:T(8,128)}), f32[64,1024]{1,0:T(8,128)}) %reduce-scatter.4.cloned.1.call-update) | async-done | bytes 262160 | tf_op jit(solution)/shard_map/reduce_scatter | solution.py:1238
  593.7 22.0 %shard_map.264 = f32[1024,1024]{1,0:T(8,128)} custom-call(s32[48]{0:T(128)} %own_ref.23, bf16[1024,4096]{1,0:T(8,128)(2,1)} %pad_maximum_fusion.c_ref.r_ref, bf16[4,48,256,256]{3,2,1,0:T(8,128)(2,1)} %bitcast.117, f32[1024,1024]{1,0:T(8,128)} %broadcast_18_base_ref.2.base_ref), custom_call_target="tpu_custom_call" | custom-call | flops 8589934592 | bytes 16777216 | tf_op jit(solution)/shard_map/pallas_call | solution.py:131
  653.3 36.1 %shard_map.266 = (f32[1024,1792]{1,0:T(8,128)}, f32[1024,384]{1,0:T(8,128)}, f32[8,8,128]{2,1,0:T(8,128)}) custom-call(s32[8]{0:T(128)} %bitcast.159, f32[1024,1792]{1,0:T(8,128)} %get-tuple-element.100.xbc_ref, f32[1024,24]{1,0:T(8,128)} %get-tuple-element.117.dt_ref, f32[1024,24]{1,0:T(8,128)} %copy.93.cum_ref, f32[24,1024]{1,0:T(8,128)} %bitcast.137, ...), custom_call_target="tpu_custom_call" | custom-call | flops 4831838208 | bytes 62914560 | tf_op jit(solution)/shard_map/pallas_call | solution.py:610
  689.4 14.2 %multiply_reduce_fusion.2 = (f32[1792]{0:T(1024)S(1)}, f32[1792]{0:T(1024)S(1)}, f32[1792]{0:T(1024)S(1)}, f32[1792]{0:T(1024)}, f32[1792]{0:T(1024)S(1)}, /*index=5*/f32[1024,1792]{1,0:T(8,128)}) fusion(f32[1024,1792]{1,0:T(8,128)S(1)} %bitcast.124, f32[1024]{0:T(1024)S(1)} %copy-done.47, f32[1024]{0:T(1024)S(1)} %copy-done.45, f32[1024]{0:T(1024)S(1)} %copy-done.43, ...), kind=kLoop, calls=%fused_computation.36 | loop fusion | flops 38526208 | bytes 36748288 | tf_op jit(solution)/shard_map/transpose(jvp())/reduce_sum | solution.py:658
  716.9 39.7 %shard_map.267 = (bf16[1024,512]{1,0:T(8,128)(2,1)}, bf16[1024,256]{1,0:T(8,128)(2,1)}) custom-call(f32[1024,4096]{1,0:T(8,128)} %shard_map.257.q_ref.k_ref.v_ref, f32[1024,4096]{1,0:T(8,128)} %shard_map.257.q_ref.k_ref.v_ref, f32[1024,4096]{1,0:T(8,128)} %shard_map.257.q_ref.k_ref.v_ref, s32[1024,1]{1,0:T(8,128)} %copy.94.segc_ref, s32[1,1024]{1,0:T(1,128)} %segr_ref.7, ...), custom_call_target="tpu_custom_call" | custom-call | flops 5368709120 | bytes 10485760 | tf_op jit(solution)/shard_map/pallas_call | solution.py:381
  775.9 21.7 %shard_map.268 = f32[1024,1024]{1,0:T(8,128)} custom-call(s32[48]{0:T(128)} %own_ref.23, bf16[1024,4096]{1,0:T(8,128)(2,1)} %pad_maximum_fusion.1.c_ref.r_ref, bf16[4,48,256,256]{3,2,1,0:T(8,128)(2,1)} %bitcast.119, f32[1024,1024]{1,0:T(8,128)} %fusion.49.base_ref), custom_call_target="tpu_custom_call" | custom-call | flops 8589934592 | bytes 16777216 | tf_op jit(solution)/shard_map/pallas_call | solution.py:131
  826.2 19.4 %shard_map.270.rest_0_ = bf16[4,48,256,256]{3,2,1,0:T(8,128)(2,1)} custom-call(s32[48]{0:T(128)} %own_ref.23, bf16[1024,1024]{1,0:T(8,128)(2,1)} %multiply_convert_fusion.5.x_ref.l_ref, bf16[1024,4096]{1,0:T(8,128)(2,1)} %pad_maximum_fusion.c_ref.r_ref, bf16[4,48,256,256]{3,2,1,0:T(8,128)(2,1)} %shard_map.269.rest_0_), custom_call_target="tpu_custom_call", output_to_operand_aliasing={{}: (3, {})} | custom-call | flops 8589934592 | bytes 16777216 | tf_op jit(solution)/shard_map/pallas_call | solution.py:178
  857.0 19.4 %shard_map.272 = bf16[4,48,256,256]{3,2,1,0:T(8,128)(2,1)} custom-call(s32[48]{0:T(128)} %own_ref.23, bf16[1024,1024]{1,0:T(8,128)(2,1)} %multiply_convert_fusion.7.x_ref.l_ref, bf16[1024,4096]{1,0:T(8,128)(2,1)} %pad_maximum_fusion.1.c_ref.r_ref, bf16[4,48,256,256]{3,2,1,0:T(8,128)(2,1)} %shard_map.271.rest_0_), custom_call_target="tpu_custom_call", output_to_operand_aliasing={{}: (3, {})} | custom-call | flops 8589934592 | bytes 16777216 | tf_op jit(solution)/shard_map/pallas_call | solution.py:178
  877.8 221.4 %shard_map.273 = (bf16[2,2,6,256,256]{4,3,2,1,0:T(8,128)(2,1)}, bf16[2,2,2,2,2048,256]{5,4,3,2,1,0:T(8,128)(2,1)}, f32[304,128]{1,0:T(8,128)}) custom-call(bf16[2,2,2,2,2,6,256,256]{7,6,5,4,3,2,1,0:T(8,128)(2,1)} %bitcast.120, bf16[2,2048,256]{2,1,0:T(8,128)(2,1)} %bitcast.130, f32[304,128]{1,0:T(8,128)} %pad_bitcast_fusion.v_ref), custom_call_target="tpu_custom_call" | custom-call | flops 12582912 | bytes 75497472 | tf_op jit(solution)/shard_map/pallas_call | solution.py:1025
  1102.9 39.9 %shard_map.274 = f32[4098,256]{1,0:T(8,128)} custom-call(s32[32]{0:T(128)} %reduce_sum.381.lo_ref, s32[32]{0:T(128)} %reduce_sum.383.hi_ref, s32[32768]{0:T(1024)} %bitcast.145, bf16[32768,256]{1,0:T(8,128)(2,1)} %bitcast.127), custom_call_target="tpu_custom_call" | custom-call | flops 1073741824 | bytes 16777216 | tf_op jit(solution)/shard_map/pallas_call | solution.py:699
  1148.6 19.7 %shard_map.275 = f32[8,128]{1,0:T(8,128)} custom-call(f32[8,128]{1,0:T(8,128)} %broadcast_in_dim.88.x_ref), custom_call_target="tpu_custom_call" | custom-call | flops 5120 | bytes 20480 | tf_op jit(solution)/shard_map/pallas_call | solution.py:811
  1204.6 44.5 %reduce-scatter.8.cloned.1.call-done = bf16[6,256,256]{2,1,0:T(8,128)(2,1)} async-done(((bf16[6,1024,256]{2,1,0:T(8,128)(2,1)}), bf16[6,256,256]{2,1,0:T(8,128)(2,1)}) %reduce-scatter.8.cloned.1.call-update) | async-done | bytes 786448 | tf_op jit(solution)/shard_map/reduce_scatter | solution.py:1338
  (309 shorter events, 333.0 us)
Async XLA Ops:
  7.2 99.0 %all-gather.9.cloned.1.call-start = ((), (), s32[]{:S(2)}) async-start(), calls=%async_computation.4 | async-start | bytes 18948096 | tf_op jit(solution)/shard_map/all_gather | solution.py:1135
  11.2 288.1 %all-gather.11.cloned.1.call-start = ((), (), s32[]{:S(2)}) async-start(), calls=%async_computation.5 | async-start | bytes 25952256 | tf_op jit(solution)/shard_map/all_gather | solution.py:1141
  130.0 88.1 %all-to-all-start = ((bf16[4,1024,256]{2,1,0:T(8,128)(2,1)}), bf16[4,1024,256]{2,1,0:T(8,128)(2,1)}, u32[]{:S(2)}, u32[]{:S(2)}) async-start(bf16[4,1024,256]{2,1,0:T(8,128)(2,1)} %bitcast.9), calls=%async_computation | async-start | bytes 4194304 | tf_op jit(solution)/shard_map/all_to_all | solution.py:1150
  134.7 321.4 %all-gather.15.cloned.1.call-start = ((), (), s32[]{:S(2)}) async-start(), calls=%async_computation.7 | async-start | bytes 10526720 | tf_op jit(solution)/shard_map/all_gather | solution.py:1144
  135.4 340.9 %all-gather.13.cloned.1.call-start = ((), (), s32[]{:S(2)}) async-start(), calls=%async_computation.6 | async-start | bytes 1179648 | tf_op jit(solution)/shard_map/all_gather | solution.py:1215
  136.4 98.9 %copy-start.38 = (f32[1024]{0:T(1024)}, f32[1024]{0:T(1024)S(1)}, u32[]{:S(2)}) copy-start(f32[1024]{0:T(1024)S(1)} %get-tuple-element.120) | copy-start | bytes 12292
  136.8 89.2 %copy-start.18 = (bf16[1024,24]{1,0:T(8,128)(2,1)}, bf16[1024,24]{1,0:T(8,128)(2,1)S(1)}, u32[]{:S(2)}) copy-start(bf16[1024,24]{1,0:T(8,128)(2,1)S(1)} %convert_element_type.150) | copy-start | bytes 147460
  142.3 83.7 %copy-start.58 = (f32[24]{0:T(128)}, f32[24]{0:T(128)S(1)}, u32[]{:S(2)}) copy-start(f32[24]{0:T(128)S(1)} %get-tuple-element.122) | copy-start | bytes 292
  142.4 181.0 %copy-start.42 = (f32[1024]{0:T(1024)}, f32[1024]{0:T(1024)S(1)}, u32[]{:S(2)}) copy-start(f32[1024]{0:T(1024)S(1)} %get-tuple-element.142) | copy-start | bytes 12292
  142.4 181.0 %copy-start.44 = (f32[1024]{0:T(1024)}, f32[1024]{0:T(1024)S(1)}, u32[]{:S(2)}) copy-start(f32[1024]{0:T(1024)S(1)} %get-tuple-element.143) | copy-start | bytes 12292
  142.4 181.0 %copy-start.46 = (f32[1024]{0:T(1024)}, f32[1024]{0:T(1024)S(1)}, u32[]{:S(2)}) copy-start(f32[1024]{0:T(1024)S(1)} %get-tuple-element.144) | copy-start | bytes 12292
  142.4 181.0 %copy-start.30 = (f32[1792]{0:T(1024)}, f32[1792]{0:T(1024)S(1)}, u32[]{:S(2)}) copy-start(f32[1792]{0:T(1024)S(1)} %get-tuple-element.125) | copy-start | bytes 21508
  142.4 181.0 %copy-start.32 = (f32[1792]{0:T(1024)}, f32[1792]{0:T(1024)S(1)}, u32[]{:S(2)}) copy-start(f32[1792]{0:T(1024)S(1)} %get-tuple-element.126) | copy-start | bytes 21508
  142.4 181.0 %copy-start.34 = (f32[1792]{0:T(1024)}, f32[1792]{0:T(1024)S(1)}, u32[]{:S(2)}) copy-start(f32[1792]{0:T(1024)S(1)} %get-tuple-element.127) | copy-start | bytes 21508
  142.4 181.0 %copy-start.36 = (f32[1792]{0:T(1024)}, f32[1792]{0:T(1024)S(1)}, u32[]{:S(2)}) copy-start(f32[1792]{0:T(1024)S(1)} %get-tuple-element.128) | copy-start | bytes 21508
  454.4 91.5 %reduce-scatter.4.cloned.1.call-start = ((), (), s32[]{:S(2)}) async-start(), calls=%async_computation.8 | async-start | bytes 2359296 | tf_op jit(solution)/shard_map/reduce_scatter | solution.py:1238
  504.5 271.4 %reduce-scatter.6.cloned.1.call-start = ((), (), s32[]{:S(2)}) async-start(), calls=%async_computation.9 | async-start | bytes 10526720 | tf_op jit(solution)/shard_map/reduce_scatter | solution.py:1246
  545.9 703.1 %reduce-scatter.8.cloned.1.call-start = ((), (), s32[]{:S(2)}) async-start(), calls=%async_computation.10 | async-start | bytes 3932160 | tf_op jit(solution)/shard_map/reduce_scatter | solution.py:1338
  713.0 43.6 %slice-start.4 = ((s8[7340032]{0:T(1024)(128)(4,1)}), s8[4194304]{0:T(1024)(128)(4,1)S(1)}, s32[]{:S(2)}) async-start(s8[7340032]{0:T(1024)(128)(4,1)} %bitcast.125), calls=%async_computation.15 | async-start | bytes 8388608
  716.9 39.8 %copy-start.37 = (f32[1792]{0:T(1024)S(1)}, f32[1792]{0:T(1024)}, u32[]{:S(2)}) copy-start(f32[1792]{0:T(1024)} %copy-done.36) | copy-start | bytes 21508
  810.2 66.2 %collective-permute-start.2 = (bf16[1024,256]{1,0:T(8,128)(2,1)S(1)}, bf16[1024,256]{1,0:T(8,128)(2,1)S(1)}, u32[]{:S(2)}, u32[]{:S(2)}) collective-permute-start(bf16[1024,256]{1,0:T(8,128)(2,1)S(1)} %get-tuple-element.110), channel_id=1, source_target_pairs={{0,24},{8,0},{16,8},{24,16},{1,25},{9,1},{17,9},{25,17},{2,26},{10... | collective-permute-start | bytes 1572872 | tf_op jit(solution)/shard_map/ppermute | solution.py:1075
  813.7 62.7 %collective-permute-start.1 = (bf16[1024,256]{1,0:T(8,128)(2,1)S(1)}, bf16[1024,256]{1,0:T(8,128)(2,1)S(1)}, u32[]{:S(2)}, u32[]{:S(2)}) collective-permute-start(bf16[1024,256]{1,0:T(8,128)(2,1)S(1)} %get-tuple-element.111), channel_id=1, source_target_pairs={{0,16},{8,24},{16,0},{24,8},{1,17},{9,25},{17,1},{25,9},{2,18},{10... | collective-permute-start | bytes 1572872 | tf_op jit(solution)/shard_map/ppermute | solution.py:1075
  813.7 62.7 %collective-permute-start = (bf16[1024,256]{1,0:T(8,128)(2,1)S(1)}, bf16[1024,256]{1,0:T(8,128)(2,1)S(1)}, u32[]{:S(2)}, u32[]{:S(2)}) collective-permute-start(bf16[1024,256]{1,0:T(8,128)(2,1)S(1)} %get-tuple-element.112), channel_id=1, source_target_pairs={{0,8},{8,16},{16,24},{24,0},{1,9},{9,17},{17,25},{25,1},{2,10},{10... | collective-permute-start | bytes 1572872 | tf_op jit(solution)/shard_map/ppermute | solution.py:1075
  1102.9 39.9 %copy-start.14 = (bf16[4112,256]{1,0:T(8,128)(2,1)S(1)}, bf16[4112,256]{1,0:T(8,128)(2,1)}, u32[]{:S(2)}) copy-start(bf16[4112,256]{1,0:T(8,128)(2,1)} %reduce-scatter.6.cloned.1.call-done) | copy-start | bytes 6316036
  (62 other events, 723.2 us)
Sparse Core Ops, SparseCore 0:
  11.3 94.7 all-gather.8
  109.6 189.6 all-gather.10
  300.9 147.8 all-gather.14
  454.5 21.7 all-gather.12
  504.7 41.2 reduce-scatter.3
  548.2 145.3 reduce-scatter.5
  1190.6 58.3 reduce-scatter.7

commit v2 on v1

--- a/solution.py
+++ b/solution.py
@@ -22,7 +22,10 @@
 CHUNK = 128
 QROWS = 256
 LANES = 128
-PAD_ROWS = 16
+TABLE_PARTS = 4
+PAD_ROWS = 16 * TABLE_PARTS
+GROUP = 4
+ROW_PART = 128
 
 BF16 = jnp.bfloat16
 F32 = jnp.float32
@@ -52,10 +55,6 @@
 def rms_gain(values, gain_vec):
     inv_scale = lax.rsqrt(jnp.mean(values * values, axis=-1, keepdims=True) + 1e-05)
     return values * inv_scale * gain_vec
-
-
-def swiglu(gate_val, up_val):
-    return jax.nn.silu(gate_val) * up_val
 
 
 def unpack(flattened):
@@ -89,65 +88,222 @@
     return jnp.dot(left, right, preferred_element_type=F32)
 
 
-def project_kernel(own_ref, x_ref, w_ref, o_ref):
-    o_ref[...] = dot_nn(x_ref[...], w_ref[...].reshape(D, BLOCK_COLS))
+def slot_spec(gathered, at, every):
+    rows, _, depth, _ = gathered.shape
+    return pl.BlockSpec(
+        (rows, 1, depth, BLOCK_COLS), lambda k, own: (0, own[at + every * k], 0, 0)
+    )
+
+
+def whole(shape):
+    return pl.BlockSpec(shape, lambda k, own: (0,) * len(shape))
+
+
+def block_of(w_ref):
+    return w_ref[...].reshape(D, BLOCK_COLS)
+
+
+def slot_call(kernel, owner, steps, in_specs, out_specs, out_shape, flops, operands):
+    nbytes = sum(o.size * o.dtype.itemsize for o in operands[:1])
+    return pl.pallas_call(
+        kernel,
+        grid_spec=pltpu.PrefetchScalarGridSpec(
+            num_scalar_prefetch=1, grid=(steps,), in_specs=in_specs, out_specs=out_specs
+        ),
+        out_shape=out_shape,
+        compiler_params=params(),
+        cost_estimate=cost(flops, flops // 512 + nbytes),
+    )(owner, *operands)
+
+
+def cols_of(k):
+    return slice(k * BLOCK_COLS, (k + 1) * BLOCK_COLS)
+
+
+def project_kernel(own_ref, x_ref, *rest):
+    o_ref = rest[-1]
+    for g, w_ref in enumerate(rest[:-1]):
+        o_ref[:, cols_of(g)] = dot_nn(x_ref[...], block_of(w_ref))
 
 
 def project(rows_in, gathered, owner, first, count):
-    rows, _, depth, _ = gathered.shape
     length = rows_in.shape[0]
+    return slot_call(
+        project_kernel,
+        owner,
+        count // GROUP,
+        [whole((length, D))] + [slot_spec(gathered, first + g, GROUP) for g in range(GROUP)],
+        pl.BlockSpec((length, GROUP * BLOCK_COLS), lambda k, own: (0, k)),
+        jax.ShapeDtypeStruct((length, count * BLOCK_COLS), F32),
+        2 * length * D * BLOCK_COLS * count,
+        [rows_in] + [gathered] * GROUP,
+    )
+
+
+def sigmoid(values):
+    return 1.0 / (1.0 + jnp.exp(-values))
+
+
+def gate_up_kernel(own_ref, x_ref, *rest):
+    w_refs, (gate_ref, up_ref, act_ref) = rest[:-3], rest[-3:]
+    half = len(w_refs) // 2
+    for g in range(half):
+        gate = dot_nn(x_ref[...], block_of(w_refs[g]))
+        up = dot_nn(x_ref[...], block_of(w_refs[half + g]))
+        gate_ref[:, cols_of(g)] = gate
+        up_ref[:, cols_of(g)] = up
+        act_ref[:, cols_of(g)] = (gate * sigmoid(gate) * up).astype(BF16)
+
+
+def project_gate_up(rows_in, gathered, owner, first, count):
+    length = rows_in.shape[0]
+    pairs = GROUP // 2
+    wide = pl.BlockSpec((length, pairs * BLOCK_COLS), lambda k, own: (0, k))
+    shapes = [jax.ShapeDtypeStruct((length, count * BLOCK_COLS), t) for t in (F32, F32, BF16)]
+    return slot_call(
+        gate_up_kernel,
+        owner,
+        count // pairs,
+        [whole((length, D))]
+        + [slot_spec(gathered, first + g, pairs) for g in range(pairs)]
+        + [slot_spec(gathered, first + count + g, pairs) for g in range(pairs)],
+        [wide] * 3,
+        shapes,
+        4 * length * D * BLOCK_COLS * count,
+        [rows_in] + [gathered] * (2 * pairs),
+    )
+
+
+def act_back_kernel(own_ref, x_ref, gate_ref, up_ref, *rest):
+    o_ref = rest[-1]
+    for g, w_ref in enumerate(rest[:-1]):
+        act_grad = dot_nn(x_ref[...], block_of(w_ref))
+        gate, up = gate_ref[:, cols_of(g)], up_ref[:, cols_of(g)]
+        sig = sigmoid(gate)
+        silu = gate * sig
+        o_ref[0, :, cols_of(g)] = (act_grad * up * (sig + silu * (1.0 - sig))).astype(BF16)
+        o_ref[1, :, cols_of(g)] = (act_grad * silu).astype(BF16)
+
+
+def project_act_back(rows_in, gate, up, gathered, owner, first, count):
+    length = rows_in.shape[0]
+    pairs = GROUP // 2
+    wide = pl.BlockSpec((length, pairs * BLOCK_COLS), lambda k, own: (0, k))
+    return slot_call(
+        act_back_kernel,
+        owner,
+        count // pairs,
+        [whole((length, D)), wide, wide]
+        + [slot_spec(gathered, first + g, pairs) for g in range(pairs)],
+        pl.BlockSpec((2, length, pairs * BLOCK_COLS), lambda k, own: (0, 0, k)),
+        jax.ShapeDtypeStruct((2, length, count * BLOCK_COLS), BF16),
+        2 * length * D * BLOCK_COLS * count,
+        [rows_in, gate, up] + [gathered] * pairs,
+    )
+
+
+def add_products(c_refs, w_refs, o_ref):
+    cols = [c_ref[...].reshape(-1, c_ref.shape[-1]) for c_ref in c_refs]
+    cols = cols[0] if len(cols) == 1 else jnp.concatenate(cols, axis=1)
+    o_ref[...] += dot_nt(cols, jnp.concatenate([block_of(w) for w in w_refs], axis=1))
+
+
+def row_parts(length):
+    return [slice(i, i + ROW_PART) for i in range(0, length, ROW_PART)]
+
+
+def back_norm_kernel(own_ref, c_ref, *rest):
+    w_refs, (base_ref, gain_ref, o_ref, n_ref) = rest[:-4], rest[-4:]
+
+    @pl.when(pl.program_id(0) == 0)
+    def _():
+        o_ref[...] = base_ref[...].astype(F32)
+
+    add_products([c_ref], w_refs, o_ref)
+
+    @pl.when(pl.program_id(0) == pl.num_programs(0) - 1)
+    def _():
+        for part in row_parts(o_ref.shape[0]):
+            n_ref[part, :] = rms_gain(o_ref[part, :], gain_ref[...]).astype(BF16)
+
+
+def back_then_norm(cols_in, gathered, owner, first, count, base, gain):
+    length = cols_in.shape[0]
+    return slot_call(
+        back_norm_kernel,
+        owner,
+        count // GROUP,
+        [pl.BlockSpec((length, GROUP * BLOCK_COLS), lambda k, own: (0, k))]
+        + [slot_spec(gathered, first + g, GROUP) for g in range(GROUP)]
+        + [whole((length, D)), whole((1, D))],
+        [whole((length, D))] * 2,
+        [jax.ShapeDtypeStruct((length, D), t) for t in (F32, BF16)],
+        2 * length * D * BLOCK_COLS * count,
+        [cols_in] + [gathered] * GROUP + [base, gain.reshape(1, D)],
+    )
+
+
+def back_grad_kernel(parts, own_ref, *rest):
+    c_refs, rest = rest[:parts], rest[parts:]
+    w_refs, rest = rest[:-8], rest[-8:]
+    start_ref, x_ref, gain_ref, more_ref, o_ref, low_ref, dgain_ref, total = rest
+
+    @pl.when(pl.program_id(0) == 0)
+    def _():
+        total[...] = start_ref[...]
+
+    add_products(c_refs, w_refs, total)
+
+    @pl.when(pl.program_id(0) == pl.num_programs(0) - 1)
+    def _():
+        dgain = jnp.zeros((1, D), F32)
+        for part in row_parts(total.shape[0]):
+            x, grad = x_ref[part, :].astype(F32), total[part, :]
+            inv = lax.rsqrt(jnp.mean(x * x, axis=-1, keepdims=True) + 1e-05)
+            unit = x * inv
+            dgain += jnp.sum(grad * unit, axis=0, keepdims=True)
+            scaled = grad * gain_ref[...]
+            back = inv * (scaled - unit * jnp.mean(scaled * unit, axis=-1, keepdims=True))
+            result = more_ref[part, :] + back
+            o_ref[part, :] = result
+            low_ref[part, :] = result.astype(BF16)
+        dgain_ref[...] = dgain
+
+
+def back_through_norm(cols_in, gathered, owner, first, count, start, x, gain, more):
+    parts, length, _ = cols_in.shape
+    group = GROUP // parts
+    every = count // parts
     return pl.pallas_call(
-        project_kernel,
+        functools.partial(back_grad_kernel, parts),
         grid_spec=pltpu.PrefetchScalarGridSpec(
             num_scalar_prefetch=1,
-            grid=(count,),
+            grid=(every // group,),
             in_specs=[
-                pl.BlockSpec((length, D), lambda k, own: (0, 0)),
                 pl.BlockSpec(
-                    (rows, 1, depth, BLOCK_COLS), lambda k, own: (0, own[first + k], 0, 0)
-                ),
-            ],
-            out_specs=pl.BlockSpec((length, BLOCK_COLS), lambda k, own: (0, k)),
+                    (1, length, group * BLOCK_COLS), lambda k, own, part=part: (part, 0, k)
+                )
+                for part in range(parts)
+            ]
+            + [
+                slot_spec(gathered, first + part * every + g, group)
+                for part in range(parts)
+                for g in range(group)
+            ]
+            + [whole((length, D)), whole((length, D)), whole((1, D)), whole((length, D))],
+            out_specs=[whole((length, D)), whole((length, D)), whole((1, D))],
+            scratch_shapes=[pltpu.VMEM((length, D), F32)],
         ),
-        out_shape=jax.ShapeDtypeStruct((length, count * BLOCK_COLS), F32),
-        compiler_params=params(),
-        cost_estimate=cost(
-            2 * length * D * BLOCK_COLS * count, count * BLOCK_COLS * (2 * D + 4 * length)
-        ),
-    )(owner, rows_in, gathered)
-
-
-def back_kernel(own_ref, c_ref, w_ref, base_ref, o_ref):
-    @pl.when(pl.program_id(0) == 0)
-    def _():
-        o_ref[...] = base_ref[...]
-
-    o_ref[...] += dot_nt(c_ref[...], w_ref[...].reshape(D, BLOCK_COLS))
-
-
-def project_back(cols_in, gathered, owner, first, count, base):
-    rows, _, depth, _ = gathered.shape
-    length = cols_in.shape[0]
-    return pl.pallas_call(
-        back_kernel,
-        grid_spec=pltpu.PrefetchScalarGridSpec(
-            num_scalar_prefetch=1,
-            grid=(count,),
-            in_specs=[
-                pl.BlockSpec((length, BLOCK_COLS), lambda k, own: (0, k)),
-                pl.BlockSpec(
-                    (rows, 1, depth, BLOCK_COLS), lambda k, own: (0, own[first + k], 0, 0)
-                ),
-                pl.BlockSpec((length, D), lambda k, own: (0, 0)),
-            ],
-            out_specs=pl.BlockSpec((length, D), lambda k, own: (0, 0)),
-        ),
-        out_shape=jax.ShapeDtypeStruct((length, D), F32),
+        out_shape=[
+            jax.ShapeDtypeStruct((length, D), F32),
+            jax.ShapeDtypeStruct((length, D), BF16),
+            jax.ShapeDtypeStruct((1, D), F32),
+        ],
         compiler_params=params(),
         cost_estimate=cost(
             2 * length * D * BLOCK_COLS * count, count * BLOCK_COLS * (2 * D + 2 * length)
         ),
-    )(owner, cols_in, gathered, base)
+    )(owner, *[cols_in] * parts, *[gathered] * GROUP, start, x, gain.reshape(1, D), more)
 
 
 def wgrad_kernel(own_ref, l_ref, r_ref, *rest):
@@ -157,17 +313,18 @@
     def _():
         turned[...] = l_ref[...].T
 
-    grad = dot_nn(turned[...], r_ref[...])
+    grad = dot_nn(turned[...], r_ref[0])
     o_ref[...] = grad.astype(BF16).reshape(o_ref.shape)
 
 
 def weight_grad(left_rows, right_cols, owner, first, like, into):
     rows, nslots, depth, _ = like
     length = left_rows.shape[0]
-    count = right_cols.shape[1] // BLOCK_COLS
+    each = right_cols.shape[2] // BLOCK_COLS
+    count = right_cols.shape[0] * each
     in_specs = [
         pl.BlockSpec((length, D), lambda k, own: (0, 0)),
-        pl.BlockSpec((length, BLOCK_COLS), lambda k, own: (0, k)),
+        pl.BlockSpec((1, length, BLOCK_COLS), lambda k, own: (k // each, 0, k % each)),
     ]
     operands = [owner, left_rows, right_cols]
     aliases = {}
@@ -272,7 +429,9 @@
     return inner, jnp.where(low, high, rest).astype(BF16)
 
 
-def attn_fwd_kernel(q_ref, k_ref, v_ref, segc_ref, segr_ref, cos_ref, sin_ref, o_ref):
+def attn_fwd_kernel(
+    q_ref, k_ref, v_ref, segc_ref, segr_ref, cos_ref, sin_ref, mixed_ref, o_ref
+):
     group = pl.program_id(0) // 2
     low = lane_iota() < HEAD_DIM
     cosine, sine = cos_ref[...], sin_ref[...]
@@ -296,7 +455,31 @@
 
 
 def attn_bwd_kernel(
-    q_ref, k_ref, v_ref, segc_ref, segr_ref, cos_ref, sin_ref, g_ref, dq_ref, dkv_ref, dk_s, dv_s
+    q_ref, k_ref, v_ref, segc_ref, segr_ref, cos_ref, sin_ref, g_ref, into_ref, o_ref, dk_s, dv_s
+):
+    step = pl.program_id(0)
+    pairs = HEADS // 2
+
+    @pl.when(step < pairs)
+    def _():
+        attn_bwd_pair(
+            q_ref, k_ref, v_ref, segc_ref, segr_ref, cos_ref, sin_ref, g_ref, o_ref, dk_s, dv_s
+        )
+
+    low = lane_iota() < HEAD_DIM
+
+    @pl.when(step == pairs)
+    def _():
+        dk = jnp.where(low, fold(dk_s[0]), fold(dk_s[1]))
+        o_ref[...] = turn_back(dk, cos_ref[...], sin_ref[...]).astype(BF16)
+
+    @pl.when(step == pairs + 1)
+    def _():
+        o_ref[...] = jnp.where(low, fold(dv_s[0]), fold(dv_s[1])).astype(BF16)
+
+
+def attn_bwd_pair(
+    q_ref, k_ref, v_ref, segc_ref, segr_ref, cos_ref, sin_ref, g_ref, dq_ref, dk_s, dv_s
 ):
     step = pl.program_id(0)
     group = step // 2
@@ -339,17 +522,10 @@
         dq = jnp.where(low, dqs[0], dqs[1]) * scale
         dq_ref[rows, :] = turn_back(dq, cosine[rows], sine[rows]).astype(BF16)
 
-    @pl.when(step == pl.num_programs(0) - 1)
-    def _():
-        dk = jnp.where(low, fold(dk_s[0]), fold(dk_s[1]))
-        dv = jnp.where(low, fold(dv_s[0]), fold(dv_s[1]))
-        dkv_ref[:, :LANES] = turn_back(dk, cosine, sine).astype(BF16)
-        dkv_ref[:, LANES:] = dv.astype(BF16)
-
 
 def attention_specs(length, base):
     return [
-        pl.BlockSpec((length, LANES), lambda p: (0, base + p)),
+        pl.BlockSpec((length, LANES), lambda p: (0, base + jnp.minimum(p, 3))),
         pl.BlockSpec((length, LANES), lambda p: (0, base + 4)),
         pl.BlockSpec((length, LANES), lambda p: (0, base + 5)),
         pl.BlockSpec((length, 1), lambda p: (0, 0)),
@@ -359,42 +535,47 @@
     ]
 
 
-def attention_forward(both_proj, segc, segr, cosine, sine):
+def attention_forward(both_proj, segc, segr, cosine, sine, mixed):
     length = both_proj.shape[0]
     base = (SSM_INNER + XBC_WIDTH) // LANES
     pairs = HEADS // 2
+    at = SSM_INNER // LANES
     return pl.pallas_call(
         attn_fwd_kernel,
         grid=(pairs,),
-        in_specs=attention_specs(length, base),
-        out_specs=pl.BlockSpec((length, LANES), lambda p: (0, p)),
-        out_shape=jax.ShapeDtypeStruct((length, HEADS * HEAD_DIM), BF16),
+        in_specs=attention_specs(length, base) + [pl.BlockSpec(memory_space=pl.ANY)],
+        out_specs=pl.BlockSpec((length, LANES), lambda p: (0, at + p)),
+        out_shape=jax.ShapeDtypeStruct(mixed.shape, BF16),
+        input_output_aliases={7: 0},
         compiler_params=params(),
-        cost_estimate=cost(4 * HEADS * length * length * HEAD_DIM, 6 * length * D, HEADS * length * length // 2),
-    )(both_proj, both_proj, both_proj, segc, segr, cosine, sine)
-
-
-def attention_backward(both_proj, segc, segr, cosine, sine, grads, grad_base):
+        cost_estimate=cost(
+            4 * HEADS * length * length * HEAD_DIM, 6 * length * D, HEADS * length * length // 2
+        ),
+    )(both_proj, both_proj, both_proj, segc, segr, cosine, sine, mixed)
+
+
+def attention_backward(both_proj, segc, segr, cosine, sine, grads, into):
     length = both_proj.shape[0]
     base = (SSM_INNER + XBC_WIDTH) // LANES
+    at = SSM_INNER // LANES
     pairs = HEADS // 2
     return pl.pallas_call(
         attn_bwd_kernel,
-        grid=(pairs,),
+        grid=(pairs + 2,),
         in_specs=attention_specs(length, base)
-        + [pl.BlockSpec((length, LANES), lambda p: (0, grad_base + p))],
-        out_specs=[
-            pl.BlockSpec((length, LANES), lambda p: (0, p)),
-            pl.BlockSpec((length, 2 * LANES), lambda p: (0, 0)),
+        + [
+            pl.BlockSpec((length, LANES), lambda p: (0, at + jnp.minimum(p, 3))),
+            pl.BlockSpec(memory_space=pl.ANY),
         ],
-        out_shape=[
-            jax.ShapeDtypeStruct((length, HEADS * HEAD_DIM), BF16),
-            jax.ShapeDtypeStruct((length, 2 * LANES), BF16),
-        ],
+        out_specs=pl.BlockSpec((length, LANES), lambda p: (0, base + p)),
+        out_shape=jax.ShapeDtypeStruct(into.shape, BF16),
+        input_output_aliases={8: 0},
         scratch_shapes=[pltpu.VMEM((2, length, LANES), F32)] * 2,
         compiler_params=params(),
-        cost_estimate=cost(10 * HEADS * length * length * HEAD_DIM, 10 * length * D, HEADS * length * length // 2),
-    )(both_proj, both_proj, both_proj, segc, segr, cosine, sine, grads)
+        cost_estimate=cost(
+            10 * HEADS * length * length * HEAD_DIM, 10 * length * D, HEADS * length * length // 2
+        ),
+    )(both_proj, both_proj, both_proj, segc, segr, cosine, sine, grads, into)
 
 
 def chunk_masks(segc_ref, segr_ref, last_ref, chunk):
@@ -429,15 +610,28 @@
 
 
 def ssm_fwd_kernel(
-    last_ref, xbc_ref, dt_ref, cum_ref, cumt_ref, skip_ref, segc_ref, segr_ref,
-    y_ref, s_ref, state,
+    last_ref, proj_ref, near_ref, cw_ref, cb_ref, gain_ref, dt_ref, cum_ref, cumt_ref, skip_ref,
+    segc_ref, segr_ref, y_ref, s_ref, xbc_ref, slope_ref, mix_ref, state, ext,
 ):
     chunk = pl.program_id(0)
 
     @pl.when(chunk == 0)
     def _():
         state[...] = jnp.zeros_like(state)
-
+        ext[:8, :] = jnp.zeros((8, XBC_WIDTH), F32)
+
+    ext[8:, :] = proj_ref[:, SSM_INNER : SSM_INNER + XBC_WIDTH]
+    for k in range(XBC_WIDTH // BLOCK_COLS):
+        cols = cols_of(k)
+        total = ext[8:, cols] * cw_ref[CONV - 1 :, cols] + cb_ref[:, cols]
+        for d in range(1, CONV):
+            taken = ext[8 - d : 8 - d + CHUNK, cols] * near_ref[:, d : d + 1]
+            total += taken * cw_ref[CONV - 1 - d : CONV - d, cols]
+        sig = sigmoid(total)
+        silu = total * sig
+        xbc_ref[:, cols] = silu
+        slope_ref[:, cols] = sig + silu * (1.0 - sig)
+    ext[:8, :] = ext[CHUNK:, :]
     s_ref[...] = state[...].reshape(s_ref.shape)
     low = lane_iota() < SSM_HEAD_DIM
     madd, carried, tail, keep = chunk_masks(segc_ref, segr_ref, last_ref, chunk)
@@ -476,18 +670,52 @@
         tail_in = wide_split(scaled * spread(low, tails, a))
         fresh = both_sides(dot_nn(into_both, jnp.concatenate([tail_in, tail_in], axis=0)))
         state[:, cols] = spread(low, keeps, a) * old + fresh
+    squares = jnp.zeros((CHUNK, 1), F32)
+    for k in range(SSM_INNER // BLOCK_COLS):
+        gate = proj_ref[:, cols_of(k)]
+        gated = y_ref[:, cols_of(k)] * (gate * sigmoid(gate))
+        squares += jnp.sum(gated * gated, axis=-1, keepdims=True)
+    inv = lax.rsqrt(squares / SSM_INNER + 1e-05)
+    for k in range(SSM_INNER // BLOCK_COLS):
+        gate = proj_ref[:, cols_of(k)]
+        gated = y_ref[:, cols_of(k)] * (gate * sigmoid(gate))
+        mix_ref[:, cols_of(k)] = (gated * inv * gain_ref[:, cols_of(k)]).astype(BF16)
 
 
 def ssm_bwd_kernel(
-    last_ref, xbc_ref, dt_ref, cum_ref, cumt_ref, skip_ref, segc_ref, segr_ref, s_ref, n_ref,
-    y_ref, g_ref, dxbc_ref, sums_ref, ends_ref, dstate,
+    last_ref, proj_ref, near_ref, cw_ref, gain_ref, xbc_ref, slope_ref, dt_ref, cum_ref, cumt_ref,
+    skip_ref, segc_ref, segr_ref, s_ref, n_ref, y_ref, out_ref, grad_ref, sums_ref, ends_ref,
+    vec_ref, dstate, g_ref, dext,
 ):
     chunk = pl.num_programs(0) - 1 - pl.program_id(0)
 
     @pl.when(pl.program_id(0) == 0)
     def _():
         dstate[...] = jnp.zeros_like(dstate)
-
+        dext[CHUNK:, :] = jnp.zeros((8, XBC_WIDTH), F32)
+        vec_ref[...] = jnp.zeros_like(vec_ref)
+
+    squares = jnp.zeros((CHUNK, 1), F32)
+    along = jnp.zeros((CHUNK, 1), F32)
+    for k in range(SSM_INNER // BLOCK_COLS):
+        cols = cols_of(k)
+        gate = proj_ref[:, cols]
+        gated = y_ref[:, cols] * (gate * sigmoid(gate))
+        squares += jnp.sum(gated * gated, axis=-1, keepdims=True)
+        along += jnp.sum(gated * out_ref[:, cols] * gain_ref[:, cols], axis=-1, keepdims=True)
+    inv = lax.rsqrt(squares / SSM_INNER + 1e-05)
+    along = along * inv / SSM_INNER
+    for k in range(SSM_INNER // BLOCK_COLS):
+        cols = cols_of(k)
+        gate = proj_ref[:, cols]
+        sig = sigmoid(gate)
+        silu = gate * sig
+        unit = y_ref[:, cols] * silu * inv
+        vec_ref[5:6, cols] += jnp.sum(out_ref[:, cols] * unit, axis=0, keepdims=True)
+        gated_grad = inv * (out_ref[:, cols] * gain_ref[:, cols] - unit * along)
+        g_ref[:, cols] = gated_grad * silu
+        gate_grad = gated_grad * y_ref[:, cols] * (sig + silu * (1.0 - sig))
+        grad_ref[:, cols] = gate_grad.astype(BF16)
     low = lane_iota() < SSM_HEAD_DIM
     madd, carried, tail, keep = chunk_masks(segc_ref, segr_ref, last_ref, chunk)
     dt, cum, cumt = dt_ref[...], cum_ref[...], cumt_ref[...]
@@ -551,127 +779,184 @@
             :LANES
         ].astype(F32)
         dstate[:, cols] = keep_wide * d_new + dot_nn(outof_t, d_carry)
-        dxbc_ref[:, cols] = d_scaled * dt_wide + skip_wide * grad
+        dext[:CHUNK, cols] = (d_scaled * dt_wide + skip_wide * grad) * slope_ref[:, cols]
         both = grad * heads
         sum_y += by_head(grad * y_ref[:, cols] - skip_wide * both - scaled * d_scaled, pick)
         sum_x += by_head(heads * d_scaled, pick)
         sum_k += by_head(both, pick)
     dgram_low = dgram.astype(BF16)
-    dxbc_ref[:, SSM_INNER : SSM_INNER + STATE] = d_into + dot_tn(dgram_low, outof)
-    dxbc_ref[:, SSM_INNER + STATE :] = d_outof + dot_nn(dgram_low, into)
+    cols = slice(SSM_INNER, SSM_INNER + STATE)
+    dext[:CHUNK, cols] = (d_into + dot_tn(dgram_low, outof)) * slope_ref[:, cols]
+    cols = slice(SSM_INNER + STATE, XBC_WIDTH)
+    dext[:CHUNK, cols] = (d_outof + dot_nn(dgram_low, into)) * slope_ref[:, cols]
+    for k in range(XBC_WIDTH // BLOCK_COLS):
+        cols = cols_of(k)
+        at = slice(SSM_INNER + k * BLOCK_COLS, SSM_INNER + (k + 1) * BLOCK_COLS)
+        before = proj_ref[:, at]
+        here = dext[:CHUNK, cols]
+        total = here * cw_ref[CONV - 1 :, cols]
+        vec_ref[CONV - 1 : CONV, cols] += jnp.sum(here * before, axis=0, keepdims=True)
+        vec_ref[CONV : CONV + 1, cols] += jnp.sum(here, axis=0, keepdims=True)
+        for d in range(1, CONV):
+            later = dext[d : d + CHUNK, cols] * near_ref[:, CONV + d : CONV + d + 1]
+            total += later * cw_ref[CONV - 1 - d : CONV - d, cols]
+            vec_ref[CONV - 1 - d : CONV - d, cols] += jnp.sum(later * before, axis=0, keepdims=True)
+        grad_ref[:, at] = total.astype(BF16)
+    dext[CHUNK:, :] = dext[:8, :]
     sums_ref[:, :LANES] = sum_y
     sums_ref[:, LANES : 2 * LANES] = sum_x
     sums_ref[:, 2 * LANES :] = sum_k
     ends_ref[...] = ends.reshape(ends_ref.shape)
 
 
-def ssm_forward(last, xbc, dt, cum, cumt, skip, segc, segr):
-    length = xbc.shape[0]
+def scan_specs(at):
+    here = lambda i, last: (at(i), 0)
+    across = lambda i, last: (0, at(i))
+    return dict(
+        rows=lambda width: pl.BlockSpec((CHUNK, width), here),
+        cols=lambda height: pl.BlockSpec((height, CHUNK), across),
+        fixed=lambda *shape: pl.BlockSpec(shape, lambda i, last: (0,) * len(shape)),
+    )
+
+
+def ssm_forward(last, both_proj, near, conv_w, conv_b, gain, dt, cum, cumt, skip, segc, segr):
+    length, width = both_proj.shape
     chunks = length // CHUNK
-    here = lambda c, last: (c, 0)
-    across = lambda c, last: (0, c)
+    spec = scan_specs(lambda i: i)
     return pl.pallas_call(
         ssm_fwd_kernel,
         grid_spec=pltpu.PrefetchScalarGridSpec(
             num_scalar_prefetch=1,
             grid=(chunks,),
             in_specs=[
-                pl.BlockSpec((CHUNK, XBC_WIDTH), here),
-                pl.BlockSpec((CHUNK, SSM_HEADS), here),
-                pl.BlockSpec((CHUNK, SSM_HEADS), here),
-                pl.BlockSpec((SSM_HEADS, CHUNK), across),
-                pl.BlockSpec((1, SSM_HEADS), lambda c, last: (0, 0)),
-                pl.BlockSpec((CHUNK, 1), here),
-                pl.BlockSpec((1, CHUNK), across),
+                spec["rows"](width),
+                spec["rows"](2 * CONV),
+                spec["fixed"](CONV, XBC_WIDTH),
+                spec["fixed"](1, XBC_WIDTH),
+                spec["fixed"](1, SSM_INNER),
+                spec["rows"](SSM_HEADS),
+                spec["rows"](SSM_HEADS),
+                spec["cols"](SSM_HEADS),
+                spec["fixed"](1, SSM_HEADS),
+                spec["rows"](1),
+                spec["cols"](1),
             ],
             out_specs=[
-                pl.BlockSpec((CHUNK, SSM_INNER), here),
+                spec["rows"](SSM_INNER),
                 pl.BlockSpec((1, STATE, SSM_INNER), lambda c, last: (c, 0, 0)),
+                spec["rows"](XBC_WIDTH),
+                spec["rows"](XBC_WIDTH),
+                spec["rows"](SSM_INNER + HEADS * HEAD_DIM),
             ],
-            scratch_shapes=[pltpu.VMEM((STATE, SSM_INNER), F32)],
+            scratch_shapes=[
+                pltpu.VMEM((STATE, SSM_INNER), F32),
+                pltpu.VMEM((CHUNK + 8, XBC_WIDTH), F32),
+            ],
         ),
         out_shape=[
             jax.ShapeDtypeStruct((length, SSM_INNER), F32),
             jax.ShapeDtypeStruct((chunks, STATE, SSM_INNER), F32),
+            jax.ShapeDtypeStruct((length, XBC_WIDTH), F32),
+            jax.ShapeDtypeStruct((length, XBC_WIDTH), F32),
+            jax.ShapeDtypeStruct((length, SSM_INNER + HEADS * HEAD_DIM), BF16),
         ],
         compiler_params=params(),
         cost_estimate=cost(
-            8 * length * SSM_INNER * STATE, 24 * length * SSM_INNER, length * CHUNK * SSM_HEADS
+            8 * length * SSM_INNER * STATE, 40 * length * SSM_INNER, length * CHUNK * SSM_HEADS
         ),
-    )(last, xbc, dt, cum, cumt, skip, segc, segr)
-
-
-def ssm_backward(last, xbc, dt, cum, cumt, skip, segc, segr, states, outputs, grads):
-    length = xbc.shape[0]
+    )(last, both_proj, near, conv_w, conv_b, gain, dt, cum, cumt, skip, segc, segr)
+
+
+def ssm_backward(
+    last, both_proj, near, conv_w, gain, xbc, slope, dt, cum, cumt, skip, segc, segr, states, outputs,
+    grads,
+):
+    length, width = both_proj.shape
     chunks = length // CHUNK
     end = chunks - 1
-    here = lambda i, last: (end - i, 0)
-    across = lambda i, last: (0, end - i)
+    spec = scan_specs(lambda i: end - i)
     return pl.pallas_call(
         ssm_bwd_kernel,
         grid_spec=pltpu.PrefetchScalarGridSpec(
             num_scalar_prefetch=1,
             grid=(chunks,),
             in_specs=[
-                pl.BlockSpec((CHUNK, XBC_WIDTH), here),
-                pl.BlockSpec((CHUNK, SSM_HEADS), here),
-                pl.BlockSpec((CHUNK, SSM_HEADS), here),
-                pl.BlockSpec((SSM_HEADS, CHUNK), across),
-                pl.BlockSpec((1, SSM_HEADS), lambda i, last: (0, 0)),
-                pl.BlockSpec((CHUNK, 1), here),
-                pl.BlockSpec((1, CHUNK), across),
+                spec["rows"](width),
+                spec["rows"](2 * CONV),
+                spec["fixed"](CONV, XBC_WIDTH),
+                spec["fixed"](1, SSM_INNER),
+                spec["rows"](XBC_WIDTH),
+                spec["rows"](XBC_WIDTH),
+                spec["rows"](SSM_HEADS),
+                spec["rows"](SSM_HEADS),
+                spec["cols"](SSM_HEADS),
+                spec["fixed"](1, SSM_HEADS),
+                spec["rows"](1),
+                spec["cols"](1),
                 pl.BlockSpec((1, STATE, SSM_INNER), lambda i, last: (end - i, 0, 0)),
                 pl.BlockSpec(
                     (1, STATE, SSM_INNER), lambda i, last: (jnp.minimum(end - i + 1, end), 0, 0)
                 ),
-                pl.BlockSpec((CHUNK, SSM_INNER), here),
-                pl.BlockSpec((CHUNK, SSM_INNER), here),
+                spec["rows"](SSM_INNER),
+                spec["rows"](grads.shape[1]),
             ],
             out_specs=[
-                pl.BlockSpec((CHUNK, XBC_WIDTH), here),
-                pl.BlockSpec((CHUNK, 3 * LANES), here),
+                spec["rows"](width),
+                spec["rows"](3 * LANES),
                 pl.BlockSpec((1, 8, LANES), lambda i, last: (end - i, 0, 0)),
+                spec["fixed"](8, XBC_WIDTH),
             ],
-            scratch_shapes=[pltpu.VMEM((STATE, SSM_INNER), F32)],
+            scratch_shapes=[
+                pltpu.VMEM((STATE, SSM_INNER), F32),
+                pltpu.VMEM((CHUNK, SSM_INNER), F32),
+                pltpu.VMEM((CHUNK + 8, XBC_WIDTH), F32),
+            ],
         ),
         out_shape=[
-            jax.ShapeDtypeStruct((length, XBC_WIDTH), F32),
+            jax.ShapeDtypeStruct((length, width), BF16),
             jax.ShapeDtypeStruct((length, 3 * LANES), F32),
             jax.ShapeDtypeStruct((chunks, 8, LANES), F32),
+            jax.ShapeDtypeStruct((8, XBC_WIDTH), F32),
         ],
         compiler_params=params(),
         cost_estimate=cost(
-            24 * length * SSM_INNER * STATE, 40 * length * SSM_INNER, length * CHUNK * SSM_HEADS
+            24 * length * SSM_INNER * STATE, 60 * length * SSM_INNER, length * CHUNK * SSM_HEADS
         ),
-    )(last, xbc, dt, cum, cumt, skip, segc, segr, states, states, outputs, grads)
-
-
-def conv_act(conv_in, conv_weight, conv_bias, segment):
-    length = conv_in.shape[0]
-    kernel = conv_weight.reshape(CONV, XBC_WIDTH)
-    conv_sum = jnp.zeros_like(conv_in) + conv_bias[None, :]
-    for offset in range(CONV):
-        shift_by = CONV - 1 - offset
-        shifted = jnp.pad(conv_in, ((shift_by, 0), (0, 0)))[:length]
-        doc_shift = jnp.pad(segment, (shift_by, 0), constant_values=-1)[:length]
-        same_doc = (doc_shift == segment).astype(F32)[:, None]
-        conv_sum = conv_sum + kernel[offset][None, :] * shifted * same_doc
-    return jax.nn.silu(conv_sum)
-
-
-def gated_norm(output, gate_part, mixer_gain):
-    return rms_gain(output * jax.nn.silu(gate_part), mixer_gain)
-
-
-def rows_kernel(lo_ref, hi_ref, ids_ref, g_ref, o_ref, wide):
+    )(
+        last, both_proj, near, conv_w, gain, xbc, slope, dt, cum, cumt, skip, segc, segr, states, states,
+        outputs, grads,
+    )
+
+
+def neighbours(segment):
+    length = segment.shape[0]
+    columns = []
+    for d in range(CONV):
+        earlier = jnp.pad(segment, (d, 0), constant_values=-1)[:length]
+        columns.append(earlier == segment)
+    for d in range(CONV):
+        later = jnp.pad(segment, (0, d), constant_values=-1)[d:]
+        columns.append(later == segment)
+    return jnp.stack(columns, axis=1).astype(F32)
+
+
+def rows_kernel(counts, lo_ref, hi_ref, ids_ref, *rest):
     step = pl.program_id(0)
+    g_refs, (o_ref, wide) = rest[:-2], rest[-2:]
+    group = wide.shape[0]
 
     @pl.when(step == 0)
     def _():
         o_ref[...] = jnp.zeros_like(o_ref)
 
-    group = g_ref.shape[0]
-    wide[...] = g_ref[...].astype(F32)
+    before = 0
+    for count, g_ref in zip(counts, g_refs):
+
+        @pl.when((step >= before) & (step < before + count))
+        def _(g_ref=g_ref):
+            wide[...] = g_ref[...].astype(F32)
+
+        before = before + count
     low, high = lo_ref[step], hi_ref[step]
 
     def one(j):
@@ -682,33 +967,46 @@
             one(low + 8 * k + u)
         return carry
 
-    def rest(j, carry):
+    def rest_of(j, carry):
         one(j)
         return carry
 
     eights = (high - low) // 8
     lax.fori_loop(0, eights, eight, 0)
-    lax.fori_loop(low + 8 * eights, high, rest, 0)
+    lax.fori_loop(low + 8 * eights, high, rest_of, 0)
 
 
 def rows_by_token(local_ids, grads, shard_rows, group):
-    count, width = grads.shape
+    width = grads[0].shape[1]
+    counts = [g.shape[0] // group for g in grads]
     lists = local_ids.reshape(-1, group)
     low = jnp.sum((lists < 0).astype(jnp.int32), axis=1)
     high = jnp.sum((lists < shard_rows).astype(jnp.int32), axis=1)
+    specs, before = [], 0
+    for count in counts:
+        specs.append(
+            pl.BlockSpec(
+                (group, width),
+                lambda i, lo, hi, ids, before=before, count=count: (
+                    jnp.clip(i - before, 0, count - 1),
+                    0,
+                ),
+            )
+        )
+        before = before + count
     return pl.pallas_call(
-        rows_kernel,
+        functools.partial(rows_kernel, counts),
         grid_spec=pltpu.PrefetchScalarGridSpec(
             num_scalar_prefetch=3,
-            grid=(count // group,),
-            in_specs=[pl.BlockSpec((group, width), lambda i, lo, hi, ids: (i, 0))],
+            grid=(before,),
+            in_specs=specs,
             out_specs=pl.BlockSpec((shard_rows, width), lambda i, lo, hi, ids: (0, 0)),
             scratch_shapes=[pltpu.VMEM((group, width), F32)],
         ),
         out_shape=jax.ShapeDtypeStruct((shard_rows, width), F32),
         compiler_params=params(),
-        cost_estimate=cost(count * width * LANES, count * width * 2),
-    )(low, high, local_ids, grads)
+        cost_estimate=cost(before * group * width * LANES, before * group * width * 2),
+    )(low, high, local_ids, *grads)
 
 
 def split_nn(left, right):
@@ -776,50 +1074,72 @@
     )(scales, rotated, block_first, block_second, left_basis, right_basis)
 
 
-def total_kernel(rows, cols, x_ref, o_ref, inbox, send_sem, recv_sem):
-    row, col = lax.axis_index("row"), lax.axis_index("col")
-    partners = []
-    bit = 1
-    while bit < cols:
-        partners.append((row, col + bit - 2 * bit * (col // bit % 2)))
-        bit = bit * 2
-    bit = 1
-    while bit < rows:
-        partners.append((row + bit - 2 * bit * (row // bit % 2), col))
-        bit = bit * 2
+def to_peers(axis, extent, place, src, box, send_sem, recv_sem):
+    copies = []
+    for k in range(1, extent):
+        peer = list(place)
+        peer[axis] = lax.rem(place[axis] + k, extent)
+        copies.append(
+            pltpu.make_async_remote_copy(
+                src_ref=src,
+                dst_ref=box.at[place[axis]],
+                send_sem=send_sem.at[k],
+                recv_sem=recv_sem.at[k],
+                device_id=tuple(peer),
+                device_id_type=MESH,
+            )
+        )
+    return copies
+
+
+def greet_peers(axes, place):
     barrier = pltpu.get_barrier_semaphore()
-    for partner in partners:
-        pl.semaphore_signal(barrier, inc=1, device_id=partner, device_id_type=MESH)
-    pl.semaphore_wait(barrier, len(partners))
-    o_ref[...] = x_ref[...]
-    for step, partner in enumerate(partners):
-        copy = pltpu.make_async_remote_copy(
-            src_ref=o_ref,
-            dst_ref=inbox.at[step],
-            send_sem=send_sem.at[step],
-            recv_sem=recv_sem.at[step],
-            device_id=partner,
-            device_id_type=MESH,
-        )
-        copy.start()
-        copy.wait()
-        o_ref[...] += inbox[step]
+    count = 0
+    for axis, extent in axes:
+        for k in range(1, extent):
+            peer = list(place)
+            peer[axis] = lax.rem(place[axis] + k, extent)
+            pl.semaphore_signal(barrier, inc=1, device_id=tuple(peer), device_id_type=MESH)
+            count += 1
+    pl.semaphore_wait(barrier, count)
+
+
+def total_kernel(rows, cols, x_ref, o_ref, col_box, row_box, col_send, col_recv, row_send, row_recv):
+    place = (lax.axis_index("row"), lax.axis_index("col"))
+    greet_peers(((0, rows), (1, cols)), place)
+    total = x_ref[...]
+    for axis, extent, box, send_sem, recv_sem in (
+        (1, cols, col_box, col_send, col_recv),
+        (0, rows, row_box, row_send, row_recv),
+    ):
+        o_ref[...] = total
+        box[place[axis]] = total
+        copies = to_peers(axis, extent, place, o_ref, box, send_sem, recv_sem)
+        for copy in copies:
+            copy.start()
+        for copy in copies:
+            copy.wait()
+        total = jnp.sum(box[...], axis=0)
+    o_ref[...] = total
 
 
 def total_over_all(values, rows, cols, collective_id):
-    steps = (rows - 1).bit_length() + (cols - 1).bit_length()
+    dma = pltpu.SemaphoreType.DMA
     return pl.pallas_call(
         functools.partial(total_kernel, rows, cols),
         in_specs=[pl.BlockSpec(memory_space=pltpu.VMEM)],
         out_specs=pl.BlockSpec(memory_space=pltpu.VMEM),
         out_shape=jax.ShapeDtypeStruct(values.shape, F32),
         scratch_shapes=[
-            pltpu.VMEM((steps,) + values.shape, F32),
-            pltpu.SemaphoreType.DMA((steps,)),
-            pltpu.SemaphoreType.DMA((steps,)),
+            pltpu.VMEM((cols,) + values.shape, F32),
+            pltpu.VMEM((rows,) + values.shape, F32),
+            dma((cols,)),
+            dma((cols,)),
+            dma((rows,)),
+            dma((rows,)),
         ],
         compiler_params=params(collective_id=collective_id, has_side_effects=True),
-        cost_estimate=cost(steps * values.size, steps * values.size * 4),
+        cost_estimate=cost(rows * cols * values.size, rows * cols * values.size * 4),
     )(values)
 
 
@@ -1065,16 +1385,241 @@
     return whole.reshape(rows, slots, depth, BLOCK_COLS), tokens.reshape(cols * count, width), total
 
 
+def doubling(place, bits):
+    def side(which):
+        axis, bit = which
+        return place[axis] // bit % 2
+
+    def partner(which):
+        axis, bit = which
+        moved = place[axis] + bit - 2 * bit * side(which)
+        return (moved, place[1]) if axis == 0 else (place[0], moved)
+
+    return side, partner
+
+
+def greet(bits, partner):
+    barrier = pltpu.get_barrier_semaphore()
+    for which in bits:
+        pl.semaphore_signal(barrier, inc=1, device_id=partner(which), device_id_type=MESH)
+    pl.semaphore_wait(barrier, len(bits))
+
+
+def joiner(side, partner, src, out, of_bits, order, after, send_sem, recv_sem):
+    def copy(k):
+        at = tuple(slice(None) if b in order[:k] else side(b) for b in of_bits)
+        region = out.at[at + after]
+        return pltpu.make_async_remote_copy(
+            src_ref=src if k == 0 else region,
+            dst_ref=region,
+            send_sem=send_sem.at[k],
+            recv_sem=recv_sem.at[k],
+            device_id=partner(order[k]),
+            device_id_type=MESH,
+        )
+
+    return copy
+
+
+def front_kernel(rows, cols, i_ref, t_ref, w_ref, io_ref, to_ref, wo_ref, *sems):
+    bits = ring_bits(rows, cols)
+    row_bits = [b for b in bits if b[0] == 0]
+    col_bits = [b for b in bits if b[0] == 1]
+    place = (lax.axis_index("row"), lax.axis_index("col"))
+    side, partner = doubling(place, bits)
+    i_send, i_recv, t_send, t_recv, w_send, w_recv, keep_sem = sems
+    greet(bits, partner)
+    own_row, own_col = tuple(side(b) for b in row_bits), tuple(side(b) for b in col_bits)
+    keeps = [
+        pltpu.make_async_copy(i_ref, io_ref.at[own_row + own_col], keep_sem.at[0]),
+        pltpu.make_async_copy(t_ref, to_ref.at[own_col], keep_sem.at[1]),
+        pltpu.make_async_copy(w_ref, wo_ref.at[own_row], keep_sem.at[2]),
+    ]
+    orders = [o[1 : len(col_bits)] + o[:1] for o in scatter_orders(rows, cols)]
+    jobs = {}
+    jobs["i", 0] = (joiner(side, partner, i_ref, io_ref, bits, bits[::-1], (), i_send, i_recv), 0, 1)
+    for p in range(t_ref.shape[0]):
+        copy = joiner(
+            side, partner, t_ref.at[p], to_ref, col_bits, orders[p % 2], (p,), t_send.at[p], t_recv.at[p]
+        )
+        jobs["t", p] = (copy, 2 + p // 2, 2)
+    for p in range(w_ref.shape[0]):
+        copy = joiner(
+            side, partner, w_ref.at[p], wo_ref, row_bits, row_bits, (p,), w_send.at[p], w_recv.at[p]
+        )
+        jobs["w", p] = (copy, 1 + p, 1)
+    run_joins(jobs, {"i": len(bits), "t": len(col_bits), "w": len(row_bits)}, keeps)
+
+
+def run_joins(jobs, stages, keeps, done=None):
+    for copy in keeps:
+        copy.start()
+    sent = []
+    for copy, _, _ in jobs.values():
+        sent.append(copy(0))
+        sent[-1].start()
+    for copy in keeps:
+        copy.wait()
+    ends = [at + every * (stages[name[0]] - 1) for name, (_, at, every) in jobs.items()]
+    for t in range(max(ends) + 1):
+        for name, (copy, at, every) in jobs.items():
+            k = (t - at) // every
+            if t < at or (t - at) % every or k >= stages[name[0]]:
+                continue
+            copy(k).wait_recv()
+            if k + 1 < stages[name[0]]:
+                sent.append(copy(k + 1))
+                sent[-1].start()
+            elif done is not None:
+                done(name[1])
+    for copy in sent:
+        copy.wait_send()
+
+
+def front_exchange(ints, table_low, weights_low, rows, cols, collective_id):
+    row_stages, col_stages = (rows - 1).bit_length(), (cols - 1).bit_length()
+    parts = TABLE_PARTS
+    shard, width = table_low.shape
+    slots = weights_low.shape[0]
+    dma = pltpu.SemaphoreType.DMA
+    ints = ints.reshape(-1, LANES)
+    outs = pl.pallas_call(
+        functools.partial(front_kernel, rows, cols),
+        in_specs=[pl.BlockSpec(memory_space=pl.ANY)] * 3,
+        out_specs=[pl.BlockSpec(memory_space=pltpu.VMEM)] * 3,
+        out_shape=[
+            jax.ShapeDtypeStruct((2,) * (row_stages + col_stages) + ints.shape, jnp.int32),
+            jax.ShapeDtypeStruct((2,) * col_stages + (parts, shard // parts, width), BF16),
+            jax.ShapeDtypeStruct((2,) * row_stages + weights_low.shape, BF16),
+        ],
+        scratch_shapes=[
+            dma((row_stages + col_stages,)),
+            dma((row_stages + col_stages,)),
+            dma((parts, col_stages)),
+            dma((parts, col_stages)),
+            dma((slots, row_stages)),
+            dma((slots, row_stages)),
+            dma((3,)),
+        ],
+        compiler_params=params(collective_id=collective_id, has_side_effects=True),
+        cost_estimate=cost(1 << 20, cols * shard * width * 4),
+    )(ints, table_low.reshape(parts, shard // parts, width), weights_low)
+    return (
+        outs[0].reshape(rows, cols, -1),
+        outs[1].reshape(cols * shard, width),
+        outs[2].reshape((rows,) + weights_low.shape),
+    )
+
+
+def weights_kernel(rows, cols, w_ref, o_ref, box, send_sem, recv_sem, keep_sem, out_sem):
+    bits = ring_bits(rows, cols)
+    col_bits = [b for b in bits if b[0] == 1]
+    place = (lax.axis_index("row"), lax.axis_index("col"))
+    side, partner = doubling(place, bits)
+    greet(col_bits, partner)
+    own = tuple(side(b) for b in col_bits)
+    slots, half = w_ref.shape[1], w_ref.shape[2] // 2
+    orders = [o[1 : len(col_bits)] + o[:1] for o in scatter_orders(rows, cols)]
+    keeps = [
+        pltpu.make_async_copy(w_ref, box.at[(slice(None),) + own], keep_sem),
+    ]
+    jobs = {}
+    outs = []
+
+    def done(u):
+        part = (slice(None),) * (1 + len(col_bits)) + parts[u]
+        outs.append(pltpu.make_async_copy(box.at[part], o_ref.at[part], out_sem.at[u]))
+        outs[-1].start()
+
+    parts = [(slot, slice(h * half, (h + 1) * half)) for slot in range(slots) for h in range(2)]
+    for slot in range(slots):
+        for h in range(2):
+            part = (slot, slice(h * half, (h + 1) * half))
+            u = 2 * slot + h
+
+            def copy(k, part=part, order=orders[h], u=u):
+                at = tuple(slice(None) if b in order[:k] else side(b) for b in col_bits)
+                region = box.at[(slice(None),) + at + part]
+                return pltpu.make_async_remote_copy(
+                    src_ref=w_ref.at[(slice(None),) + part] if k == 0 else region,
+                    dst_ref=region,
+                    send_sem=send_sem.at[u, k],
+                    recv_sem=recv_sem.at[u, k],
+                    device_id=partner(order[k]),
+                    device_id_type=MESH,
+                )
+
+            jobs["w", u] = (copy, slot, 1)
+    run_joins(jobs, {"w": len(col_bits)}, keeps, done)
+    for copy in outs:
+        copy.wait()
+
+
+def gather_weights(weights, rows, cols, collective_id):
+    _, slots, depth, width = weights.shape
+    col_stages = (cols - 1).bit_length()
+    dma = pltpu.SemaphoreType.DMA
+    shape = (rows,) + (2,) * col_stages + (slots, depth, width)
+    out = pl.pallas_call(
+        functools.partial(weights_kernel, rows, cols),
+        in_specs=[pl.BlockSpec(memory_space=pl.ANY)],
+        out_specs=pl.BlockSpec(memory_space=pl.ANY),
+        out_shape=jax.ShapeDtypeStruct(shape, BF16),
+        scratch_shapes=[
+            pltpu.VMEM(shape, BF16),
+            dma((2 * slots, col_stages)),
+            dma((2 * slots, col_stages)),
+            dma,
+            dma((2 * slots,)),
+        ],
+        compiler_params=params(collective_id=collective_id, has_side_effects=True),
+        cost_estimate=cost(1 << 20, 4 * cols * weights.size),
+    )(weights)
+    return out.reshape(rows, cols * slots, depth, width)
+
+
+def columns_kernel(cols, x_ref, o_ref, send_sem, recv_sem):
+    place = (lax.axis_index("row"), lax.axis_index("col"))
+    greet_peers(((1, cols),), place)
+    o_ref[place[1]] = x_ref[...]
+    copies = to_peers(1, cols, place, x_ref, o_ref, send_sem, recv_sem)
+    for copy in copies:
+        copy.start()
+    for copy in copies:
+        copy.wait()
+
+
+def gather_columns(values, cols, collective_id):
+    dma = pltpu.SemaphoreType.DMA
+    return pl.pallas_call(
+        functools.partial(columns_kernel, cols),
+        in_specs=[pl.BlockSpec(memory_space=pltpu.VMEM)],
+        out_specs=pl.BlockSpec(memory_space=pltpu.VMEM),
+        out_shape=jax.ShapeDtypeStruct((cols,) + values.shape, values.dtype),
+        scratch_shapes=[dma((cols,)), dma((cols,))],
+        compiler_params=params(collective_id=collective_id, has_side_effects=True),
+        cost_estimate=cost(1024, cols * values.size * 4),
+    )(values)
+
+
+def piece_order(rows):
+    order = [0] + [k for pair in range(1, rows // 2 + 1) for k in (pair, rows - pair)][: rows - 1]
+    return order[: rows // 2], order[rows // 2 :]
+
+
 def exchange_rows(values, rows):
     row = lax.axis_index("row")
     width = values.shape[1] // rows
     arrived = []
-    for k in range(rows):
-        part = lax.dynamic_slice_in_dim(values, (row + k) % rows * width, width, 1)
-        if k > 0:
-            part = lax.ppermute(part, "row", [(r, (r + k) % rows) for r in range(rows)])
-        arrived.append(part)
-    return jnp.concatenate(arrived, axis=0)
+    for group in piece_order(rows):
+        parts = []
+        for k in group:
+            part = lax.dynamic_slice_in_dim(values, (row + k) % rows * width, width, 1)
+            if k > 0:
+                part = lax.ppermute(part, "row", [(r, (r + k) % rows) for r in range(rows)])
+            parts.append(part)
+        arrived.append(jnp.concatenate(parts, axis=0))
+    return arrived
 
 
 def adam_step(weights, grads, first, second, steps_done, decay, rate):
@@ -1132,30 +1677,33 @@
     table_low = table.astype(BF16)
     shard_padded = -(-shard_rows // PAD_ROWS) * PAD_ROWS
     padded = jnp.pad(table_low, ((0, shard_padded - shard_rows), (0, 0)))
-    table_cols = lax.all_gather(padded, "col", axis=0, tiled=True)
     order = jnp.argsort(tokens)
-    sent = jnp.concatenate(
-        [tokens, jnp.sort(tokens), loss_targets[0], loss_valid[0]]
-    ).reshape(1, -1)
-    ints = lax.all_gather(sent, ("row", "col"), axis=0, tiled=True).reshape(rows, cols, -1)
-    gathered = lax.all_gather(
-        block_weights.astype(BF16), ("row", "col"), axis=0, tiled=True
-    ).reshape(rows, nblocks, depth, BLOCK_COLS)
+    sent = jnp.concatenate([tokens, jnp.sort(tokens), loss_targets[0], loss_valid[0]])
+    ints, table_cols, weight_rows = front_exchange(
+        sent, padded, block_weights.astype(BF16), rows, cols, 2
+    )
+    padded, weight_rows, table_cols = lax.optimization_barrier((padded, weight_rows, table_cols))
     table_rows = lax.all_gather(padded, "row", axis=1, tiled=True)
     token_list = lax.dynamic_index_in_dim(ints, col_index, 1, False)[:, :length].reshape(-1)
     owners = token_list // shard_rows
     looked_up = jnp.take(
         table_cols, token_list + owners * (shard_padded - shard_rows), axis=0, mode="clip"
     )
+    looked_up, weight_rows = lax.optimization_barrier((looked_up, weight_rows))
     embedded = lax.all_to_all(looked_up, "row", split_axis=0, concat_axis=1, tiled=True)
+    gathered = gather_weights(weight_rows, rows, cols, 3)
     sorted_ints = ints[:, :, length : 2 * length]
-    sorted_all = jnp.stack(
-        [
-            lax.dynamic_index_in_dim(sorted_ints, (row_index - k) % rows, 0, False)
-            for k in range(rows)
-        ],
-        axis=1,
-    ).reshape(-1)
+    sorted_all = [
+        jnp.stack(
+            [
+                lax.dynamic_index_in_dim(sorted_ints, (row_index - k) % rows, 0, False)
+                for k in part
+            ],
+            axis=1,
+        ).reshape(-1)
+        for part in piece_order(rows)
+    ]
+    sorted_all = jnp.concatenate(sorted_all)
     labels_all = lax.dynamic_index_in_dim(ints, row_index, 0, False)[:, 2 * length :]
     targets_all = labels_all[:, :count_rows].reshape(-1)
     valid_all = labels_all[:, count_rows:].reshape(-1)
@@ -1171,9 +1719,7 @@
     last_docs = segment.reshape(chunks, CHUNK)[:, CHUNK - 1]
     cosine, sine = rope_tables(length)
 
-    embed_wide = embedded.astype(F32)
-    normed_wide, first_norm_back = jax.vjp(rms_gain, embed_wide, gain_rows[0])
-    normed = normed_wide.astype(BF16)
+    normed = rms_gain(embedded.astype(F32), gain_rows[0]).astype(BF16)
     both_proj = project(normed, gathered, block_owner, 0, in_blocks)
     time_raw = jnp.dot(normed, time_low, preferred_element_type=F32)
 
@@ -1188,31 +1734,27 @@
         length, SSM_HEADS
     )
     cumt = cum.T
-    act_xbc, conv_back = jax.vjp(
-        lambda u, w, b: conv_act(u, w, b, segment),
-        both_proj[:, SSM_INNER:in_cols],
-        conv_weight,
-        conv_bias,
-    )
-    skip_row = skip_gain[None, :]
-    scan_in = (last_docs, act_xbc, step_size, cum, cumt, skip_row, segc, segr)
-    scan_out, states = ssm_forward(*scan_in)
-    mixer_wide, gated_back = jax.vjp(gated_norm, scan_out, both_proj[:, :SSM_INNER], mixer_gain)
-    context = attention_forward(both_proj, segc, segr, cosine, sine)
-    branch_in = jnp.concatenate([mixer_wide.astype(BF16), context], axis=1)
-    hidden_one = project_back(branch_in, gathered, block_owner, branch_at, branch_blocks, embed_wide)
-    second_wide, second_norm_back = jax.vjp(rms_gain, hidden_one, gain_rows[1])
-    normed_two = second_wide.astype(BF16)
-    gate_up = project(normed_two, gathered, block_owner, gate_at, gate_blocks)
-    activated, swiglu_back = jax.vjp(swiglu, gate_up[:, :FF], gate_up[:, FF:])
-    act_low = activated.astype(BF16)
-    hidden_two = project_back(act_low, gathered, block_owner, down_at, down_blocks, hidden_one)
-    final_wide, final_norm_back = jax.vjp(rms_gain, hidden_two, gain_rows[2])
-    final_out = final_wide.astype(BF16)
+    near = neighbours(segment)
+    conv_rows = conv_weight.reshape(CONV, XBC_WIDTH)
+    gain_row = mixer_gain.reshape(1, SSM_INNER)
+    times = (step_size, cum, cumt, skip_gain[None, :], segc, segr)
+    scan_out, states, act_xbc, slope, mixed = ssm_forward(
+        last_docs, both_proj, near, conv_rows, conv_bias[None, :], gain_row, *times
+    )
+    branch_in = attention_forward(both_proj, segc, segr, cosine, sine, mixed)
+    hidden_one, normed_two = back_then_norm(
+        branch_in, gathered, block_owner, branch_at, branch_blocks, embedded, gain_rows[1]
+    )
+    gate_val, up_val, act_low = project_gate_up(
+        normed_two, gathered, block_owner, gate_at, down_blocks
+    )
+    hidden_two, final_out = back_then_norm(
+        act_low, gathered, block_owner, down_at, down_blocks, hidden_one, gain_rows[2]
+    )
     positions = loss_positions[0]
     chosen = (positions[:, None] == jnp.arange(length, dtype=jnp.int32)[None, :]).astype(BF16)
     picked_rows = jnp.dot(chosen, final_out, preferred_element_type=F32).astype(BF16)
-    rows_all = lax.all_gather(picked_rows, "col", axis=0, tiled=True)
+    rows_all = gather_columns(picked_rows, cols, 4).reshape(-1, D)
 
     logits = jnp.einsum("rd,vd->rv", rows_all, table_rows, preferred_element_type=F32)
     local_target = targets_all - col_index * shard_rows
@@ -1222,7 +1764,10 @@
     row_top = jnp.max(logits, axis=1)
     row_total = jnp.sum(jnp.exp(logits - row_top[:, None]), axis=1)
     target_logit = jnp.sum(jnp.where(onehot, logits, 0.0), axis=1)
-    parts = lax.all_gather(jnp.stack([row_top, row_total, target_logit]), "col", axis=0)
+    no_part = jnp.zeros_like(row_top)
+    parts = gather_columns(
+        jnp.stack([row_top, row_total, target_logit] + [no_part] * 5), cols, 5
+    )
     top_all = jnp.max(parts[:, 0], axis=0)
     total_all = jnp.sum(parts[:, 1] * jnp.exp(parts[:, 0] - top_all[None, :]), axis=0)
     target_all = jnp.sum(parts[:, 2], axis=0)
@@ -1245,26 +1790,42 @@
     table_loss_low, rows_grad = lax.optimization_barrier((table_loss_grad.astype(BF16), rows_grad))
     table_loss_mine = lax.psum_scatter(table_loss_low, "row", scatter_dimension=1, tiled=True)
     final_grad = jnp.zeros((length, D), F32).at[positions].add(rows_grad)
+    _, final_norm_back = jax.vjp(rms_gain, hidden_two, gain_rows[2])
     hidden_two_grad, gain_final_grad = final_norm_back(final_grad)
     down_in = hidden_two_grad.astype(BF16)
-    act_grad = project(down_in, gathered, block_owner, down_at, down_blocks)
     like = (rows, nblocks, depth, BLOCK_COLS)
-    gate_grad, up_grad = swiglu_back(act_grad)
-    gate_up_grad = jnp.concatenate([gate_grad, up_grad], axis=1).astype(BF16)
-    no_base = jnp.zeros((length, D), F32)
-    normed_two_grad = project_back(
-        gate_up_grad, gathered, block_owner, gate_at, gate_blocks, no_base
-    )
-    hidden_one_part, gain_ff_grad = second_norm_back(normed_two_grad)
-    hidden_one_grad = hidden_two_grad + hidden_one_part
-    branch_grad_low = hidden_one_grad.astype(BF16)
+    gate_up_grad = project_act_back(
+        down_in, gate_val, up_val, gathered, block_owner, down_at, down_blocks
+    )
+    hidden_one_grad, branch_grad_low, gain_ff_grad = back_through_norm(
+        gate_up_grad,
+        gathered,
+        block_owner,
+        gate_at,
+        gate_blocks,
+        jnp.zeros((length, D), F32),
+        hidden_one,
+        gain_rows[1],
+        hidden_two_grad,
+    )
     branch_out_grad = project(branch_grad_low, gathered, block_owner, branch_at, branch_blocks)
 
-    dq, dkv = attention_backward(
-        both_proj, segc, segr, cosine, sine, branch_out_grad, SSM_INNER // LANES
-    )
-    scan_grad, gate_part_grad, mixer_gain_grad = gated_back(branch_out_grad[:, :SSM_INNER])
-    xbc_grad, sums, ends = ssm_backward(*scan_in, states, scan_out, scan_grad)
+    in_grad_low, sums, ends, mixer_vectors = ssm_backward(
+        last_docs,
+        both_proj,
+        near,
+        conv_rows,
+        gain_row,
+        act_xbc,
+        slope,
+        *times,
+        states,
+        scan_out,
+        branch_out_grad,
+    )
+    in_grad_low = attention_backward(
+        both_proj, segc, segr, cosine, sine, branch_out_grad, in_grad_low
+    )
     sum_y, sum_x, sum_k = (
         sums[:, i * LANES : i * LANES + SSM_HEADS] for i in range(3)
     )
@@ -1275,38 +1836,45 @@
     time_grad, time_bias_grad, decay_log_grad = steps_back(
         (sum_x, decays_grad.reshape(length, SSM_HEADS))
     )
-    conv_in_grad, conv_weight_grad, conv_bias_grad = conv_back(xbc_grad)
-    in_grad_low = jnp.concatenate(
-        [gate_part_grad.astype(BF16), conv_in_grad.astype(BF16), dq, dkv], axis=1
-    )
     in_grad_low, table_loss_mine = lax.optimization_barrier((in_grad_low, table_loss_mine))
     time_grad_low = time_grad.astype(BF16)
     grad_time = jnp.einsum("td,th->dh", normed, time_grad_low, preferred_element_type=F32)
     time_part = jnp.einsum("th,dh->td", time_grad_low, time_low, preferred_element_type=F32)
-    normed_grad = project_back(in_grad_low, gathered, block_owner, 0, in_blocks, time_part)
-    embed_part, gain_in_grad = first_norm_back(normed_grad)
-    embed_grad = (hidden_one_grad + embed_part).astype(BF16)
+    _, embed_grad, gain_in_grad = back_through_norm(
+        in_grad_low[None],
+        gathered,
+        block_owner,
+        0,
+        in_blocks,
+        time_part,
+        embedded,
+        gain_rows[0],
+        hidden_one_grad,
+    )
     placed = (order[:, None] == jnp.arange(length, dtype=jnp.int32)[None, :]).astype(BF16)
     embed_sorted = jnp.dot(placed, embed_grad, preferred_element_type=F32).astype(BF16)
     embed_sorted, down_in, normed_two, branch_grad_low, normed = lax.optimization_barrier(
         (embed_sorted, down_in, normed_two, branch_grad_low, normed)
     )
-    pieces = exchange_rows(embed_sorted, rows)
-    grad_slots = weight_grad(down_in, act_low, block_owner, down_at, like, None)
+    early, late = exchange_rows(embed_sorted, rows)
+    grad_slots = weight_grad(down_in, act_low[None], block_owner, down_at, like, None)
     grad_slots = weight_grad(normed_two, gate_up_grad, block_owner, gate_at, like, grad_slots)
-    grad_slots = weight_grad(branch_grad_low, branch_in, block_owner, branch_at, like, grad_slots)
-    grad_slots = weight_grad(normed, in_grad_low, block_owner, 0, like, grad_slots)
-    grad_slots, pieces = lax.optimization_barrier((grad_slots, pieces))
+    early_tokens = lax.all_gather(early, "col", axis=0, tiled=True)
+    grad_slots = weight_grad(
+        branch_grad_low, branch_in[None], block_owner, branch_at, like, grad_slots
+    )
+    grad_slots = weight_grad(normed, in_grad_low[None], block_owner, 0, like, grad_slots)
+    early_tokens, late, grad_slots = lax.optimization_barrier((early_tokens, late, grad_slots))
     vector_grad = jnp.concatenate(
         [
-            conv_weight_grad,
-            conv_bias_grad,
+            mixer_vectors[:CONV].reshape(-1),
+            mixer_vectors[CONV],
             time_bias_grad,
             decay_log_grad,
             skip_grad,
-            mixer_gain_grad,
-            gain_in_grad,
-            gain_ff_grad,
+            mixer_vectors[CONV + 1, :SSM_INNER],
+            gain_in_grad[0],
+            gain_ff_grad[0],
             gain_final_grad,
             grad_time.reshape(-1),
             jnp.sum(own_loss)[None],
@@ -1315,11 +1883,12 @@
     nvec = vector_params.shape[0]
     packed_len = -(-(nvec + 1) // (8 * LANES)) * 8 * LANES
     to_sum = jnp.pad(vector_grad, (0, packed_len - nvec - 1)).reshape(-1, LANES)
-    grad_whole, grads_tokens, summed = tail_exchange(grad_slots, pieces, to_sum, rows, cols, 1)
+    grad_whole, late_tokens, summed = tail_exchange(grad_slots, late, to_sum, rows, cols, 1)
     summed = summed.reshape(-1)
     vector_total, loss_sum = summed[:nvec], summed[nvec]
-    local_tokens = sorted_all - col_index * shard_rows
-    table_input_grad = rows_by_token(local_tokens, grads_tokens, shard_rows, length)
+    table_input_grad = rows_by_token(
+        sorted_all - col_index * shard_rows, (early_tokens, late_tokens), shard_rows, length
+    )
     table_grad = table_loss_mine[:shard_rows].astype(F32) + table_input_grad
     grad_mine_wide = lax.dynamic_index_in_dim(grad_whole, row_index, 0, False).astype(F32)
     square_part = jnp.sum(grad_mine_wide * grad_mine_wide) + jnp.sum(table_grad * table_grad)

time: 1270 us -> 1140 us (0.90)
  Pallas kernels: 618 us -> 827 us
  waiting for transfers between devices: 272 us -> 90.3 us
  other arithmetic: 181 us -> 75.8 us
  blocking collectives: 54.1 us -> 0 us
    pallas_call x10 -> x14, Pallas kernels: 214 us -> 438 us  [the longest x1 113 us: gather_weights(): pl.pallas_call(functools.partial(weights_kernel, rows, cols), in_specs=[p...]
    all_gather x3 -> x1, waiting for transfers between devices: 124 us -> 0.01 us  [body(): early_tokens = lax.all_gather(early, 'col', axis=0, tiled=True)]
    all_to_all x1, waiting for transfers between devices: 75.7 us -> 0.01 us  [body(): lax.all_to_all(looked_up, 'row', split_axis=0, concat_axis=1, tiled=True)]
    all_gather x2 -> x0, blocking collectives: 54.1 us -> none  [the longest x1 44.6 us: body(): lax.all_gather(sent, ('row', 'col'), axis=0, tiled=True)]
    convert_element_type x9 -> x3, other arithmetic: 40.5 us -> 4.85 us  [the longest x2 4.01 us: body(): normed = rms_gain(embedded.astype(F32), gain_rows[0]).astype(BF16)]
    pallas_call x1, Pallas kernels: 221 us -> 186 us  [tail_exchange(): pl.pallas_call(functools.partial(tail_kernel, rows, cols, slots), in_spec...]
    pallas_call x1, Pallas kernels: 36.1 us -> 52.2 us  [ssm_backward(): pl.pallas_call(ssm_bwd_kernel, grid_spec=pltpu.PrefetchScalarGridSpec(num...]
    concatenate x4 -> x2, other arithmetic: 18 us -> 2.08 us  [exchange_rows(): arrived.append(jnp.concatenate(parts, axis=0))]
  transfers between devices with their start and end apart: 11 -> 9, of which waited for: 6 -> 3; matrix products, arithmetic and copies ran while one was open for 18% -> 11% of each run, Pallas kernels for 23% -> 39%
where the time goes in v2:
time: 1140 us; the launch traced here: 1120 us
  Pallas kernels  827 us (73%)
  waiting for transfers between devices  90.3 us (8%)
  other arithmetic  75.8 us (7%)
  local copies, waits for them, and re-layouts  54.9 us (5%)
  matrix products  45 us (4%)
  between operations  22 us (2%)
    pallas_call x1, Pallas kernels, tail_exchange(): pl.pallas_call(functools.partial(tail_kernel, rows, cols, slots), in_spec...  186 us
    pallas_call x1, Pallas kernels, gather_weights(): pl.pallas_call(functools.partial(weights_kernel, rows, cols), in_specs=[p...  113 us
    pallas_call x1, Pallas kernels, front_exchange(): pl.pallas_call(functools.partial(front_kernel, rows, cols), in_specs=[pl....  97.7 us
    pallas_call x6, Pallas kernels, slot_call(): pl.pallas_call(kernel, grid_spec=pltpu.PrefetchScalarGridSpec(num_scalar_...  80.7 us
    pallas_call x4, Pallas kernels, weight_grad(): pl.pallas_call(wgrad_kernel, grid_spec=pltpu.PrefetchScalarGridSpec(num_s...  61.9 us
    pallas_call x1, Pallas kernels, ssm_backward(): pl.pallas_call(ssm_bwd_kernel, grid_spec=pltpu.PrefetchScalarGridSpec(num...  52.2 us
    reduce_scatter x1, waiting for transfers between devices, body(): lax.psum_scatter(partial_update, 'row', scatter_dimension=1, tiled=True)  45 us
    pallas_call x2, Pallas kernels, back_through_norm(): pl.pallas_call(functools.partial(back_grad_kernel, parts), grid_spec=pltp...  42.6 us
  transfers between devices with their start and end apart: 9, of which 3 were waited for; matrix products, arithmetic and copies ran while one was open for 11% of the time, Pallas kernels for 39%

profile of v2, /device:TPU:0, one launch (start us, length us, event | category | flops | bytes accessed | tf_op | source)
XLA Modules:
  0.0 1122.4 jit_solution(17730247498661191314)
XLA Ops:
  17.4 97.7 %shard_map.257 = (s32[2,2,2,2,2,17,128]{6,5,4,3,2,1,0:T(8,128)}, bf16[2,2,2,4,1040,256]{5,4,3,2,1,0:T(8,128)(2,1)}, bf16[2,2,6,256,256]{4,3,2,1,0:T(8,128)(2,1)}) custom-call(s32[17,128]{1,0:T(8,128)} %bitcast.194, bf16[4,1040,256]{2,1,0:T(8,128)(2,1)} %bitcast.163, bf16[6,256,256]{2,1,0:T(8,128)(2,1)} %convert_element_type.97.w_ref), custom_call_target="tpu_custom_call" | custom-call | flops 1048576 | bytes 34078720 | tf_op jit(solution)/shard_map/pallas_call | solution.py:1486
  116.4 24.0 %gather_fusion = bf16[4096,256]{1,0:T(8,128)(2,1)} fusion(bf16[33280,256]{1,0:T(8,128)(2,1)} %bitcast.166, s32[4096]{0:T(1024)S(1)} %broadcast_clamp_fusion), kind=kCustom, calls=%fused_computation | custom fusion | bytes 4210688 | tf_op jit(solution)/shard_map/jit(_take)/gather | solution.py:1689
  152.1 113.1 %shard_map.258 = bf16[4,2,2,2,6,256,256]{6,5,4,3,2,1,0:T(8,128)(2,1)} custom-call(bf16[4,6,256,256]{3,2,1,0:T(8,128)(2,1)} %bitcast.174), custom_call_target="tpu_custom_call" | custom-call | flops 1048576 | bytes 50331648 | tf_op jit(solution)/shard_map/pallas_call | solution.py:1563
  288.8 15.2 %shard_map.259.proj_ref.q_ref.k_ref.v_ref = f32[1024,4096]{1,0:T(8,128)} custom-call(s32[48]{0:T(128)} %own_ref.23, bf16[1024,1024]{1,0:T(8,128)(2,1)} %multiply_convert_fusion.1.x_ref.l_ref, bf16[4,48,256,256]{3,2,1,0:T(8,128)(2,1)} %bitcast.126, bf16[4,48,256,256]{3,2,1,0:T(8,128)(2,1)} %bitcast.127, bf16[4,48,256,256]{3,2,1,0:T(8,128)(2,1)} %bitcast.128, ...), custom_call_target="tpu_custom_call" | custom-call | flops 8589934592 | bytes 18874368 | tf_op jit(solution)/shard_map/pallas_call | solution.py:108
  304.1 32.0 %shard_map.260 = (f32[1024,1536]{1,0:T(8,128)}, f32[8,128,1536]{2,1,0:T(8,128)}, f32[1024,1792]{1,0:T(8,128)}, f32[1024,1792]{1,0:T(8,128)}, bf16[1024,2048]{1,0:T(8,128)(2,1)}) custom-call(s32[8]{0:T(128)} %bitcast.203, f32[1024,4096]{1,0:T(8,128)} %shard_map.259.proj_ref.q_ref.k_ref.v_ref, f32[1024,8]{1,0:T(8,128)} %convert_element_type.101.near_ref, ...), custom_call_target="tpu_custom_call" | custom-call | flops 1610612736 | bytes 62914560 | tf_op jit(solution)/shard_map/pallas_call | solution.py:826
  336.0 24.3 %shard_map.261.c_ref = bf16[1024,2048]{1,0:T(8,128)(2,1)} custom-call(f32[1024,4096]{1,0:T(8,128)} %shard_map.259.proj_ref.q_ref.k_ref.v_ref, f32[1024,4096]{1,0:T(8,128)} %shard_map.259.proj_ref.q_ref.k_ref.v_ref, f32[1024,4096]{1,0:T(8,128)} %shard_map.259.proj_ref.q_ref.k_ref.v_ref, s32[1024,1]{1,0:T(8,128)} %copy.94.segc_ref, ...), custom_call_target="tpu_custom_call", output_to_operand_aliasing={{}: (7, {})} | custom-call | flops 2147483648 | bytes 6291456 | tf_op jit(solution)/shard_map/pallas_call | solution.py:543
  372.4 15.7 %shard_map.263 = (f32[1024,2048]{1,0:T(8,128)}, f32[1024,2048]{1,0:T(8,128)}, bf16[1024,2048]{1,0:T(8,128)(2,1)}) custom-call(s32[48]{0:T(128)} %own_ref.23, bf16[1024,1024]{1,0:T(8,128)(2,1)} %get-tuple-element.97.x_ref.l_ref, bf16[4,48,256,256]{3,2,1,0:T(8,128)(2,1)} %bitcast.134, bf16[4,48,256,256]{3,2,1,0:T(8,128)(2,1)} %bitcast.135, ...), custom_call_target="tpu_custom_call" | custom-call | flops 8589934592 | bytes 18874368 | tf_op jit(solution)/shard_map/pallas_call | solution.py:108
  388.1 12.9 %shard_map.264 = (f32[1024,1024]{1,0:T(8,128)}, bf16[1024,1024]{1,0:T(8,128)(2,1)}) custom-call(s32[48]{0:T(128)} %own_ref.23, bf16[1024,2048]{1,0:T(8,128)(2,1)} %get-tuple-element.74.c_ref, bf16[4,48,256,256]{3,2,1,0:T(8,128)(2,1)} %bitcast.140, bf16[4,48,256,256]{3,2,1,0:T(8,128)(2,1)} %bitcast.139, bf16[4,48,256,256]{3,2,1,0:T(8,128)(2,1)} %bitcast.138, ...), custom_call_target="tpu_custom_call" | custom-call | flops 4294967296 | bytes 12582912 | tf_op jit(solution)/shard_map/pallas_call | solution.py:108
  403.8 16.8 %shard_map.265 = bf16[8,64,1024]{2,1,0:T(8,128)(2,1)} custom-call(bf16[64,1024]{1,0:T(8,128)(2,1)} %convolution_convert_fusion.1.x_ref), custom_call_target="tpu_custom_call" | custom-call | flops 1024 | bytes 2097152 | tf_op jit(solution)/shard_map/pallas_call | solution.py:1594
  443.7 12.2 %fusion.53 = f32[512,1024]{1,0:T(8,128)} fusion(bf16[4160,1024]{1,0:T(8,128)(2,1)} %all-gather.3.cloned.1.call-done, f32[512,4160]{0,1:T(8,128)} %copy-done.5, f32[512]{0:T(512)S(1)} %get-tuple-element.167, f32[512]{0:T(512)S(1)} %get-tuple-element.127, s32[512]{0:T(512)S(1)} %copy-done.26, pred[4160]{0:T(1024)(128)(4,1)S(1)} %copy-done.22), kind=kOutput, calls=%fused_computation.151 | convolution fusion | flops 4376985600 | bytes 19146816 | tf_op jit(solution)/shard_map/rv,vd->rd/dot_general | solution.py:1784
  466.6 31.2 %reduce-scatter.4.cloned.1.call-done = f32[64,1024]{1,0:T(8,128)} async-done(((f32[512,1024]{1,0:T(8,128)}), f32[64,1024]{1,0:T(8,128)}) %reduce-scatter.4.cloned.1.call-update) | async-done | bytes 262160 | tf_op jit(solution)/shard_map/reduce_scatter | solution.py:1783
  514.5 15.1 %shard_map.267.rest_0_.rest_1_.r_ref = bf16[2,1024,2048]{2,1,0:T(8,128)(2,1)} custom-call(s32[48]{0:T(128)} %own_ref.23, bf16[1024,1024]{1,0:T(8,128)(2,1)} %get-tuple-element.98.x_ref.l_ref, f32[1024,2048]{1,0:T(8,128)} %get-tuple-element.80.gate_ref, f32[1024,2048]{1,0:T(8,128)} %get-tuple-element.81.up_ref, bf16[4,48,256,256]{3,2,1,0:T(8,128)(2,1)} %bitcast.142, ...), custom_call_target="tpu_custom_call" | custom-call | flops 4294967296 | bytes 10485760 | tf_op jit(solution)/shard_map/pallas_call | solution.py:108
  532.1 21.5 %shard_map.268 = (f32[1024,1024]{1,0:T(8,128)}, bf16[1024,1024]{1,0:T(8,128)(2,1)}, f32[1,1024]{1,0:T(1,128)}) custom-call(s32[48]{0:T(128)} %own_ref.23, bf16[2,1024,2048]{2,1,0:T(8,128)(2,1)} %shard_map.267.rest_0_.rest_1_.r_ref, bf16[2,1024,2048]{2,1,0:T(8,128)(2,1)} %shard_map.267.rest_0_.rest_1_.r_ref, bf16[4,48,256,256]{3,2,1,0:T(8,128)(2,1)} %bitcast.144, ...), custom_call_target="tpu_custom_call" | custom-call | flops 8589934592 | bytes 16777216 | tf_op jit(solution)/shard_map/pallas_call | solution.py:277
  563.4 52.2 %shard_map.270 = (bf16[1024,4096]{1,0:T(8,128)(2,1)}, f32[1024,384]{1,0:T(8,128)}, f32[8,8,128]{2,1,0:T(8,128)}, f32[8,1792]{1,0:T(8,128)}) custom-call(s32[8]{0:T(128)} %bitcast.204, f32[1024,4096]{1,0:T(8,128)} %shard_map.259.proj_ref.q_ref.k_ref.v_ref, f32[1024,8]{1,0:T(8,128)} %convert_element_type.101.near_ref, f32[4,1792]{1,0:T(4,128)} %reshape.308.cw_ref, ...), custom_call_target="tpu_custom_call" | custom-call | flops 4831838208 | bytes 94371840 | tf_op jit(solution)/shard_map/pallas_call | solution.py:878
  623.8 39.3 %shard_map.271 = bf16[1024,4096]{1,0:T(8,128)(2,1)} custom-call(f32[1024,4096]{1,0:T(8,128)} %shard_map.259.proj_ref.q_ref.k_ref.v_ref, f32[1024,4096]{1,0:T(8,128)} %shard_map.259.proj_ref.q_ref.k_ref.v_ref, f32[1024,4096]{1,0:T(8,128)} %shard_map.259.proj_ref.q_ref.k_ref.v_ref, s32[1024,1]{1,0:T(8,128)} %copy.94.segc_ref, ...), custom_call_target="tpu_custom_call", output_to_operand_aliasing={{}: (8, {})} | custom-call | flops 5368709120 | bytes 10485760 | tf_op jit(solution)/shard_map/pallas_call | solution.py:562
  663.2 21.1 %shard_map.272 = (f32[1024,1024]{1,0:T(8,128)}, bf16[1024,1024]{1,0:T(8,128)(2,1)}, f32[1,1024]{1,0:T(1,128)}) custom-call(s32[48]{0:T(128)} %own_ref.23, bf16[1,1024,4096]{2,1,0:T(8,128)(2,1)} %bitcast.157, bf16[4,48,256,256]{3,2,1,0:T(8,128)(2,1)} %bitcast.152, bf16[4,48,256,256]{3,2,1,0:T(8,128)(2,1)} %bitcast.153, bf16[4,48,256,256]{3,2,1,0:T(8,128)(2,1)} %bitcast.154, ...), custom_call_target="tpu_custom_call" | custom-call | flops 8589934592 | bytes 16777216 | tf_op jit(solution)/shard_map/pallas_call | solution.py:277
  690.8 14.0 %collective-permute-done = bf16[1024,256]{1,0:T(8,128)(2,1)S(1)} collective-permute-done((bf16[1024,256]{1,0:T(8,128)(2,1)S(1)}, bf16[1024,256]{1,0:T(8,128)(2,1)S(1)}, u32[]{:S(2)}, u32[]{:S(2)}) %collective-permute-start) | collective-permute-done | bytes 524320 | tf_op jit(solution)/shard_map/ppermute | solution.py:1619
  729.6 19.5 %shard_map.274.rest_0_ = bf16[4,48,256,256]{3,2,1,0:T(8,128)(2,1)} custom-call(s32[48]{0:T(128)} %own_ref.23, bf16[1024,1024]{1,0:T(8,128)(2,1)} %get-tuple-element.97.x_ref.l_ref, bf16[2,1024,2048]{2,1,0:T(8,128)(2,1)} %shard_map.267.rest_0_.rest_1_.r_ref, bf16[4,48,256,256]{3,2,1,0:T(8,128)(2,1)} %shard_map.273.rest_0_), custom_call_target="tpu_custom_call", output_to_operand_aliasing={{}: (3, {})} | custom-call | flops 8589934592 | bytes 16777216 | tf_op jit(solution)/shard_map/pallas_call | solution.py:335
  760.5 19.4 %shard_map.276 = bf16[4,48,256,256]{3,2,1,0:T(8,128)(2,1)} custom-call(s32[48]{0:T(128)} %own_ref.23, bf16[1024,1024]{1,0:T(8,128)(2,1)} %multiply_convert_fusion.1.x_ref.l_ref, bf16[1,1024,4096]{2,1,0:T(8,128)(2,1)} %bitcast.158, bf16[4,48,256,256]{3,2,1,0:T(8,128)(2,1)} %shard_map.275.rest_0_), custom_call_target="tpu_custom_call", output_to_operand_aliasing={{}: (3, {})} | custom-call | flops 8589934592 | bytes 16777216 | tf_op jit(solution)/shard_map/pallas_call | solution.py:335
  780.9 186.1 %shard_map.277 = (bf16[2,2,6,256,256]{4,3,2,1,0:T(8,128)(2,1)}, bf16[2,2,2,2,1024,256]{5,4,3,2,1,0:T(8,128)(2,1)}, f32[304,128]{1,0:T(8,128)}) custom-call(bf16[2,2,2,2,2,6,256,256]{7,6,5,4,3,2,1,0:T(8,128)(2,1)} %bitcast.156, bf16[2,1024,256]{2,1,0:T(8,128)(2,1)} %bitcast.172, f32[304,128]{1,0:T(8,128)} %pad_bitcast_fusion.v_ref), custom_call_target="tpu_custom_call" | custom-call | flops 12582912 | bytes 75497472 | tf_op jit(solution)/shard_map/pallas_call | solution.py:1345
  969.2 39.4 %shard_map.278 = f32[4098,256]{1,0:T(8,128)} custom-call(s32[32]{0:T(128)} %get-tuple-element.117.lo_ref, s32[32]{0:T(128)} %get-tuple-element.116.hi_ref, s32[32768]{0:T(1024)} %add_subtract_fusion.1.ids_ref, bf16[16384,256]{1,0:T(8,128)(2,1)} %all-gather.5.cloned.1.call-done.rest_0_, bf16[16384,256]{1,0:T(8,128)(2,1)} %bitcast.168), custom_call_target="tpu_custom_call" | custom-call | flops 1073741824 | bytes 16777216 | tf_op jit(solution)/shard_map/pallas_call | solution.py:997
  1014.4 13.7 %shard_map.279 = f32[8,128]{1,0:T(8,128)} custom-call(f32[8,128]{1,0:T(8,128)} %broadcast_in_dim.81.x_ref), custom_call_target="tpu_custom_call" | custom-call | flops 32768 | bytes 131072 | tf_op jit(solution)/shard_map/pallas_call | solution.py:1128
  1053.1 12.1 %multiply_subtract_fusion = (f32[4098,256]{1,0:T(8,128)}, f32[4098,256]{1,0:T(8,128)}, f32[4098,256]{1,0:T(8,128)}) fusion(f32[4098,256]{1,0:T(8,128)} %param.30, f32[]{:T(128)} %bitcast.53, f32[]{:T(128)} %bitcast.52, f32[]{:T(128)} %min.3, f32[4098,256]{1,0:T(8,128)} %shard_map.278, bf16[4160,256]{1,0:T(8,128)(2,1)S(1)} %copy-done.6, ...), kind=kLoop, calls=%fused_computation.14 | loop fusion | flops 18883584 | bytes 31472652 | tf_op jit(solution)/shard_map/sub | solution.py:1633
  1065.1 45.0 %reduce-scatter.8.cloned.1.call-done = bf16[6,256,256]{2,1,0:T(8,128)(2,1)} async-done(((bf16[6,1024,256]{2,1,0:T(8,128)(2,1)}), bf16[6,256,256]{2,1,0:T(8,128)(2,1)}) %reduce-scatter.8.cloned.1.call-update) | async-done | bytes 786448 | tf_op jit(solution)/shard_map/reduce_scatter | solution.py:1907
  (218 shorter events, 207.1 us)
Async XLA Ops:
  7.2 413.5 %all-gather.3.cloned.1.call-start = ((), (), s32[]{:S(2)}) async-start(), calls=%async_computation.4 | async-start | bytes 10649600 | tf_op jit(solution)/shard_map/all_gather | solution.py:1686
  116.1 149.7 %copy-start.13 = (s32[4,8,2176]{2,1,0:T(8,128)}, s32[4,8,2176]{2,1,0:T(8,128)S(1)}, u32[]{:S(2)}) copy-start(s32[4,8,2176]{2,1,0:T(8,128)S(1)} %reshape.305) | copy-start | bytes 835588
  140.4 130.6 %all-to-all-start = ((bf16[4,1024,256]{2,1,0:T(8,128)(2,1)}), bf16[4,1024,256]{2,1,0:T(8,128)(2,1)S(1)}, u32[]{:S(2)}, u32[]{:S(2)}) async-start(bf16[4,1024,256]{2,1,0:T(8,128)(2,1)} %bitcast.169), calls=%async_computation | async-start | bytes 4194304 | tf_op jit(solution)/shard_map/all_to_all | solution.py:1693
  144.7 353.1 %reduce-scatter.4.cloned.1.call-start = ((), (), s32[]{:S(2)}) async-start(), calls=%async_computation.5 | async-start | bytes 2359296 | tf_op jit(solution)/shard_map/reduce_scatter | solution.py:1783
  145.5 141.4 %copy-start.20 = (f32[1024]{0:T(1024)}, f32[1024]{0:T(1024)S(1)}, u32[]{:S(2)}) copy-start(f32[1024]{0:T(1024)S(1)} %get-tuple-element.143) | copy-start | bytes 12292
  145.9 137.2 %copy-start.9 = (bf16[1024,24]{1,0:T(8,128)(2,1)}, bf16[1024,24]{1,0:T(8,128)(2,1)S(1)}, u32[]{:S(2)}) copy-start(bf16[1024,24]{1,0:T(8,128)(2,1)S(1)} %convert_element_type.105) | copy-start | bytes 147460
  270.9 17.9 %copy-start.27 = (f32[24]{0:T(128)}, f32[24]{0:T(128)S(1)}, u32[]{:S(2)}) copy-start(f32[24]{0:T(128)S(1)} %get-tuple-element.145) | copy-start | bytes 292
  285.9 18.1 %copy-start.11 = (f32[8,3,8,128]{3,2,0,1:T(8,128)}, f32[8,3,8,128]{3,2,0,1:T(8,128)S(1)}, u32[]{:S(2)}) copy-start(f32[8,3,8,128]{3,2,0,1:T(8,128)S(1)} %copy.128) | copy-start | bytes 294916
  388.0 12.9 %copy-start.31 = (s32[1,64]{1,0:T(1,128)S(1)}, s32[1,64]{1,0:T(1,128)}, u32[]{:S(2)}) copy-start(s32[1,64]{1,0:T(1,128)} %param.20) | copy-start | bytes 772
  388.0 15.7 %copy-start.25 = (f32[8,64]{1,0:T(8,128)S(1)}, f32[8,64]{1,0:T(8,128)}, u32[]{:S(2)}) copy-start(f32[8,64]{1,0:T(8,128)} %get-tuple-element.156) | copy-start | bytes 6148
  388.0 32.6 %copy-start.22 = (pred[4160]{0:T(1024)(128)(4,1)S(1)}, pred[4160]{0:T(1024)(128)(4,1)}, u32[]{:S(2)}) copy-start(pred[4160]{0:T(1024)(128)(4,1)} %iota_compare_fusion.10) | copy-start | bytes 12484
  455.9 207.2 %reduce-scatter.6.cloned.1.call-start = ((), (), s32[]{:S(2)}) async-start(), calls=%async_computation.6 | async-start | bytes 10649600 | tf_op jit(solution)/shard_map/reduce_scatter | solution.py:1791
  497.8 283.1 %all-gather.5.cloned.1.call-start = ((), (), s32[]{:S(2)}) async-start(), calls=%async_computation.7 | async-start | bytes 9437184 | tf_op jit(solution)/shard_map/all_gather | solution.py:1862
  563.4 55.6 %copy-start.8 = (f32[1024,24]{1,0:T(8,128)S(1)}, f32[1024,24]{1,0:T(8,128)}, u32[]{:S(2)}) copy-start(f32[1024,24]{1,0:T(8,128)} %get-tuple-element.171) | copy-start | bytes 294916
  563.4 55.6 %copy-start.28 = (f32[24]{0:T(128)S(1)}, f32[24]{0:T(128)}, u32[]{:S(2)}) copy-start(f32[24]{0:T(128)} %copy-done.27) | copy-start | bytes 292
  663.2 21.1 %copy-start.34 = (s32[1024]{0:T(1024)S(1)}, s32[1024]{0:T(1024)}, u32[]{:S(2)}) copy-start(s32[1024]{0:T(1024)} %get-tuple-element.63) | copy-start | bytes 12292
  688.2 17.8 %slice-start = ((s32[4,8,2176]{2,1,0:T(8,128)}), s32[4,8,1024]{2,1,0:T(8,128)S(1)}, s32[]{:S(2)}) async-start(s32[4,8,2176]{2,1,0:T(8,128)} %copy-done.13), calls=%async_computation.9 | async-start | bytes 262144 | tf_op jit(solution)/shard_map/slice | solution.py:1695
  688.2 21.7 %copy-start = (bf16[1024,1024]{1,0:T(8,128)(2,1)S(1)}, bf16[1024,1024]{1,0:T(8,128)(2,1)}, u32[]{:S(2)}) copy-start(bf16[1024,1024]{1,0:T(8,128)(2,1)} %multiply_convert_fusion.1.x_ref.l_ref) | copy-start | bytes 6291460
  689.3 15.5 %collective-permute-start = (bf16[1024,256]{1,0:T(8,128)(2,1)S(1)}, bf16[1024,256]{1,0:T(8,128)(2,1)S(1)}, u32[]{:S(2)}, u32[]{:S(2)}) collective-permute-start(bf16[1024,256]{1,0:T(8,128)(2,1)S(1)} %get-tuple-element.134), channel_id=1, source_target_pairs={{0,8},{8,16},{16,24},{24,0},{1,9},{9,17},{17,25},{25,1},{2,10},{10... | collective-permute-start | bytes 1572872 | tf_op jit(solution)/shard_map/ppermute | solution.py:1619
  705.9 404.3 %reduce-scatter.8.cloned.1.call-start = ((), (), s32[]{:S(2)}) async-start(), calls=%async_computation.8 | async-start | bytes 3932160 | tf_op jit(solution)/shard_map/reduce_scatter | solution.py:1907
  714.3 65.6 %collective-permute-start.1 = (bf16[1024,256]{1,0:T(8,128)(2,1)}, bf16[1024,256]{1,0:T(8,128)(2,1)S(1)}, u32[]{:S(2)}, u32[]{:S(2)}) collective-permute-start(bf16[1024,256]{1,0:T(8,128)(2,1)} %get-tuple-element.132), channel_id=1, source_target_pairs={{0,24},{8,0},{16,8},{24,16},{1,25},{9,1},{17,9},{25,17},{2,26},{10... | collective-permute-start | bytes 1572872 | tf_op jit(solution)/shard_map/ppermute | solution.py:1619
  715.8 64.1 %collective-permute-start.2 = (bf16[1024,256]{1,0:T(8,128)(2,1)S(1)}, bf16[1024,256]{1,0:T(8,128)(2,1)S(1)}, u32[]{:S(2)}, u32[]{:S(2)}) collective-permute-start(bf16[1024,256]{1,0:T(8,128)(2,1)S(1)} %get-tuple-element.133), channel_id=1, source_target_pairs={{0,16},{8,24},{16,0},{24,8},{1,17},{9,25},{17,1},{25,9},{2,18},{10... | collective-permute-start | bytes 1572872 | tf_op jit(solution)/shard_map/ppermute | solution.py:1619
  969.2 39.4 %copy-start.6 = (bf16[4160,256]{1,0:T(8,128)(2,1)S(1)}, bf16[4160,256]{1,0:T(8,128)(2,1)}, u32[]{:S(2)}) copy-start(bf16[4160,256]{1,0:T(8,128)(2,1)} %reduce-scatter.6.cloned.1.call-done) | copy-start | bytes 6389764
  1008.6 20.7 %copy-start.14 = (f32[304,128]{1,0:T(8,128)S(1)}, f32[304,128]{1,0:T(8,128)}, u32[]{:S(2)}) copy-start(f32[304,128]{1,0:T(8,128)} %get-tuple-element.104) | copy-start | bytes 466948
  (23 other events, 175.5 us)
Sparse Core Ops, SparseCore 0:
  115.2 198.0 all-gather.2
  456.1 41.6 reduce-scatter.3
  500.3 146.5 reduce-scatter.5
  706.0 52.5 all-gather.4
  1051.0 59.0 reduce-scatter.7

commit v3 on v2

--- a/solution.py
+++ b/solution.py
@@ -22,10 +22,11 @@
 CHUNK = 128
 QROWS = 256
 LANES = 128
+NO_TOKEN = 1 << 30
 TABLE_PARTS = 4
 PAD_ROWS = 16 * TABLE_PARTS
 GROUP = 4
-ROW_PART = 128
+ROW_PART = 64
 
 BF16 = jnp.bfloat16
 F32 = jnp.float32
@@ -389,14 +390,6 @@
     return jnp.where(keep, values, moved)
 
 
-def attention_mask(segc_ref, segr_ref, low_row, low_col, wide):
-    doc_rows = segc_ref[low_row : low_row + QROWS, :]
-    doc_cols = segr_ref[:, low_col : low_col + wide]
-    row_pos = low_row + lax.broadcasted_iota(jnp.int32, (QROWS, wide), 0)
-    col_pos = low_col + lax.broadcasted_iota(jnp.int32, (QROWS, wide), 1)
-    return (doc_rows == doc_cols) & (row_pos >= col_pos)
-
-
 def attention_probs(query, key, allowed):
     scores = jnp.where(allowed, dot_nt(query, key), -1e30)
     row_top = jnp.max(scores, axis=-1, keepdims=True)
@@ -429,44 +422,75 @@
     return inner, jnp.where(low, high, rest).astype(BF16)
 
 
+def picked_queries(pos_ref, q_ref, cos_ref, sin_ref, rows):
+    count = rows.shape[1]
+    for i in range(count):
+        at = pl.ds(pos_ref[i], 1)
+        for k, ref in enumerate((q_ref, cos_ref, sin_ref)):
+            rows[k, i : i + 1, :] = ref[at, :]
+    cosine, sine = rows[1], rows[2]
+    turned = turn(rows[0], cosine, sine) * HEAD_DIM ** (-0.5)
+    return jnp.concatenate(head_operands(turned), axis=0), cosine, sine
+
+
+def picked_mask(pos_col_ref, seg_col_ref, segr_ref):
+    positions = lax.broadcasted_iota(jnp.int32, (1, segr_ref.shape[1]), 1)
+    allowed = (seg_col_ref[...] == segr_ref[...]) & (pos_col_ref[...] >= positions)
+    return jnp.concatenate([allowed.astype(F32)] * 2, axis=0) > 0.5
+
+
 def attn_fwd_kernel(
-    q_ref, k_ref, v_ref, segc_ref, segr_ref, cos_ref, sin_ref, mixed_ref, o_ref
+    pos_ref, q_ref, k_ref, v_ref, pos_col_ref, seg_col_ref, segr_ref, cos_ref, sin_ref, o_ref, rows
 ):
     group = pl.program_id(0) // 2
     low = lane_iota() < HEAD_DIM
-    cosine, sine = cos_ref[...], sin_ref[...]
-    length = cosine.shape[0]
-    query_h = head_operands(turn(q_ref[...], cosine, sine) * HEAD_DIM ** (-0.5))
-    key, _ = group_operands(doubled(turn(k_ref[...], cosine, sine), group))
+    count = o_ref.shape[0]
+    query, _, _ = picked_queries(pos_ref, q_ref, cos_ref, sin_ref, rows)
+    key, _ = group_operands(doubled(turn(k_ref[...], cos_ref[...], sin_ref[...]), group))
     _, value = group_operands(doubled(v_ref[...], group))
-    for block in range(length // QROWS):
-        low_row = block * QROWS
-        low_col = max(0, low_row - 2 * QROWS)
-        wide = low_row + QROWS - low_col
-        rows, cols = slice(low_row, low_row + QROWS), slice(low_col, low_col + wide)
-        allowed = attention_mask(segc_ref, segr_ref, low_row, low_col, wide)
-        outs = []
-        for h in range(2):
-            weights, total = attention_probs(query_h[h][rows], key[cols], allowed)
-            weights_high, weights_rest = split(weights)
-            mixed = dot_nn(weights_high, value[cols]) + dot_nn(weights_rest, value[cols])
-            outs.append(fold(mixed) / total)
-        o_ref[rows, :] = jnp.where(low, outs[0], outs[1]).astype(BF16)
+    allowed = picked_mask(pos_col_ref, seg_col_ref, segr_ref)
+    weights, total = attention_probs(query, key, allowed)
+    high, rest = split(weights)
+    out = fold(dot_nn(high, value) + dot_nn(rest, value)) / total
+    o_ref[...] = jnp.where(low, out[:count], out[count:]).astype(BF16)
 
 
 def attn_bwd_kernel(
-    q_ref, k_ref, v_ref, segc_ref, segr_ref, cos_ref, sin_ref, g_ref, into_ref, o_ref, dk_s, dv_s
+    pos_ref, q_ref, k_ref, v_ref, pos_col_ref, seg_col_ref, segr_ref, cos_ref, sin_ref, g_ref,
+    place_ref, into_ref, o_ref, rows, dk_s, dv_s,
 ):
     step = pl.program_id(0)
     pairs = HEADS // 2
+    low = lane_iota() < HEAD_DIM
+
+    @pl.when(step == 0)
+    def _():
+        dk_s[...] = jnp.zeros_like(dk_s)
+        dv_s[...] = jnp.zeros_like(dv_s)
 
     @pl.when(step < pairs)
     def _():
-        attn_bwd_pair(
-            q_ref, k_ref, v_ref, segc_ref, segr_ref, cos_ref, sin_ref, g_ref, o_ref, dk_s, dv_s
+        group = step // 2
+        count = g_ref.shape[0]
+        query, cosine, sine = picked_queries(pos_ref, q_ref, cos_ref, sin_ref, rows)
+        grad = jnp.concatenate(head_operands(g_ref[...]), axis=0)
+        key, key_out = group_operands(doubled(turn(k_ref[...], cos_ref[...], sin_ref[...]), group))
+        value, _ = group_operands(doubled(v_ref[...], group))
+        allowed = picked_mask(pos_col_ref, seg_col_ref, segr_ref)
+        weights, total = attention_probs(query, key, allowed)
+        probs = weights * (1.0 / total)
+        dprobs = dot_nt(grad, value)
+        delta = jnp.sum(probs * dprobs, axis=-1, keepdims=True)
+        dscores = jnp.concatenate(split(probs * (dprobs - delta)), axis=0)
+        dq = fold(dot_nn(dscores[: 2 * count], key_out) + dot_nn(dscores[2 * count :], key_out))
+        dq = jnp.where(low, dq[:count], dq[count:]) * HEAD_DIM ** (-0.5)
+        dq_low = turn_back(dq, cosine, sine).astype(BF16)
+        o_ref[...] = dot_nn(place_ref[...], dq_low).astype(BF16)
+        inner_q, inner_g = query[:, :LANES], grad[:, :LANES]
+        dv_s[group] += dot_tn(
+            jnp.concatenate(split(probs), axis=0), jnp.concatenate([inner_g, inner_g], axis=0)
         )
-
-    low = lane_iota() < HEAD_DIM
+        dk_s[group] += dot_tn(dscores, jnp.concatenate([inner_q, inner_q], axis=0))
 
     @pl.when(step == pairs)
     def _():
@@ -478,104 +502,69 @@
         o_ref[...] = jnp.where(low, fold(dv_s[0]), fold(dv_s[1])).astype(BF16)
 
 
-def attn_bwd_pair(
-    q_ref, k_ref, v_ref, segc_ref, segr_ref, cos_ref, sin_ref, g_ref, dq_ref, dk_s, dv_s
-):
-    step = pl.program_id(0)
-    group = step // 2
-    low = lane_iota() < HEAD_DIM
-    cosine, sine = cos_ref[...], sin_ref[...]
-    length = cosine.shape[0]
-
-    @pl.when(step == 0)
-    def _():
-        dk_s[...] = jnp.zeros_like(dk_s)
-        dv_s[...] = jnp.zeros_like(dv_s)
-
-    scale = HEAD_DIM ** (-0.5)
-    query_h = head_operands(turn(q_ref[...], cosine, sine) * scale)
-    grad_h = head_operands(g_ref[...])
-    key, key_out = group_operands(doubled(turn(k_ref[...], cosine, sine), group))
-    value, _ = group_operands(doubled(v_ref[...], group))
-    for block in range(length // QROWS):
-        low_row = block * QROWS
-        low_col = max(0, low_row - 2 * QROWS)
-        wide = low_row + QROWS - low_col
-        rows, cols = slice(low_row, low_row + QROWS), slice(low_col, low_col + wide)
-        allowed = attention_mask(segc_ref, segr_ref, low_row, low_col, wide)
-        dqs, ps, dss = [], [], []
-        for h in range(2):
-            weights, total = attention_probs(query_h[h][rows], key[cols], allowed)
-            probs = weights * (1.0 / total)
-            dprobs = dot_nt(grad_h[h][rows], value[cols])
-            delta = jnp.sum(probs * dprobs, axis=-1, keepdims=True)
-            dscores = split(probs * (dprobs - delta))
-            dqs.append(fold(dot_nn(dscores[0], key_out[cols]) + dot_nn(dscores[1], key_out[cols])))
-            ps.append(probs.astype(BF16))
-            dss.append(dscores[0])
-        both_p = jnp.concatenate(ps, axis=0)
-        both_d = jnp.concatenate(dss, axis=0)
-        both_g = jnp.concatenate([grad_h[h][rows, :LANES] for h in range(2)], axis=0)
-        both_q = jnp.concatenate([query_h[h][rows, :LANES] for h in range(2)], axis=0)
-        dv_s[group, cols, :] += dot_tn(both_p, both_g)
-        dk_s[group, cols, :] += dot_tn(both_d, both_q)
-        dq = jnp.where(low, dqs[0], dqs[1]) * scale
-        dq_ref[rows, :] = turn_back(dq, cosine[rows], sine[rows]).astype(BF16)
-
-
-def attention_specs(length, base):
+def attention_specs(length, count, base):
+    fixed = lambda *shape: pl.BlockSpec(shape, lambda p, pos: (0, 0))
     return [
-        pl.BlockSpec((length, LANES), lambda p: (0, base + jnp.minimum(p, 3))),
-        pl.BlockSpec((length, LANES), lambda p: (0, base + 4)),
-        pl.BlockSpec((length, LANES), lambda p: (0, base + 5)),
-        pl.BlockSpec((length, 1), lambda p: (0, 0)),
-        pl.BlockSpec((1, length), lambda p: (0, 0)),
-        pl.BlockSpec((length, LANES), lambda p: (0, 0)),
-        pl.BlockSpec((length, LANES), lambda p: (0, 0)),
+        pl.BlockSpec((length, LANES), lambda p, pos: (0, base + jnp.minimum(p, 3))),
+        pl.BlockSpec((length, LANES), lambda p, pos: (0, base + 4)),
+        pl.BlockSpec((length, LANES), lambda p, pos: (0, base + 5)),
+        fixed(count, 1),
+        fixed(count, 1),
+        fixed(1, length),
+        fixed(length, LANES),
+        fixed(length, LANES),
     ]
 
 
-def attention_forward(both_proj, segc, segr, cosine, sine, mixed):
-    length = both_proj.shape[0]
+def attention_forward(both_proj, positions, pos_col, seg_col, segr, cosine, sine):
+    length, count = both_proj.shape[0], positions.shape[0]
     base = (SSM_INNER + XBC_WIDTH) // LANES
-    pairs = HEADS // 2
-    at = SSM_INNER // LANES
     return pl.pallas_call(
         attn_fwd_kernel,
-        grid=(pairs,),
-        in_specs=attention_specs(length, base) + [pl.BlockSpec(memory_space=pl.ANY)],
-        out_specs=pl.BlockSpec((length, LANES), lambda p: (0, at + p)),
-        out_shape=jax.ShapeDtypeStruct(mixed.shape, BF16),
-        input_output_aliases={7: 0},
+        grid_spec=pltpu.PrefetchScalarGridSpec(
+            num_scalar_prefetch=1,
+            grid=(HEADS // 2,),
+            in_specs=attention_specs(length, count, base),
+            out_specs=pl.BlockSpec((count, LANES), lambda p, pos: (0, p)),
+            scratch_shapes=[pltpu.VMEM((3, count, LANES), F32)],
+        ),
+        out_shape=jax.ShapeDtypeStruct((count, HEADS * HEAD_DIM), BF16),
         compiler_params=params(),
         cost_estimate=cost(
-            4 * HEADS * length * length * HEAD_DIM, 6 * length * D, HEADS * length * length // 2
+            4 * HEADS * count * length * HEAD_DIM, 6 * length * D, HEADS * length * count
         ),
-    )(both_proj, both_proj, both_proj, segc, segr, cosine, sine, mixed)
-
-
-def attention_backward(both_proj, segc, segr, cosine, sine, grads, into):
-    length = both_proj.shape[0]
+    )(positions, both_proj, both_proj, both_proj, pos_col, seg_col, segr, cosine, sine)
+
+
+def attention_backward(
+    both_proj, positions, pos_col, seg_col, segr, cosine, sine, grads, place, into
+):
+    length, count = both_proj.shape[0], positions.shape[0]
     base = (SSM_INNER + XBC_WIDTH) // LANES
     at = SSM_INNER // LANES
     pairs = HEADS // 2
     return pl.pallas_call(
         attn_bwd_kernel,
-        grid=(pairs + 2,),
-        in_specs=attention_specs(length, base)
-        + [
-            pl.BlockSpec((length, LANES), lambda p: (0, at + jnp.minimum(p, 3))),
-            pl.BlockSpec(memory_space=pl.ANY),
-        ],
-        out_specs=pl.BlockSpec((length, LANES), lambda p: (0, base + p)),
+        grid_spec=pltpu.PrefetchScalarGridSpec(
+            num_scalar_prefetch=1,
+            grid=(pairs + 2,),
+            in_specs=attention_specs(length, count, base)
+            + [
+                pl.BlockSpec((count, LANES), lambda p, pos: (0, at + jnp.minimum(p, 3))),
+                pl.BlockSpec((length, count), lambda p, pos: (0, 0)),
+                pl.BlockSpec(memory_space=pl.ANY),
+            ],
+            out_specs=pl.BlockSpec((length, LANES), lambda p, pos: (0, base + p)),
+            scratch_shapes=[pltpu.VMEM((3, count, LANES), F32)]
+            + [pltpu.VMEM((2, length, LANES), F32)] * 2,
+        ),
         out_shape=jax.ShapeDtypeStruct(into.shape, BF16),
-        input_output_aliases={8: 0},
-        scratch_shapes=[pltpu.VMEM((2, length, LANES), F32)] * 2,
+        input_output_aliases={11: 0},
         compiler_params=params(),
         cost_estimate=cost(
-            10 * HEADS * length * length * HEAD_DIM, 10 * length * D, HEADS * length * length // 2
+            10 * HEADS * count * length * HEAD_DIM, 10 * length * D, HEADS * length * count
         ),
-    )(both_proj, both_proj, both_proj, segc, segr, cosine, sine, grads, into)
+    )(positions, both_proj, both_proj, both_proj, pos_col, seg_col, segr, cosine, sine, grads, place, into)
 
 
 def chunk_masks(segc_ref, segr_ref, last_ref, chunk):
@@ -846,7 +835,7 @@
                 pl.BlockSpec((1, STATE, SSM_INNER), lambda c, last: (c, 0, 0)),
                 spec["rows"](XBC_WIDTH),
                 spec["rows"](XBC_WIDTH),
-                spec["rows"](SSM_INNER + HEADS * HEAD_DIM),
+                spec["rows"](SSM_INNER),
             ],
             scratch_shapes=[
                 pltpu.VMEM((STATE, SSM_INNER), F32),
@@ -858,7 +847,7 @@
             jax.ShapeDtypeStruct((chunks, STATE, SSM_INNER), F32),
             jax.ShapeDtypeStruct((length, XBC_WIDTH), F32),
             jax.ShapeDtypeStruct((length, XBC_WIDTH), F32),
-            jax.ShapeDtypeStruct((length, SSM_INNER + HEADS * HEAD_DIM), BF16),
+            jax.ShapeDtypeStruct((length, SSM_INNER), BF16),
         ],
         compiler_params=params(),
         cost_estimate=cost(
@@ -1602,6 +1591,68 @@
     )(values)
 
 
+def scatter_columns_kernel(rows, cols, x_ref, o_ref, *rest):
+    bits = [b for b in ring_bits(rows, cols) if b[0] == 1]
+    stages = len(bits)
+    boxes, (send_sem, recv_sem) = rest[:stages], rest[stages:]
+    place = (lax.axis_index("row"), lax.axis_index("col"))
+    side, partner = doubling(place, bits)
+    orders = [o[:stages] for o in scatter_orders(rows, cols)]
+    greet(bits, partner)
+
+    def held(stage, h, side_of):
+        left = [b for b in bits if b not in orders[h][:stage]]
+        at = tuple(side_of if b == orders[h][stage] else slice(None) for b in left)
+        return x_ref.at[at + (h,)] if stage == 0 else boxes[stage - 1].at[(h,) + at]
+
+    def send(stage, h):
+        which = orders[h][stage]
+        return pltpu.make_async_remote_copy(
+            src_ref=held(stage, h, 1 - side(which)),
+            dst_ref=boxes[stage].at[h],
+            send_sem=send_sem.at[stage, h],
+            recv_sem=recv_sem.at[stage, h],
+            device_id=partner(which),
+            device_id_type=MESH,
+        )
+
+    sent = []
+    for stage in range(stages + 1):
+        for h in range(2):
+            if stage > 0:
+                sent[2 * (stage - 1) + h].wait_recv()
+                total = held(stage - 1, h, side(orders[h][stage - 1]))[...] + boxes[stage - 1][h]
+                if stage == stages:
+                    o_ref[h] = total
+                else:
+                    boxes[stage - 1][h] = total
+            if stage < stages:
+                sent.append(send(stage, h))
+                sent[-1].start()
+    for copy in sent:
+        copy.wait_send()
+
+
+def scatter_columns(values, rows, cols, collective_id):
+    count, width = values.shape[0] // cols, values.shape[1]
+    stages = (cols - 1).bit_length()
+    dma = pltpu.SemaphoreType.DMA
+    out = pl.pallas_call(
+        functools.partial(scatter_columns_kernel, rows, cols),
+        in_specs=[pl.BlockSpec(memory_space=pltpu.VMEM)],
+        out_specs=pl.BlockSpec(memory_space=pltpu.VMEM),
+        out_shape=jax.ShapeDtypeStruct((2, count // 2, width), F32),
+        scratch_shapes=[
+            pltpu.VMEM((2,) + (2,) * (stages - s - 1) + (count // 2, width), F32)
+            for s in range(stages)
+        ]
+        + [dma((stages, 2)), dma((stages, 2))],
+        compiler_params=params(collective_id=collective_id, has_side_effects=True),
+        cost_estimate=cost(values.size, values.size * 8),
+    )(values.reshape((2,) * stages + (2, count // 2, width)))
+    return out.reshape(count, width)
+
+
 def piece_order(rows):
     order = [0] + [k for pair in range(1, rows // 2 + 1) for k in (pair, rows - pair)][: rows - 1]
     return order[: rows // 2], order[rows // 2 :]
@@ -1677,8 +1728,11 @@
     table_low = table.astype(BF16)
     shard_padded = -(-shard_rows // PAD_ROWS) * PAD_ROWS
     padded = jnp.pad(table_low, ((0, shard_padded - shard_rows), (0, 0)))
-    order = jnp.argsort(tokens)
-    sent = jnp.concatenate([tokens, jnp.sort(tokens), loss_targets[0], loss_valid[0]])
+    in_order = jnp.sort(tokens)
+    repeats = jnp.pad(in_order[1:] == in_order[:-1], (1, 0))
+    different = jnp.sort(jnp.where(repeats, NO_TOKEN, in_order))
+    token_place = jnp.sum((different[:, None] < tokens[None, :]).astype(jnp.int32), axis=0)
+    sent = jnp.concatenate([tokens, different, loss_targets[0], loss_valid[0]])
     ints, table_cols, weight_rows = front_exchange(
         sent, padded, block_weights.astype(BF16), rows, cols, 2
     )
@@ -1741,19 +1795,25 @@
     scan_out, states, act_xbc, slope, mixed = ssm_forward(
         last_docs, both_proj, near, conv_rows, conv_bias[None, :], gain_row, *times
     )
-    branch_in = attention_forward(both_proj, segc, segr, cosine, sine, mixed)
+    positions = loss_positions[0]
+    pos_col = positions[:, None]
+    hits = pos_col == jnp.arange(length, dtype=jnp.int32)[None, :]
+    chosen, place = hits.astype(BF16), hits.T.astype(BF16)
+    seg_col = jnp.sum(jnp.where(hits, segr, 0), axis=1, keepdims=True)
+    choose = lambda values: jnp.dot(chosen, values, preferred_element_type=F32).astype(BF16)
+    spread_rows = lambda values: jnp.dot(hits.T.astype(F32), values, precision=highest)
+    picked_in = (positions, pos_col, seg_col, segr, cosine, sine)
+    context = attention_forward(both_proj, *picked_in)
+    branch_in = jnp.concatenate([choose(mixed), context], axis=1)
     hidden_one, normed_two = back_then_norm(
-        branch_in, gathered, block_owner, branch_at, branch_blocks, embedded, gain_rows[1]
+        branch_in, gathered, block_owner, branch_at, branch_blocks, choose(embedded), gain_rows[1]
     )
     gate_val, up_val, act_low = project_gate_up(
         normed_two, gathered, block_owner, gate_at, down_blocks
     )
-    hidden_two, final_out = back_then_norm(
+    hidden_two, picked_rows = back_then_norm(
         act_low, gathered, block_owner, down_at, down_blocks, hidden_one, gain_rows[2]
     )
-    positions = loss_positions[0]
-    chosen = (positions[:, None] == jnp.arange(length, dtype=jnp.int32)[None, :]).astype(BF16)
-    picked_rows = jnp.dot(chosen, final_out, preferred_element_type=F32).astype(BF16)
     rows_all = gather_columns(picked_rows, cols, 4).reshape(-1, D)
 
     logits = jnp.einsum("rd,vd->rv", rows_all, table_rows, preferred_element_type=F32)
@@ -1780,16 +1840,16 @@
         (jnp.exp(logits - log_total[:, None]) - onehot.astype(F32))
         * (valid_wide / valid_count)[:, None]
     ).astype(BF16)
-    rows_grad = lax.psum_scatter(
-        jnp.einsum("rv,vd->rd", logit_grad, table_rows, preferred_element_type=F32),
-        "col",
-        scatter_dimension=0,
-        tiled=True,
-    )
+    rows_part = jnp.einsum("rv,vd->rd", logit_grad, table_rows, preferred_element_type=F32)
     table_loss_grad = jnp.einsum("rv,rd->vd", logit_grad, rows_all, preferred_element_type=F32)
-    table_loss_low, rows_grad = lax.optimization_barrier((table_loss_grad.astype(BF16), rows_grad))
+    table_loss_low, rows_part = lax.optimization_barrier((table_loss_grad.astype(BF16), rows_part))
+    rows_grad = scatter_columns(rows_part, rows, cols, 6)
     table_loss_mine = lax.psum_scatter(table_loss_low, "row", scatter_dimension=1, tiled=True)
-    final_grad = jnp.zeros((length, D), F32).at[positions].add(rows_grad)
+    equal = pos_col == positions[None, :]
+    numbers = jnp.arange(count_rows, dtype=jnp.int32)
+    again = jnp.any(equal & (numbers[None, :] < numbers[:, None]), axis=1)
+    adds = jnp.where(again[:, None], 0.0, equal.astype(F32))
+    final_grad = jnp.dot(adds, rows_grad, precision=highest)
     _, final_norm_back = jax.vjp(rms_gain, hidden_two, gain_rows[2])
     hidden_two_grad, gain_final_grad = final_norm_back(final_grad)
     down_in = hidden_two_grad.astype(BF16)
@@ -1803,7 +1863,7 @@
         block_owner,
         gate_at,
         gate_blocks,
-        jnp.zeros((length, D), F32),
+        jnp.zeros((count_rows, D), F32),
         hidden_one,
         gain_rows[1],
         hidden_two_grad,
@@ -1821,10 +1881,10 @@
         *times,
         states,
         scan_out,
-        branch_out_grad,
+        spread_rows(branch_out_grad[:, :SSM_INNER]),
     )
     in_grad_low = attention_backward(
-        both_proj, segc, segr, cosine, sine, branch_out_grad, in_grad_low
+        both_proj, *picked_in, branch_out_grad, place, in_grad_low
     )
     sum_y, sum_x, sum_k = (
         sums[:, i * LANES : i * LANES + SSM_HEADS] for i in range(3)
@@ -1836,7 +1896,6 @@
     time_grad, time_bias_grad, decay_log_grad = steps_back(
         (sum_x, decays_grad.reshape(length, SSM_HEADS))
     )
-    in_grad_low, table_loss_mine = lax.optimization_barrier((in_grad_low, table_loss_mine))
     time_grad_low = time_grad.astype(BF16)
     grad_time = jnp.einsum("td,th->dh", normed, time_grad_low, preferred_element_type=F32)
     time_part = jnp.einsum("th,dh->td", time_grad_low, time_low, preferred_element_type=F32)
@@ -1849,12 +1908,14 @@
         time_part,
         embedded,
         gain_rows[0],
-        hidden_one_grad,
-    )
-    placed = (order[:, None] == jnp.arange(length, dtype=jnp.int32)[None, :]).astype(BF16)
+        spread_rows(hidden_one_grad),
+    )
+    placed = (jnp.arange(length, dtype=jnp.int32)[:, None] == token_place[None, :]).astype(BF16)
     embed_sorted = jnp.dot(placed, embed_grad, preferred_element_type=F32).astype(BF16)
-    embed_sorted, down_in, normed_two, branch_grad_low, normed = lax.optimization_barrier(
-        (embed_sorted, down_in, normed_two, branch_grad_low, normed)
+    embed_sorted, table_loss_mine, down_in, normed_two, branch_grad_low, normed = (
+        lax.optimization_barrier(
+            (embed_sorted, table_loss_mine, down_in, normed_two, branch_grad_low, normed)
+        )
     )
     early, late = exchange_rows(embed_sorted, rows)
     grad_slots = weight_grad(down_in, act_low[None], block_owner, down_at, like, None)

time: 1140 us -> 1000 us (0.88)
  Pallas kernels: 827 us -> 723 us
  waiting for transfers between devices: 90.3 us -> 58.9 us
  matrix products: 45 us -> 58.8 us
    pallas_call x6, Pallas kernels: 80.7 us -> 40.9 us  [slot_call(): pl.pallas_call(kernel, grid_spec=pltpu.PrefetchScalarGridSpec(num_scalar_...]
    reduce_scatter x1 -> x0, waiting for transfers between devices: 31.2 us -> none  [body(): lax.psum_scatter(jnp.einsum('rv,vd->rd', logit_grad, table_rows, preferre...]
    pallas_call x2 -> x3, Pallas kernels: 63.6 us -> 41 us  [the longest x1 19 us: scatter_columns(): pl.pallas_call(functools.partial(scatter_columns_kernel, rows, cols), in_...]
    pallas_call x4, Pallas kernels: 61.9 us -> 45.4 us  [weight_grad(): pl.pallas_call(wgrad_kernel, grid_spec=pltpu.PrefetchScalarGridSpec(num_s...]
    pallas_call x2, Pallas kernels: 42.6 us -> 28.8 us  [back_through_norm(): pl.pallas_call(functools.partial(back_grad_kernel, parts), grid_spec=pltp...]
    dot_general x1 -> x5, matrix products: 2.77 us -> 15.4 us  [the longest x2 9.66 us: body(): jnp.dot(hits.T.astype(F32), values, precision=highest)]
  transfers between devices with their start and end apart: 9 -> 8, of which waited for: 3 -> 2; matrix products, arithmetic and copies ran while one was open for 11% -> 11% of each run, Pallas kernels for 39% -> 37%
where the time goes in v3:
time: 1000 us; the launch traced here: 993 us
  Pallas kernels  723 us (72%)
  other arithmetic  71.1 us (7%)
  waiting for transfers between devices  58.9 us (6%)
  matrix products  58.8 us (6%)
  local copies, waits for them, and re-layouts  50.2 us (5%)
  between operations  21.9 us (2%)
    pallas_call x1, Pallas kernels, tail_exchange(): pl.pallas_call(functools.partial(tail_kernel, rows, cols, slots), in_spec...  187 us
    pallas_call x1, Pallas kernels, gather_weights(): pl.pallas_call(functools.partial(weights_kernel, rows, cols), in_specs=[p...  113 us
    pallas_call x1, Pallas kernels, front_exchange(): pl.pallas_call(functools.partial(front_kernel, rows, cols), in_specs=[pl....  97.7 us
    pallas_call x1, Pallas kernels, ssm_backward(): pl.pallas_call(ssm_bwd_kernel, grid_spec=pltpu.PrefetchScalarGridSpec(num...  51.5 us
    pallas_call x4, Pallas kernels, weight_grad(): pl.pallas_call(wgrad_kernel, grid_spec=pltpu.PrefetchScalarGridSpec(num_s...  45.4 us
    reduce_scatter x1, waiting for transfers between devices, body(): lax.psum_scatter(partial_update, 'row', scatter_dimension=1, tiled=True)  45 us
    pallas_call x6, Pallas kernels, slot_call(): pl.pallas_call(kernel, grid_spec=pltpu.PrefetchScalarGridSpec(num_scalar_...  40.9 us
    pallas_call x1, Pallas kernels, ssm_forward(): pl.pallas_call(ssm_fwd_kernel, grid_spec=pltpu.PrefetchScalarGridSpec(num...  32.1 us
  transfers between devices with their start and end apart: 8, of which 2 were waited for; matrix products, arithmetic and copies ran while one was open for 11% of the time, Pallas kernels for 37%

profile of v3, /device:TPU:0, one launch (start us, length us, event | category | flops | bytes accessed | tf_op | source)
XLA Modules:
  0.0 992.9 jit_solution(493294096895725082)
XLA Ops:
  23.8 97.7 %shard_map.257 = (s32[2,2,2,2,2,17,128]{6,5,4,3,2,1,0:T(8,128)}, bf16[2,2,2,4,1040,256]{5,4,3,2,1,0:T(8,128)(2,1)}, bf16[2,2,6,256,256]{4,3,2,1,0:T(8,128)(2,1)}) custom-call(s32[17,128]{1,0:T(8,128)} %bitcast.211, bf16[4,1040,256]{2,1,0:T(8,128)(2,1)} %bitcast.166, bf16[6,256,256]{2,1,0:T(8,128)(2,1)} %convert_element_type.114.w_ref), custom_call_target="tpu_custom_call" | custom-call | flops 1048576 | bytes 34078720 | tf_op jit(solution)/shard_map/pallas_call | solution.py:1475
  122.8 24.0 %gather_fusion = bf16[4096,256]{1,0:T(8,128)(2,1)} fusion(bf16[33280,256]{1,0:T(8,128)(2,1)} %bitcast.168, s32[4096]{0:T(1024)S(1)} %broadcast_clamp_fusion), kind=kCustom, calls=%fused_computation | custom fusion | bytes 4210688 | tf_op jit(solution)/shard_map/jit(_take)/gather | solution.py:1743
  161.6 113.2 %shard_map.258 = bf16[4,2,2,2,6,256,256]{6,5,4,3,2,1,0:T(8,128)(2,1)} custom-call(bf16[4,6,256,256]{3,2,1,0:T(8,128)(2,1)} %bitcast.176), custom_call_target="tpu_custom_call" | custom-call | flops 1048576 | bytes 50331648 | tf_op jit(solution)/shard_map/pallas_call | solution.py:1552
  292.3 15.1 %shard_map.259.proj_ref.q_ref.k_ref.v_ref = f32[1024,4096]{1,0:T(8,128)} custom-call(s32[48]{0:T(128)} %own_ref.23, bf16[1024,1024]{1,0:T(8,128)(2,1)} %multiply_convert_fusion.1.x_ref.l_ref, bf16[4,48,256,256]{3,2,1,0:T(8,128)(2,1)} %bitcast.130, bf16[4,48,256,256]{3,2,1,0:T(8,128)(2,1)} %bitcast.131, bf16[4,48,256,256]{3,2,1,0:T(8,128)(2,1)} %bitcast.132, ...), custom_call_target="tpu_custom_call" | custom-call | flops 8589934592 | bytes 18874368 | tf_op jit(solution)/shard_map/pallas_call | solution.py:109
  307.4 8.6 shard_map.261
  316.0 32.1 %shard_map.260 = (f32[1024,1536]{1,0:T(8,128)}, f32[8,128,1536]{2,1,0:T(8,128)}, f32[1024,1792]{1,0:T(8,128)}, f32[1024,1792]{1,0:T(8,128)}, bf16[1024,1536]{1,0:T(8,128)(2,1)}) custom-call(s32[8]{0:T(128)} %bitcast.221, f32[1024,4096]{1,0:T(8,128)} %shard_map.259.proj_ref.q_ref.k_ref.v_ref, f32[1024,8]{1,0:T(8,128)} %convert_element_type.119.near_ref, ...), custom_call_target="tpu_custom_call" | custom-call | flops 1610612736 | bytes 62914560 | tf_op jit(solution)/shard_map/pallas_call | solution.py:815
  369.0 16.7 %shard_map.265 = bf16[8,64,1024]{2,1,0:T(8,128)(2,1)} custom-call(bf16[64,1024]{1,0:T(8,128)(2,1)} %get-tuple-element.74.x_ref), custom_call_target="tpu_custom_call" | custom-call | flops 1024 | bytes 2097152 | tf_op jit(solution)/shard_map/pallas_call | solution.py:1583
  385.8 8.1 fusion.74
  408.3 10.7 %convolution_convert_fusion = bf16[4160,1024]{1,0:T(8,128)(2,1)} fusion(bf16[512,1024]{1,0:T(8,128)(2,1)S(1)} %bitcast.184, f32[512,4160]{0,1:T(8,128)} %copy-done.2, f32[512]{0:T(512)S(1)} %get-tuple-element.166, f32[512]{0:T(512)S(1)} %get-tuple-element.124, s32[512]{0:T(512)S(1)} %copy-done.30, pred[4160]{0:T(1024)(128)(4,1)S(1)} %iota_compare_fusion.15), kind=kOutput, calls=%fused_computation.1 | convolution fusion | flops 4381245440 | bytes 18098240 | tf_op jit(solution)/shard_map/rv,rd->vd/dot_general | solution.py:1844
  418.9 12.1 %fusion.67 = f32[512,1024]{1,0:T(8,128)} fusion(bf16[4160,1024]{1,0:T(8,128)(2,1)} %all-gather.3.cloned.1.call-done, f32[512,4160]{0,1:T(8,128)} %copy-done.2, f32[512]{0:T(512)S(1)} %get-tuple-element.166, f32[512]{0:T(512)S(1)} %get-tuple-element.124, s32[512]{0:T(512)S(1)} %copy-done.30, pred[4160]{0:T(1024)(128)(4,1)S(1)} %iota_compare_fusion.15), kind=kOutput, calls=%fused_computation.172 | convolution fusion | flops 4376985600 | bytes 19146816 | tf_op jit(solution)/shard_map/rv,vd->rd/dot_general | solution.py:1843
  433.3 19.0 %shard_map.267 = f32[2,32,1024]{2,1,0:T(8,128)} custom-call(f32[2,2,2,2,32,1024]{5,4,3,2,1,0:T(8,128)} %bitcast.177), custom_call_target="tpu_custom_call" | custom-call | flops 524288 | bytes 4194304 | tf_op jit(solution)/shard_map/pallas_call | solution.py:1640
  478.8 51.5 %shard_map.271 = (bf16[1024,4096]{1,0:T(8,128)(2,1)}, f32[1024,384]{1,0:T(8,128)}, f32[8,8,128]{2,1,0:T(8,128)}, f32[8,1792]{1,0:T(8,128)}) custom-call(s32[8]{0:T(128)} %bitcast.222, f32[1024,4096]{1,0:T(8,128)} %shard_map.259.proj_ref.q_ref.k_ref.v_ref, f32[1024,8]{1,0:T(8,128)} %convert_element_type.119.near_ref, f32[4,1792]{1,0:T(4,128)} %reshape.288.cw_ref, ...), custom_call_target="tpu_custom_call" | custom-call | flops 4831838208 | bytes 94371840 | tf_op jit(solution)/shard_map/pallas_call | solution.py:867
  533.6 13.4 %shard_map.272 = bf16[1024,4096]{1,0:T(8,128)(2,1)} custom-call(s32[64]{0:T(128)} %bitcast.197, f32[1024,4096]{1,0:T(8,128)} %shard_map.259.proj_ref.q_ref.k_ref.v_ref, f32[1024,4096]{1,0:T(8,128)} %shard_map.259.proj_ref.q_ref.k_ref.v_ref, f32[1024,4096]{1,0:T(8,128)} %shard_map.259.proj_ref.q_ref.k_ref.v_ref, ...), custom_call_target="tpu_custom_call", output_to_operand_aliasing={{}: (11, {})} | custom-call | flops 335544320 | bytes 10485760 | tf_op jit(solution)/shard_map/pallas_call | solution.py:546
  555.9 21.1 %shard_map.273 = (f32[1024,1024]{1,0:T(8,128)}, bf16[1024,1024]{1,0:T(8,128)(2,1)}, f32[1,1024]{1,0:T(1,128)}) custom-call(s32[48]{0:T(128)} %own_ref.23, bf16[1,1024,4096]{2,1,0:T(8,128)(2,1)} %bitcast.161, bf16[4,48,256,256]{3,2,1,0:T(8,128)(2,1)} %bitcast.156, bf16[4,48,256,256]{3,2,1,0:T(8,128)(2,1)} %bitcast.157, bf16[4,48,256,256]{3,2,1,0:T(8,128)(2,1)} %bitcast.158, ...), custom_call_target="tpu_custom_call" | custom-call | flops 8589934592 | bytes 16777216 | tf_op jit(solution)/shard_map/pallas_call | solution.py:278
  586.9 13.8 %collective-permute-done = bf16[1024,256]{1,0:T(8,128)(2,1)S(1)} collective-permute-done((bf16[1024,256]{1,0:T(8,128)(2,1)S(1)}, bf16[1024,256]{1,0:T(8,128)(2,1)S(1)}, u32[]{:S(2)}, u32[]{:S(2)}) %collective-permute-start) | collective-permute-done | bytes 524320 | tf_op jit(solution)/shard_map/ppermute | solution.py:1670
  621.0 12.0 %shard_map.275.rest_0_ = bf16[4,48,256,256]{3,2,1,0:T(8,128)(2,1)} custom-call(s32[48]{0:T(128)} %own_ref.23, bf16[64,1024]{1,0:T(8,128)(2,1)} %get-tuple-element.94.x_ref.l_ref, bf16[2,64,2048]{2,1,0:T(8,128)(2,1)} %shard_map.268.rest_0_.rest_1_.r_ref, bf16[4,48,256,256]{3,2,1,0:T(8,128)(2,1)} %shard_map.274.rest_0_), custom_call_target="tpu_custom_call", output_to_operand_aliasing={{}: (3, {})} | custom-call | flops 536870912 | bytes 8912896 | tf_op jit(solution)/shard_map/pallas_call | solution.py:336
  640.0 19.4 %shard_map.277 = bf16[4,48,256,256]{3,2,1,0:T(8,128)(2,1)} custom-call(s32[48]{0:T(128)} %own_ref.23, bf16[1024,1024]{1,0:T(8,128)(2,1)} %multiply_convert_fusion.1.x_ref.l_ref, bf16[1,1024,4096]{2,1,0:T(8,128)(2,1)} %bitcast.162, bf16[4,48,256,256]{3,2,1,0:T(8,128)(2,1)} %shard_map.276.rest_0_), custom_call_target="tpu_custom_call", output_to_operand_aliasing={{}: (3, {})} | custom-call | flops 8589934592 | bytes 16777216 | tf_op jit(solution)/shard_map/pallas_call | solution.py:336
  660.4 187.2 %shard_map.278 = (bf16[2,2,6,256,256]{4,3,2,1,0:T(8,128)(2,1)}, bf16[2,2,2,2,1024,256]{5,4,3,2,1,0:T(8,128)(2,1)}, f32[304,128]{1,0:T(8,128)}) custom-call(bf16[2,2,2,2,2,6,256,256]{7,6,5,4,3,2,1,0:T(8,128)(2,1)} %bitcast.160, bf16[2,1024,256]{2,1,0:T(8,128)(2,1)} %bitcast.174, f32[304,128]{1,0:T(8,128)} %pad_bitcast_fusion.v_ref), custom_call_target="tpu_custom_call" | custom-call | flops 12582912 | bytes 75497472 | tf_op jit(solution)/shard_map/pallas_call | solution.py:1334
  851.3 30.7 %shard_map.279 = f32[4098,256]{1,0:T(8,128)} custom-call(s32[32]{0:T(128)} %get-tuple-element.114.lo_ref, s32[32]{0:T(128)} %get-tuple-element.113.hi_ref, s32[32768]{0:T(1024)} %add_subtract_fusion.1.ids_ref, bf16[16384,256]{1,0:T(8,128)(2,1)} %all-gather.5.cloned.1.call-done.rest_0_, bf16[16384,256]{1,0:T(8,128)(2,1)} %bitcast.170), custom_call_target="tpu_custom_call" | custom-call | flops 1073741824 | bytes 16777216 | tf_op jit(solution)/shard_map/pallas_call | solution.py:986
  887.8 11.3 %shard_map.280 = f32[8,128]{1,0:T(8,128)} custom-call(f32[8,128]{1,0:T(8,128)} %broadcast_in_dim.128.x_ref), custom_call_target="tpu_custom_call" | custom-call | flops 32768 | bytes 131072 | tf_op jit(solution)/shard_map/pallas_call | solution.py:1117
  901.6 8.7 shard_map.281.rot_ref
  910.9 10.4 %shard_map.282 = (f32[6,256,256]{2,1,0:T(8,128)}, f32[6,256,256]{2,1,0:T(8,128)}, bf16[6,1024,256]{2,1,0:T(8,128)(2,1)}) custom-call(f32[3]{0:T(128)} %pad_maximum_fusion.5.scale_ref, f32[6,256,256]{2,1,0:T(8,128)} %shard_map.281.rot_ref, f32[6,256,256]{2,1,0:T(8,128)} %m_ref.1, f32[6,256,256]{2,1,0:T(8,128)} %v_ref.1, f32[6,256,1024]{2,1,0:T(8,128)} %l_ref.3, ...), custom_call_target="tpu_custom_call" | custom-call | flops 2415919104 | bytes 11010048 | tf_op jit(solution)/shard_map/pallas_call | solution.py:1048
  923.5 12.5 %multiply_subtract_fusion = (f32[4098,256]{1,0:T(8,128)}, f32[4098,256]{1,0:T(8,128)}, f32[4098,256]{1,0:T(8,128)}) fusion(f32[4098,256]{1,0:T(8,128)} %param.30, f32[]{:T(128)} %bitcast.55, f32[]{:T(128)} %bitcast.54, f32[]{:T(128)} %min.3, f32[4098,256]{1,0:T(8,128)} %shard_map.279, bf16[4160,256]{1,0:T(8,128)(2,1)S(1)} %copy-done.3, ...), kind=kLoop, calls=%fused_computation.12 | loop fusion | flops 18883584 | bytes 31472652 | tf_op jit(solution)/shard_map/sub | solution.py:1684
  935.9 45.0 %reduce-scatter.5.cloned.1.call-done = bf16[6,256,256]{2,1,0:T(8,128)(2,1)} async-done(((bf16[6,1024,256]{2,1,0:T(8,128)(2,1)}), bf16[6,256,256]{2,1,0:T(8,128)(2,1)}) %reduce-scatter.5.cloned.1.call-update) | async-done | bytes 786448 | tf_op jit(solution)/shard_map/reduce_scatter | solution.py:1968
  (232 shorter events, 176.9 us)
Async XLA Ops:
  7.2 378.6 %all-gather.3.cloned.1.call-start = ((), (), s32[]{:S(2)}) async-start(), calls=%async_computation.3 | async-start | bytes 10649600 | tf_op jit(solution)/shard_map/all_gather | solution.py:1740
  21.6 99.9 %copy-start.27 = (s32[1024]{0:T(1024)}, s32[1024]{0:T(1024)S(1)}, u32[]{:S(2)}) copy-start(s32[1024]{0:T(1024)S(1)} %get-tuple-element.62) | copy-start | bytes 12292
  122.6 37.7 %copy-start.10 = (s32[4,8,2176]{2,1,0:T(8,128)}, s32[4,8,2176]{2,1,0:T(8,128)S(1)}, u32[]{:S(2)}) copy-start(s32[4,8,2176]{2,1,0:T(8,128)S(1)} %reshape.285) | copy-start | bytes 835588
  122.8 28.3 %copy-start.12 = (f32[38216]{0:T(1024)S(1)}, f32[38216]{0:T(1024)}, u32[]{:S(2)}) copy-start(f32[38216]{0:T(1024)} %param.33) | copy-start | bytes 458596
  146.9 132.4 %all-to-all-start = ((bf16[4,1024,256]{2,1,0:T(8,128)(2,1)}), bf16[4,1024,256]{2,1,0:T(8,128)(2,1)S(1)}, u32[]{:S(2)}, u32[]{:S(2)}) async-start(bf16[4,1024,256]{2,1,0:T(8,128)(2,1)} %bitcast.171), calls=%async_computation | async-start | bytes 4194304 | tf_op jit(solution)/shard_map/all_to_all | solution.py:1747
  151.2 431.2 %reduce-scatter.3.cloned.1.call-start = ((), (), s32[]{:S(2)}) async-start(), calls=%async_computation.4 | async-start | bytes 10649600 | tf_op jit(solution)/shard_map/reduce_scatter | solution.py:1847
  154.1 136.1 %copy-start.23 = (f32[1024]{0:T(1024)}, f32[1024]{0:T(1024)S(1)}, u32[]{:S(2)}) copy-start(f32[1024]{0:T(1024)S(1)} %get-tuple-element.142) | copy-start | bytes 12292
  157.0 129.0 %copy-start.5 = (bf16[1024,24]{1,0:T(8,128)(2,1)}, bf16[1024,24]{1,0:T(8,128)(2,1)S(1)}, u32[]{:S(2)}) copy-start(bf16[1024,24]{1,0:T(8,128)(2,1)S(1)} %convert_element_type.123) | copy-start | bytes 147460
  290.2 61.3 %copy-start.1 = (bf16[4,128,8,256]{3,2,0,1:T(8,128)(2,1)}, bf16[4,128,8,256]{3,2,0,1:T(8,128)(2,1)S(1)}, u32[]{:S(2)}) copy-start(bf16[4,128,8,256]{3,2,0,1:T(8,128)(2,1)S(1)} %copy.136) | copy-start | bytes 6291460
  316.0 32.1 %copy-start.20 = (s32[1,64]{1,0:T(1,128)S(1)}, s32[1,64]{1,0:T(1,128)}, u32[]{:S(2)}) copy-start(s32[1,64]{1,0:T(1,128)} %param.20) | copy-start | bytes 772
  316.0 34.7 %copy-start.15 = (bf16[64,512]{1,0:T(8,128)(2,1)S(1)}, bf16[64,512]{1,0:T(8,128)(2,1)}, u32[]{:S(2)}) copy-start(bf16[64,512]{1,0:T(8,128)(2,1)} %shard_map.261) | copy-start | bytes 196612
  393.9 14.4 %copy-start.9 = (bf16[8,64,1024]{2,1,0:T(8,128)(2,1)S(1)}, bf16[8,64,1024]{2,1,0:T(8,128)(2,1)}, u32[]{:S(2)}) copy-start(bf16[8,64,1024]{2,1,0:T(8,128)(2,1)} %shard_map.265) | copy-start | bytes 3145732
  431.1 21.2 %copy-start.22 = (f32[1024]{0:T(1024)S(1)}, f32[1024]{0:T(1024)}, u32[]{:S(2)}) copy-start(f32[1024]{0:T(1024)} %get-tuple-element.140) | copy-start | bytes 12292
  431.1 229.3 %all-gather.5.cloned.1.call-start = ((), (), s32[]{:S(2)}) async-start(), calls=%async_computation.5 | async-start | bytes 9437184 | tf_op jit(solution)/shard_map/all_gather | solution.py:1923
  533.6 13.5 %copy-start.4 = (f32[1024,24]{1,0:T(8,128)S(1)}, f32[1024,24]{1,0:T(8,128)}, u32[]{:S(2)}) copy-start(f32[1024,24]{1,0:T(8,128)} %get-tuple-element.170) | copy-start | bytes 294916
  533.6 15.7 %copy-start.16 = (f32[64,1024]{1,0:T(8,128)S(1)}, f32[64,1024]{1,0:T(8,128)}, u32[]{:S(2)}) copy-start(f32[64,1024]{1,0:T(8,128)} %get-tuple-element.88) | copy-start | bytes 786436
  533.6 15.7 %copy-start.21 = (s32[1,64]{1,0:T(1,128)S(1)}, s32[1,64]{1,0:T(1,128)}, u32[]{:S(2)}) copy-start(s32[1,64]{1,0:T(1,128)} %param.20) | copy-start | bytes 772
  582.3 20.2 %slice-start = ((s32[4,8,2176]{2,1,0:T(8,128)}), s32[4,8,1024]{2,1,0:T(8,128)S(1)}, s32[]{:S(2)}) async-start(s32[4,8,2176]{2,1,0:T(8,128)} %copy-done.10), calls=%async_computation.7 | async-start | bytes 262144 | tf_op jit(solution)/shard_map/slice | solution.py:1749
  582.3 22.8 %copy-start = (bf16[1024,1024]{1,0:T(8,128)(2,1)S(1)}, bf16[1024,1024]{1,0:T(8,128)(2,1)}, u32[]{:S(2)}) copy-start(bf16[1024,1024]{1,0:T(8,128)(2,1)} %multiply_convert_fusion.1.x_ref.l_ref) | copy-start | bytes 6291460
  585.0 15.7 %collective-permute-start = (bf16[1024,256]{1,0:T(8,128)(2,1)S(1)}, bf16[1024,256]{1,0:T(8,128)(2,1)S(1)}, u32[]{:S(2)}, u32[]{:S(2)}) collective-permute-start(bf16[1024,256]{1,0:T(8,128)(2,1)S(1)} %get-tuple-element.131), channel_id=1, source_target_pairs={{0,8},{8,16},{16,24},{24,0},{1,9},{9,17},{17,25},{25,1},{2,10},{10... | collective-permute-start | bytes 1572872 | tf_op jit(solution)/shard_map/ppermute | solution.py:1670
  601.7 379.2 %reduce-scatter.5.cloned.1.call-start = ((), (), s32[]{:S(2)}) async-start(), calls=%async_computation.6 | async-start | bytes 3932160 | tf_op jit(solution)/shard_map/reduce_scatter | solution.py:1968
  612.2 47.2 %collective-permute-start.1 = (bf16[1024,256]{1,0:T(8,128)(2,1)}, bf16[1024,256]{1,0:T(8,128)(2,1)S(1)}, u32[]{:S(2)}, u32[]{:S(2)}) collective-permute-start(bf16[1024,256]{1,0:T(8,128)(2,1)} %get-tuple-element.129), channel_id=1, source_target_pairs={{0,24},{8,0},{16,8},{24,16},{1,25},{9,1},{17,9},{25,17},{2,26},{10... | collective-permute-start | bytes 1572872 | tf_op jit(solution)/shard_map/ppermute | solution.py:1670
  613.9 45.4 %collective-permute-start.2 = (bf16[1024,256]{1,0:T(8,128)(2,1)S(1)}, bf16[1024,256]{1,0:T(8,128)(2,1)S(1)}, u32[]{:S(2)}, u32[]{:S(2)}) collective-permute-start(bf16[1024,256]{1,0:T(8,128)(2,1)S(1)} %get-tuple-element.130), channel_id=1, source_target_pairs={{0,16},{8,24},{16,0},{24,8},{1,17},{9,25},{17,1},{25,9},{2,18},{10... | collective-permute-start | bytes 1572872 | tf_op jit(solution)/shard_map/ppermute | solution.py:1670
  851.3 30.7 %copy-start.3 = (bf16[4160,256]{1,0:T(8,128)(2,1)S(1)}, bf16[4160,256]{1,0:T(8,128)(2,1)}, u32[]{:S(2)}) copy-start(bf16[4160,256]{1,0:T(8,128)(2,1)} %reduce-scatter.3.cloned.1.call-done) | copy-start | bytes 6389764
  (24 other events, 171.1 us)
Sparse Core Ops, SparseCore 0:
  121.7 198.0 all-gather.2
  431.2 146.9 reduce-scatter.2
  601.8 52.6 all-gather.4
  921.4 59.4 reduce-scatter.4

commit v4 on v3

--- a/solution.py
+++ b/solution.py
@@ -351,6 +351,29 @@
             2 * length * D * BLOCK_COLS * count, count * BLOCK_COLS * (2 * D + 2 * length)
         ),
     )(*operands)
+
+
+def embed_kernel(x_ref, gain_ref, e_ref, n_ref):
+    rows = jnp.concatenate([x_ref[r] for r in range(x_ref.shape[0])], axis=1)
+    e_ref[...] = rows
+    n_ref[...] = rms_gain(rows.astype(F32), gain_ref[...]).astype(BF16)
+
+
+def embed_and_norm(column_parts, gain):
+    parts, length, width = column_parts.shape
+    step = 2 * CHUNK
+    return pl.pallas_call(
+        embed_kernel,
+        grid=(length // step,),
+        in_specs=[
+            pl.BlockSpec((parts, step, width), lambda i: (0, i, 0)),
+            pl.BlockSpec((1, D), lambda i: (0, 0)),
+        ],
+        out_specs=[pl.BlockSpec((step, D), lambda i: (i, 0))] * 2,
+        out_shape=[jax.ShapeDtypeStruct((length, D), BF16)] * 2,
+        compiler_params=params(),
+        cost_estimate=cost(8 * length * D, 6 * length * D),
+    )(column_parts, gain.reshape(1, D))
 
 
 def rope_tables(length):
@@ -723,8 +746,7 @@
     d_into = jnp.zeros((CHUNK, STATE), F32)
     d_outof = jnp.zeros((CHUNK, STATE), F32)
     sum_y = jnp.zeros((CHUNK, LANES), F32)
-    sum_x = jnp.zeros((CHUNK, LANES), F32)
-    sum_k = jnp.zeros((CHUNK, LANES), F32)
+    sum_xk = jnp.zeros((CHUNK, LANES), F32)
     ends = jnp.zeros((8, LANES), F32)
     lane_pos = lax.broadcasted_iota(jnp.int32, (LANES, LANES), 0) // SSM_HEAD_DIM
     head_pos = lax.broadcasted_iota(jnp.int32, (LANES, LANES), 1)
@@ -737,6 +759,8 @@
     for p in range(SSM_HEADS // 2):
         a, cols = 2 * p, slice(p * LANES, (p + 1) * LANES)
         pick = jnp.where(lane_pos + a == head_pos, 1.0, 0.0).astype(BF16)
+        pick_next = jnp.where(lane_pos + a + SSM_HEADS == head_pos, 1.0, 0.0).astype(BF16)
+        pick_two = jnp.concatenate([pick, pick_next], axis=0)
         pick = jnp.concatenate([pick, pick], axis=0)
         heads, grad = xbc_ref[:, cols], g_ref[:, cols]
         dt_wide = spread(low, dt, a)
@@ -771,8 +795,8 @@
         dext[:CHUNK, cols] = (d_scaled * dt_wide + skip_wide * grad) * slope_ref[:, cols]
         both = grad * heads
         sum_y += by_head(grad * y_ref[:, cols] - skip_wide * both - scaled * d_scaled, pick)
-        sum_x += by_head(heads * d_scaled, pick)
-        sum_k += by_head(both, pick)
+        pair = jnp.concatenate([heads * d_scaled, both], axis=1).astype(BF16)
+        sum_xk += dot_nn(pair, pick_two)
     dgram_low = dgram.astype(BF16)
     cols = slice(SSM_INNER, SSM_INNER + STATE)
     dext[:CHUNK, cols] = (d_into + dot_tn(dgram_low, outof)) * slope_ref[:, cols]
@@ -793,8 +817,7 @@
         grad_ref[:, at] = total.astype(BF16)
     dext[CHUNK:, :] = dext[:8, :]
     sums_ref[:, :LANES] = sum_y
-    sums_ref[:, LANES : 2 * LANES] = sum_x
-    sums_ref[:, 2 * LANES :] = sum_k
+    sums_ref[:, LANES:] = sum_xk
     ends_ref[...] = ends.reshape(ends_ref.shape)
 
 
@@ -891,7 +914,7 @@
             ],
             out_specs=[
                 spec["rows"](width),
-                spec["rows"](3 * LANES),
+                spec["rows"](2 * LANES),
                 pl.BlockSpec((1, 8, LANES), lambda i, last: (end - i, 0, 0)),
                 spec["fixed"](8, XBC_WIDTH),
             ],
@@ -903,7 +926,7 @@
         ),
         out_shape=[
             jax.ShapeDtypeStruct((length, width), BF16),
-            jax.ShapeDtypeStruct((length, 3 * LANES), F32),
+            jax.ShapeDtypeStruct((length, 2 * LANES), F32),
             jax.ShapeDtypeStruct((chunks, 8, LANES), F32),
             jax.ShapeDtypeStruct((8, XBC_WIDTH), F32),
         ],
@@ -1258,7 +1281,7 @@
             for h in range(2):
                 flying["tok", 0, h] = start(tok(0, h))
     steps = slots + stages + len(row_bits) - 1
-    tok_at = [(k + 1) * steps // (len(col_bits) + 1) for k in range(len(col_bits))]
+    tok_at = [steps - 1 - 2 * (len(col_bits) - 1 - k) for k in range(len(col_bits))]
     for t in range(steps):
         if t < stages:
             flying["vec", t].wait_recv()
@@ -1591,6 +1614,39 @@
     )(values)
 
 
+def rows_gather_kernel(rows, cols, x_ref, o_ref, send_sem, recv_sem):
+    col_bits = [b for b in ring_bits(rows, cols) if b[0] == 1]
+    place = (lax.axis_index("row"), lax.axis_index("col"))
+    side, partner = doubling(place, col_bits)
+    orders = [o[1 : len(col_bits)] + o[:1] for o in scatter_orders(rows, cols)]
+    greet(col_bits, partner)
+    own = tuple(side(b) for b in col_bits)
+    jobs = {}
+    for h in range(2):
+        o_ref[own + (h,)] = x_ref[h]
+        copy = joiner(
+            side, partner, x_ref.at[h], o_ref, col_bits, orders[h], (h,), send_sem.at[h], recv_sem.at[h]
+        )
+        jobs["x", h] = (copy, 0, 1)
+    run_joins(jobs, {"x": len(col_bits)}, [])
+
+
+def gather_rows(values, rows, cols, collective_id):
+    count, width = values.shape
+    stages = (cols - 1).bit_length()
+    dma = pltpu.SemaphoreType.DMA
+    out = pl.pallas_call(
+        functools.partial(rows_gather_kernel, rows, cols),
+        in_specs=[pl.BlockSpec(memory_space=pltpu.VMEM)],
+        out_specs=pl.BlockSpec(memory_space=pltpu.VMEM),
+        out_shape=jax.ShapeDtypeStruct((2,) * stages + (2, count // 2, width), values.dtype),
+        scratch_shapes=[dma((2, stages)), dma((2, stages))],
+        compiler_params=params(collective_id=collective_id, has_side_effects=True),
+        cost_estimate=cost(1024, cols * values.size * 4),
+    )(values.reshape(2, count // 2, width))
+    return out.reshape(cols * count, width)
+
+
 def scatter_columns_kernel(rows, cols, x_ref, o_ref, *rest):
     bits = [b for b in ring_bits(rows, cols) if b[0] == 1]
     stages = len(bits)
@@ -1655,7 +1711,7 @@
 
 def piece_order(rows):
     order = [0] + [k for pair in range(1, rows // 2 + 1) for k in (pair, rows - pair)][: rows - 1]
-    return order[: rows // 2], order[rows // 2 :]
+    return order[: rows // 4], order[rows // 4 :]
 
 
 def exchange_rows(values, rows):
@@ -1744,7 +1800,9 @@
         table_cols, token_list + owners * (shard_padded - shard_rows), axis=0, mode="clip"
     )
     looked_up, weight_rows = lax.optimization_barrier((looked_up, weight_rows))
-    embedded = lax.all_to_all(looked_up, "row", split_axis=0, concat_axis=1, tiled=True)
+    arrived = lax.all_to_all(
+        looked_up.reshape(rows, length, -1), "row", split_axis=0, concat_axis=0, tiled=True
+    )
     gathered = gather_weights(weight_rows, rows, cols, 3)
     sorted_ints = ints[:, :, length : 2 * length]
     sorted_all = [
@@ -1773,7 +1831,7 @@
     last_docs = segment.reshape(chunks, CHUNK)[:, CHUNK - 1]
     cosine, sine = rope_tables(length)
 
-    normed = rms_gain(embedded.astype(F32), gain_rows[0]).astype(BF16)
+    embedded, normed = embed_and_norm(arrived, gain_rows[0])
     both_proj = project(normed, gathered, block_owner, 0, in_blocks)
     time_raw = jnp.dot(normed, time_low, preferred_element_type=F32)
 
@@ -1814,7 +1872,7 @@
     hidden_two, picked_rows = back_then_norm(
         act_low, gathered, block_owner, down_at, down_blocks, hidden_one, gain_rows[2]
     )
-    rows_all = gather_columns(picked_rows, cols, 4).reshape(-1, D)
+    rows_all = gather_rows(picked_rows, rows, cols, 4)
 
     logits = jnp.einsum("rd,vd->rv", rows_all, table_rows, preferred_element_type=F32)
     local_target = targets_all - col_index * shard_rows
@@ -1887,7 +1945,7 @@
         both_proj, *picked_in, branch_out_grad, place, in_grad_low
     )
     sum_y, sum_x, sum_k = (
-        sums[:, i * LANES : i * LANES + SSM_HEADS] for i in range(3)
+        sums[:, at : at + SSM_HEADS] for at in (0, LANES, LANES + SSM_HEADS)
     )
     skip_grad = jnp.sum(sum_k, axis=0)
     cum_grad = sum_y.reshape(chunks, CHUNK, SSM_HEADS)

time: 1000 us -> 973 us (0.973)
  waiting for transfers between devices: 58.9 us -> 45 us
  Pallas kernels: 723 us -> 711 us
    pallas_call x2 -> x1, Pallas kernels: 24.7 us -> 6.3 us  [gather_columns(): pl.pallas_call(functools.partial(columns_kernel, cols), in_specs=[pl.Bloc...]
    pallas_call x0 -> x2, Pallas kernels: none -> 18.1 us  [the longest x1 13.7 us: gather_rows(): pl.pallas_call(functools.partial(rows_gather_kernel, rows, cols), in_spec...]
    ppermute x3, waiting for transfers between devices: 13.8 us -> 0.01 us  [exchange_rows(): part = lax.ppermute(part, 'row', [(r, (r + k) % rows) for r in range(rows)])]
    pallas_call x1, Pallas kernels: 187 us -> 176 us  [tail_exchange(): pl.pallas_call(functools.partial(tail_kernel, rows, cols, slots), in_spec...]
  transfers between devices with their start and end apart: 8 -> 8, of which waited for: 2 -> 1; matrix products, arithmetic and copies ran while one was open for 11% -> 11% of each run, Pallas kernels for 37% -> 38%
where the time goes in v4:
time: 973 us; the launch traced here: 961 us
  Pallas kernels  711 us (73%)
  other arithmetic  62.9 us (6%)
  matrix products  60.7 us (6%)
  local copies, waits for them, and re-layouts  48.9 us (5%)
  waiting for transfers between devices  45 us (5%)
  between operations  21.9 us (2%)
  starting transfers between devices  10.9 us (1%)
    pallas_call x1, Pallas kernels, tail_exchange(): pl.pallas_call(functools.partial(tail_kernel, rows, cols, slots), in_spec...  176 us
    pallas_call x1, Pallas kernels, gather_weights(): pl.pallas_call(functools.partial(weights_kernel, rows, cols), in_specs=[p...  113 us
    pallas_call x1, Pallas kernels, front_exchange(): pl.pallas_call(functools.partial(front_kernel, rows, cols), in_specs=[pl....  97.7 us
    pallas_call x1, Pallas kernels, ssm_backward(): pl.pallas_call(ssm_bwd_kernel, grid_spec=pltpu.PrefetchScalarGridSpec(num...  50.6 us
    pallas_call x4, Pallas kernels, weight_grad(): pl.pallas_call(wgrad_kernel, grid_spec=pltpu.PrefetchScalarGridSpec(num_s...  45.5 us
    reduce_scatter x1, waiting for transfers between devices, body(): lax.psum_scatter(partial_update, 'row', scatter_dimension=1, tiled=True)  44.9 us
    pallas_call x6, Pallas kernels, slot_call(): pl.pallas_call(kernel, grid_spec=pltpu.PrefetchScalarGridSpec(num_scalar_...  40.7 us
    pallas_call x1, Pallas kernels, ssm_forward(): pl.pallas_call(ssm_fwd_kernel, grid_spec=pltpu.PrefetchScalarGridSpec(num...  32.1 us
  transfers between devices with their start and end apart: 8, of which 1 were waited for; matrix products, arithmetic and copies ran while one was open for 11% of the time, Pallas kernels for 38%

profile of v4, /device:TPU:0, one launch (start us, length us, event | category | flops | bytes accessed | tf_op | source)
XLA Modules:
  0.0 960.8 jit_solution(8445255725473839287)
XLA Ops:
  23.8 97.7 %shard_map.257 = (s32[2,2,2,2,2,17,128]{6,5,4,3,2,1,0:T(8,128)}, bf16[2,2,2,4,1040,256]{5,4,3,2,1,0:T(8,128)(2,1)}, bf16[2,2,6,256,256]{4,3,2,1,0:T(8,128)(2,1)}) custom-call(s32[17,128]{1,0:T(8,128)} %bitcast.198, bf16[4,1040,256]{2,1,0:T(8,128)(2,1)} %bitcast.156, bf16[6,256,256]{2,1,0:T(8,128)(2,1)} %convert_element_type.97.w_ref), custom_call_target="tpu_custom_call" | custom-call | flops 1048576 | bytes 34078720 | tf_op jit(solution)/shard_map/pallas_call | solution.py:1498
  122.8 24.0 %gather_fusion = bf16[4096,256]{1,0:T(8,128)(2,1)} fusion(bf16[33280,256]{1,0:T(8,128)(2,1)} %bitcast.157, s32[4096]{0:T(1024)S(1)} %broadcast_clamp_fusion), kind=kCustom, calls=%fused_computation | custom fusion | bytes 4210688 | tf_op jit(solution)/shard_map/jit(_take)/gather | solution.py:1799
  161.0 113.2 %shard_map.259 = bf16[4,2,2,2,6,256,256]{6,5,4,3,2,1,0:T(8,128)(2,1)} custom-call(bf16[4,6,256,256]{3,2,1,0:T(8,128)(2,1)} %bitcast.163), custom_call_target="tpu_custom_call" | custom-call | flops 1048576 | bytes 50331648 | tf_op jit(solution)/shard_map/pallas_call | solution.py:1575
  290.4 15.1 %shard_map.260.proj_ref.q_ref.k_ref.v_ref = f32[1024,4096]{1,0:T(8,128)} custom-call(s32[48]{0:T(128)} %own_ref.23, bf16[1024,1024]{1,0:T(8,128)(2,1)} %get-tuple-element.96.x_ref.l_ref, bf16[4,48,256,256]{3,2,1,0:T(8,128)(2,1)} %bitcast.123, bf16[4,48,256,256]{3,2,1,0:T(8,128)(2,1)} %bitcast.124, bf16[4,48,256,256]{3,2,1,0:T(8,128)(2,1)} %bitcast.125, ...), custom_call_target="tpu_custom_call" | custom-call | flops 8589934592 | bytes 18874368 | tf_op jit(solution)/shard_map/pallas_call | solution.py:109
  305.5 8.6 shard_map.262
  314.1 32.1 %shard_map.261 = (f32[1024,1536]{1,0:T(8,128)}, f32[8,128,1536]{2,1,0:T(8,128)}, f32[1024,1792]{1,0:T(8,128)}, f32[1024,1792]{1,0:T(8,128)}, bf16[1024,1536]{1,0:T(8,128)(2,1)}) custom-call(s32[8]{0:T(128)} %bitcast.210, f32[1024,4096]{1,0:T(8,128)} %shard_map.260.proj_ref.q_ref.k_ref.v_ref, f32[1024,8]{1,0:T(8,128)} %convert_element_type.99.near_ref, ...), custom_call_target="tpu_custom_call" | custom-call | flops 1610612736 | bytes 62914560 | tf_op jit(solution)/shard_map/pallas_call | solution.py:838
  367.0 13.7 %shard_map.266 = bf16[2,2,2,2,32,1024]{5,4,3,2,1,0:T(8,128)(2,1)} custom-call(bf16[2,32,1024]{2,1,0:T(8,128)(2,1)} %bitcast.181), custom_call_target="tpu_custom_call" | custom-call | flops 1024 | bytes 2097152 | tf_op jit(solution)/shard_map/pallas_call | solution.py:1638
  380.8 8.3 fusion.69
  401.8 10.7 %convolution_convert_fusion = bf16[4160,1024]{1,0:T(8,128)(2,1)} fusion(bf16[512,1024]{1,0:T(8,128)(2,1)S(1)} %bitcast.172, f32[512,4160]{0,1:T(8,128)} %copy-done.1, f32[512]{0:T(512)S(1)} %get-tuple-element.166, f32[512]{0:T(512)S(1)} %get-tuple-element.128, s32[512]{0:T(512)S(1)} %copy-done.33, pred[4160]{0:T(1024)(128)(4,1)S(1)} %iota_compare_fusion.15), kind=kOutput, calls=%fused_computation.1 | convolution fusion | flops 4381245440 | bytes 18098240 | tf_op jit(solution)/shard_map/rv,rd->vd/dot_general | solution.py:1902
  412.5 12.1 %fusion.62 = f32[512,1024]{1,0:T(8,128)} fusion(bf16[4160,1024]{1,0:T(8,128)(2,1)} %all-gather.3.cloned.1.call-done, f32[512,4160]{0,1:T(8,128)} %copy-done.1, f32[512]{0:T(512)S(1)} %get-tuple-element.166, f32[512]{0:T(512)S(1)} %get-tuple-element.128, s32[512]{0:T(512)S(1)} %copy-done.33, pred[4160]{0:T(1024)(128)(4,1)S(1)} %iota_compare_fusion.15), kind=kOutput, calls=%fused_computation.161 | convolution fusion | flops 4376985600 | bytes 19146816 | tf_op jit(solution)/shard_map/rv,vd->rd/dot_general | solution.py:1901
  426.8 18.6 %shard_map.268 = f32[2,32,1024]{2,1,0:T(8,128)} custom-call(f32[2,2,2,2,32,1024]{5,4,3,2,1,0:T(8,128)} %bitcast.165), custom_call_target="tpu_custom_call" | custom-call | flops 524288 | bytes 4194304 | tf_op jit(solution)/shard_map/pallas_call | solution.py:1696
  454.4 7.7 shard_map.270
  471.9 50.6 %shard_map.272 = (bf16[1024,4096]{1,0:T(8,128)(2,1)}, f32[1024,256]{1,0:T(8,128)}, f32[8,8,128]{2,1,0:T(8,128)}, f32[8,1792]{1,0:T(8,128)}) custom-call(s32[8]{0:T(128)} %bitcast.211, f32[1024,4096]{1,0:T(8,128)} %shard_map.260.proj_ref.q_ref.k_ref.v_ref, f32[1024,8]{1,0:T(8,128)} %convert_element_type.99.near_ref, f32[4,1792]{1,0:T(4,128)} %reshape.270.cw_ref, ...), custom_call_target="tpu_custom_call" | custom-call | flops 4831838208 | bytes 94371840 | tf_op jit(solution)/shard_map/pallas_call | solution.py:890
  525.9 13.4 %shard_map.273 = bf16[1024,4096]{1,0:T(8,128)(2,1)} custom-call(s32[64]{0:T(128)} %bitcast.185, f32[1024,4096]{1,0:T(8,128)} %shard_map.260.proj_ref.q_ref.k_ref.v_ref, f32[1024,4096]{1,0:T(8,128)} %shard_map.260.proj_ref.q_ref.k_ref.v_ref, f32[1024,4096]{1,0:T(8,128)} %shard_map.260.proj_ref.q_ref.k_ref.v_ref, ...), custom_call_target="tpu_custom_call", output_to_operand_aliasing={{}: (11, {})} | custom-call | flops 335544320 | bytes 10485760 | tf_op jit(solution)/shard_map/pallas_call | solution.py:569
  547.1 21.0 %shard_map.274 = (f32[1024,1024]{1,0:T(8,128)}, bf16[1024,1024]{1,0:T(8,128)(2,1)}, f32[1,1024]{1,0:T(1,128)}) custom-call(s32[48]{0:T(128)} %own_ref.23, bf16[1,1024,4096]{2,1,0:T(8,128)(2,1)} %bitcast.154, bf16[4,48,256,256]{3,2,1,0:T(8,128)(2,1)} %bitcast.149, bf16[4,48,256,256]{3,2,1,0:T(8,128)(2,1)} %bitcast.150, bf16[4,48,256,256]{3,2,1,0:T(8,128)(2,1)} %bitcast.151, ...), custom_call_target="tpu_custom_call" | custom-call | flops 8589934592 | bytes 16777216 | tf_op jit(solution)/shard_map/pallas_call | solution.py:278
  599.8 12.0 %shard_map.276.rest_0_ = bf16[4,48,256,256]{3,2,1,0:T(8,128)(2,1)} custom-call(s32[48]{0:T(128)} %own_ref.23, bf16[64,1024]{1,0:T(8,128)(2,1)} %get-tuple-element.98.x_ref.l_ref, bf16[2,64,2048]{2,1,0:T(8,128)(2,1)} %shard_map.269.rest_0_.rest_1_.r_ref, bf16[4,48,256,256]{3,2,1,0:T(8,128)(2,1)} %shard_map.275.rest_0_), custom_call_target="tpu_custom_call", output_to_operand_aliasing={{}: (3, {})} | custom-call | flops 536870912 | bytes 8912896 | tf_op jit(solution)/shard_map/pallas_call | solution.py:336
  618.8 19.4 %shard_map.278 = bf16[4,48,256,256]{3,2,1,0:T(8,128)(2,1)} custom-call(s32[48]{0:T(128)} %own_ref.23, bf16[1024,1024]{1,0:T(8,128)(2,1)} %get-tuple-element.96.x_ref.l_ref, bf16[1,1024,4096]{2,1,0:T(8,128)(2,1)} %bitcast.155, bf16[4,48,256,256]{3,2,1,0:T(8,128)(2,1)} %shard_map.277.rest_0_), custom_call_target="tpu_custom_call", output_to_operand_aliasing={{}: (3, {})} | custom-call | flops 8589934592 | bytes 16777216 | tf_op jit(solution)/shard_map/pallas_call | solution.py:336
  639.5 176.0 %shard_map.279 = (bf16[2,2,6,256,256]{4,3,2,1,0:T(8,128)(2,1)}, bf16[2,2,2,2,1536,256]{5,4,3,2,1,0:T(8,128)(2,1)}, f32[304,128]{1,0:T(8,128)}) custom-call(bf16[2,2,2,2,2,6,256,256]{7,6,5,4,3,2,1,0:T(8,128)(2,1)} %bitcast.153, bf16[2,1536,256]{2,1,0:T(8,128)(2,1)} %bitcast.160, f32[304,128]{1,0:T(8,128)} %pad_bitcast_fusion.v_ref), custom_call_target="tpu_custom_call" | custom-call | flops 12582912 | bytes 75497472 | tf_op jit(solution)/shard_map/pallas_call | solution.py:1357
  819.2 30.4 %shard_map.280 = f32[4098,256]{1,0:T(8,128)} custom-call(s32[32]{0:T(128)} %reduce_sum.212.lo_ref, s32[32]{0:T(128)} %reduce_sum.213.hi_ref, s32[32768]{0:T(1024)} %copy-done.11, bf16[8192,256]{1,0:T(8,128)(2,1)} %all-gather.5.cloned.1.call-done.rest_0_, bf16[24576,256]{1,0:T(8,128)(2,1)} %bitcast.158), custom_call_target="tpu_custom_call" | custom-call | flops 1073741824 | bytes 16777216 | tf_op jit(solution)/shard_map/pallas_call | solution.py:1009
  855.4 11.7 %shard_map.281 = f32[8,128]{1,0:T(8,128)} custom-call(f32[8,128]{1,0:T(8,128)} %broadcast_in_dim.127.x_ref), custom_call_target="tpu_custom_call" | custom-call | flops 32768 | bytes 131072 | tf_op jit(solution)/shard_map/pallas_call | solution.py:1140
  869.7 8.7 shard_map.282.rot_ref
  878.9 10.4 %shard_map.283 = (f32[6,256,256]{2,1,0:T(8,128)}, f32[6,256,256]{2,1,0:T(8,128)}, bf16[6,1024,256]{2,1,0:T(8,128)(2,1)}) custom-call(f32[3]{0:T(128)} %pad_maximum_fusion.4.scale_ref, f32[6,256,256]{2,1,0:T(8,128)} %shard_map.282.rot_ref, f32[6,256,256]{2,1,0:T(8,128)} %m_ref.1, f32[6,256,256]{2,1,0:T(8,128)} %v_ref.1, f32[6,256,1024]{2,1,0:T(8,128)} %l_ref.3, ...), custom_call_target="tpu_custom_call" | custom-call | flops 2415919104 | bytes 11010048 | tf_op jit(solution)/shard_map/pallas_call | solution.py:1071
  891.5 12.5 %multiply_subtract_fusion = (f32[4098,256]{1,0:T(8,128)}, f32[4098,256]{1,0:T(8,128)}, f32[4098,256]{1,0:T(8,128)}) fusion(f32[4098,256]{1,0:T(8,128)} %param.30, f32[]{:T(128)} %bitcast.53, f32[]{:T(128)} %bitcast.52, f32[]{:T(128)} %min.3, f32[4098,256]{1,0:T(8,128)} %shard_map.280, bf16[4160,256]{1,0:T(8,128)(2,1)S(1)} %copy-done.4, ...), kind=kLoop, calls=%fused_computation.10 | loop fusion | flops 18883584 | bytes 31472652 | tf_op jit(solution)/shard_map/sub | solution.py:1740
  903.9 44.9 %reduce-scatter.5.cloned.1.call-done = bf16[6,256,256]{2,1,0:T(8,128)(2,1)} async-done(((bf16[6,1024,256]{2,1,0:T(8,128)(2,1)}), bf16[6,256,256]{2,1,0:T(8,128)(2,1)}) %reduce-scatter.5.cloned.1.call-update) | async-done | bytes 786448 | tf_op jit(solution)/shard_map/reduce_scatter | solution.py:2026
  (231 shorter events, 166.3 us)
Async XLA Ops:
  7.2 373.6 %all-gather.3.cloned.1.call-start = ((), (), s32[]{:S(2)}) async-start(), calls=%async_computation.3 | async-start | bytes 10649600 | tf_op jit(solution)/shard_map/all_gather | solution.py:1796
  21.6 99.9 %copy-start.30 = (s32[1024]{0:T(1024)}, s32[1024]{0:T(1024)S(1)}, u32[]{:S(2)}) copy-start(s32[1024]{0:T(1024)S(1)} %get-tuple-element.64) | copy-start | bytes 12292
  122.6 37.0 %copy-start.13 = (s32[4,8,2176]{2,1,0:T(8,128)}, s32[4,8,2176]{2,1,0:T(8,128)S(1)}, u32[]{:S(2)}) copy-start(s32[4,8,2176]{2,1,0:T(8,128)S(1)} %reshape.266) | copy-start | bytes 835588
  122.8 28.3 %copy-start.15 = (f32[38216]{0:T(1024)S(1)}, f32[38216]{0:T(1024)}, u32[]{:S(2)}) copy-start(f32[38216]{0:T(1024)} %param.33) | copy-start | bytes 458596
  146.9 132.4 %all-to-all-start = ((bf16[4,1024,256]{2,1,0:T(8,128)(2,1)}), bf16[4,1024,256]{2,1,0:T(8,128)(2,1)S(1)}, u32[]{:S(2)}, u32[]{:S(2)}) async-start(bf16[4,1024,256]{2,1,0:T(8,128)(2,1)} %bitcast.159), calls=%async_computation | async-start | bytes 4194304 | tf_op jit(solution)/shard_map/all_to_all | solution.py:1803
  151.2 422.2 %reduce-scatter.3.cloned.1.call-start = ((), (), s32[]{:S(2)}) async-start(), calls=%async_computation.4 | async-start | bytes 10649600 | tf_op jit(solution)/shard_map/reduce_scatter | solution.py:1905
  156.3 128.7 %copy-start.5 = (bf16[1024,24]{1,0:T(8,128)(2,1)}, bf16[1024,24]{1,0:T(8,128)(2,1)S(1)}, u32[]{:S(2)}) copy-start(bf16[1024,24]{1,0:T(8,128)(2,1)S(1)} %convert_element_type.100) | copy-start | bytes 147460
  278.6 26.9 %copy-start.34 = (f32[24]{0:T(128)}, f32[24]{0:T(128)S(1)}, u32[]{:S(2)}) copy-start(f32[24]{0:T(128)S(1)} %get-tuple-element.148) | copy-start | bytes 292
  289.4 16.1 %copy-start.10 = (f32[8,3,8,128]{3,2,0,1:T(8,128)}, f32[8,3,8,128]{3,2,0,1:T(8,128)S(1)}, u32[]{:S(2)}) copy-start(f32[8,3,8,128]{3,2,0,1:T(8,128)S(1)} %copy.131) | copy-start | bytes 294916
  314.1 32.1 %copy-start.23 = (s32[1,64]{1,0:T(1,128)S(1)}, s32[1,64]{1,0:T(1,128)}, u32[]{:S(2)}) copy-start(s32[1,64]{1,0:T(1,128)} %param.20) | copy-start | bytes 772
  314.1 34.8 %copy-start.18 = (bf16[64,512]{1,0:T(8,128)(2,1)S(1)}, bf16[64,512]{1,0:T(8,128)(2,1)}, u32[]{:S(2)}) copy-start(bf16[64,512]{1,0:T(8,128)(2,1)} %shard_map.262) | copy-start | bytes 196612
  424.6 20.8 %copy-start.25 = (f32[1024]{0:T(1024)S(1)}, f32[1024]{0:T(1024)}, u32[]{:S(2)}) copy-start(f32[1024]{0:T(1024)} %get-tuple-element.144) | copy-start | bytes 12292
  424.6 214.9 %all-gather.5.cloned.1.call-start = ((), (), s32[]{:S(2)}) async-start(), calls=%async_computation.5 | async-start | bytes 4718592 | tf_op jit(solution)/shard_map/all_gather | solution.py:1981
  525.9 13.4 %copy-start.7 = (f32[1024,256]{1,0:T(8,128)S(1)}, f32[1024,256]{1,0:T(8,128)}, u32[]{:S(2)}) copy-start(f32[1024,256]{1,0:T(8,128)} %get-tuple-element.90) | copy-start | bytes 3145732
  525.9 13.4 %copy-start.9 = (f32[1024,24]{1,0:T(8,128)S(1)}, f32[1024,24]{1,0:T(8,128)}, u32[]{:S(2)}) copy-start(f32[1024,24]{1,0:T(8,128)} %get-tuple-element.170) | copy-start | bytes 294916
  525.9 13.4 %copy-start.35 = (f32[24]{0:T(128)S(1)}, f32[24]{0:T(128)}, u32[]{:S(2)}) copy-start(f32[24]{0:T(128)} %copy-done.34) | copy-start | bytes 292
  525.9 14.5 %copy-start.19 = (f32[64,1024]{1,0:T(8,128)S(1)}, f32[64,1024]{1,0:T(8,128)}, u32[]{:S(2)}) copy-start(f32[64,1024]{1,0:T(8,128)} %get-tuple-element.92) | copy-start | bytes 786436
  525.9 14.5 %copy-start.24 = (s32[1,64]{1,0:T(1,128)S(1)}, s32[1,64]{1,0:T(1,128)}, u32[]{:S(2)}) copy-start(s32[1,64]{1,0:T(1,128)} %param.20) | copy-start | bytes 772
  576.3 372.6 %reduce-scatter.5.cloned.1.call-start = ((), (), s32[]{:S(2)}) async-start(), calls=%async_computation.6 | async-start | bytes 3932160 | tf_op jit(solution)/shard_map/reduce_scatter | solution.py:2026
  577.4 22.4 %copy-start.11 = (s32[32768]{0:T(1024)}, s32[32768]{0:T(1024)S(1)}, u32[]{:S(2)}) copy-start(s32[32768]{0:T(1024)S(1)} %get-tuple-element.126.ids_ref) | copy-start | bytes 393220
  586.7 51.5 %collective-permute-start = (bf16[1024,256]{1,0:T(8,128)(2,1)}, bf16[1024,256]{1,0:T(8,128)(2,1)S(1)}, u32[]{:S(2)}, u32[]{:S(2)}) collective-permute-start(bf16[1024,256]{1,0:T(8,128)(2,1)} %get-tuple-element.133), channel_id=1, source_target_pairs={{0,8},{8,16},{16,24},{24,0},{1,9},{9,17},{17,25},{25,1},{2,10},{10... | collective-permute-start | bytes 1572872 | tf_op jit(solution)/shard_map/ppermute | solution.py:1726
  588.9 49.3 %collective-permute-start.2 = (bf16[1024,256]{1,0:T(8,128)(2,1)}, bf16[1024,256]{1,0:T(8,128)(2,1)S(1)}, u32[]{:S(2)}, u32[]{:S(2)}) collective-permute-start(bf16[1024,256]{1,0:T(8,128)(2,1)} %get-tuple-element.134), channel_id=1, source_target_pairs={{0,16},{8,24},{16,0},{24,8},{1,17},{9,25},{17,1},{25,9},{2,18},{10... | collective-permute-start | bytes 1572872 | tf_op jit(solution)/shard_map/ppermute | solution.py:1726
  591.1 47.2 %collective-permute-start.1 = (bf16[1024,256]{1,0:T(8,128)(2,1)S(1)}, bf16[1024,256]{1,0:T(8,128)(2,1)S(1)}, u32[]{:S(2)}, u32[]{:S(2)}) collective-permute-start(bf16[1024,256]{1,0:T(8,128)(2,1)S(1)} %get-tuple-element.135), channel_id=1, source_target_pairs={{0,24},{8,0},{16,8},{24,16},{1,25},{9,1},{17,9},{25,17},{2,26},{10... | collective-permute-start | bytes 1572872 | tf_op jit(solution)/shard_map/ppermute | solution.py:1726
  819.2 30.4 %copy-start.4 = (bf16[4160,256]{1,0:T(8,128)(2,1)S(1)}, bf16[4160,256]{1,0:T(8,128)(2,1)}, u32[]{:S(2)}) copy-start(bf16[4160,256]{1,0:T(8,128)(2,1)} %reduce-scatter.3.cloned.1.call-done) | copy-start | bytes 6389764
  (27 other events, 177.7 us)
Sparse Core Ops, SparseCore 0:
  121.7 198.0 all-gather.2
  424.7 147.4 reduce-scatter.2
  576.4 37.2 all-gather.4
  889.4 59.3 reduce-scatter.4

commit v5 on v4

--- a/solution.py
+++ b/solution.py
@@ -23,6 +23,7 @@
 QROWS = 256
 LANES = 128
 NO_TOKEN = 1 << 30
+LISTS = 4
 TABLE_PARTS = 4
 PAD_ROWS = 16 * TABLE_PARTS
 GROUP = 4
@@ -955,7 +956,7 @@
 def rows_kernel(counts, lo_ref, hi_ref, ids_ref, *rest):
     step = pl.program_id(0)
     g_refs, (o_ref, wide) = rest[:-2], rest[-2:]
-    group = wide.shape[0]
+    group = wide.shape[0] // LISTS
 
     @pl.when(step == 0)
     def _():
@@ -969,28 +970,30 @@
             wide[...] = g_ref[...].astype(F32)
 
         before = before + count
-    low, high = lo_ref[step], hi_ref[step]
-
-    def one(j):
-        o_ref[pl.ds(ids_ref[step * group + j], 1), :] += wide[pl.ds(j, 1), :]
-
-    def eight(k, carry):
-        for u in range(8):
-            one(low + 8 * k + u)
-        return carry
-
-    def rest_of(j, carry):
-        one(j)
-        return carry
-
-    eights = (high - low) // 8
-    lax.fori_loop(0, eights, eight, 0)
-    lax.fori_loop(low + 8 * eights, high, rest_of, 0)
+    for q in range(LISTS):
+        at = step * LISTS + q
+        low, high = lo_ref[at], hi_ref[at]
+
+        def one(j, at=at, q=q):
+            o_ref[pl.ds(ids_ref[at * group + j], 1), :] += wide[pl.ds(q * group + j, 1), :]
+
+        def eight(k, carry, one=one, low=low):
+            for u in range(8):
+                one(low + 8 * k + u)
+            return carry
+
+        def rest_of(j, carry, one=one):
+            one(j)
+            return carry
+
+        eights = (high - low) // 8
+        lax.fori_loop(0, eights, eight, 0)
+        lax.fori_loop(low + 8 * eights, high, rest_of, 0)
 
 
 def rows_by_token(local_ids, grads, shard_rows, group):
     width = grads[0].shape[1]
-    counts = [g.shape[0] // group for g in grads]
+    counts = [g.shape[0] // (LISTS * group) for g in grads]
     lists = local_ids.reshape(-1, group)
     low = jnp.sum((lists < 0).astype(jnp.int32), axis=1)
     high = jnp.sum((lists < shard_rows).astype(jnp.int32), axis=1)
@@ -998,7 +1001,7 @@
     for count in counts:
         specs.append(
             pl.BlockSpec(
-                (group, width),
+                (LISTS * group, width),
                 lambda i, lo, hi, ids, before=before, count=count: (
                     jnp.clip(i - before, 0, count - 1),
                     0,
@@ -1013,11 +1016,11 @@
             grid=(before,),
             in_specs=specs,
             out_specs=pl.BlockSpec((shard_rows, width), lambda i, lo, hi, ids: (0, 0)),
-            scratch_shapes=[pltpu.VMEM((group, width), F32)],
+            scratch_shapes=[pltpu.VMEM((LISTS * group, width), F32)],
         ),
         out_shape=jax.ShapeDtypeStruct((shard_rows, width), F32),
         compiler_params=params(),
-        cost_estimate=cost(before * group * width * LANES, before * group * width * 2),
+        cost_estimate=cost(before * group * width * LANES, before * group * width * 8),
     )(low, high, local_ids, *grads)
 
 
@@ -1454,12 +1457,12 @@
         copy = joiner(
             side, partner, t_ref.at[p], to_ref, col_bits, orders[p % 2], (p,), t_send.at[p], t_recv.at[p]
         )
-        jobs["t", p] = (copy, 2 + p // 2, 2)
+        jobs["t", p] = (copy, 1 + p // 2, 3)
     for p in range(w_ref.shape[0]):
         copy = joiner(
             side, partner, w_ref.at[p], wo_ref, row_bits, row_bits, (p,), w_send.at[p], w_recv.at[p]
         )
-        jobs["w", p] = (copy, 1 + p, 1)
+        jobs["w", p] = (copy, p, 1)
     run_joins(jobs, {"i": len(bits), "t": len(col_bits), "w": len(row_bits)}, keeps)
 
 

time: 973 us -> 957 us (0.984)
  Pallas kernels: 711 us -> 696 us
  transfers between devices with their start and end apart: 8 -> 8, of which waited for: 1 -> 1; matrix products, arithmetic and copies ran while one was open for 11% -> 11% of each run, Pallas kernels for 38% -> 39%
where the time goes in v5:
time: 957 us; the launch traced here: 947 us
  Pallas kernels  696 us (73%)
  other arithmetic  62.9 us (7%)
  matrix products  60.8 us (6%)
  local copies, waits for them, and re-layouts  50.1 us (5%)
  waiting for transfers between devices  45.1 us (5%)
  between operations  21.9 us (2%)
  starting transfers between devices  9.58 us (1%)
    pallas_call x1, Pallas kernels, tail_exchange(): pl.pallas_call(functools.partial(tail_kernel, rows, cols, slots), in_spec...  177 us
    pallas_call x1, Pallas kernels, gather_weights(): pl.pallas_call(functools.partial(weights_kernel, rows, cols), in_specs=[p...  113 us
    pallas_call x1, Pallas kernels, front_exchange(): pl.pallas_call(functools.partial(front_kernel, rows, cols), in_specs=[pl....  91.5 us
    pallas_call x1, Pallas kernels, ssm_backward(): pl.pallas_call(ssm_bwd_kernel, grid_spec=pltpu.PrefetchScalarGridSpec(num...  50.6 us
    pallas_call x4, Pallas kernels, weight_grad(): pl.pallas_call(wgrad_kernel, grid_spec=pltpu.PrefetchScalarGridSpec(num_s...  45.4 us
    reduce_scatter x1, waiting for transfers between devices, body(): lax.psum_scatter(partial_update, 'row', scatter_dimension=1, tiled=True)  45 us
    pallas_call x6, Pallas kernels, slot_call(): pl.pallas_call(kernel, grid_spec=pltpu.PrefetchScalarGridSpec(num_scalar_...  40.7 us
    pallas_call x1, Pallas kernels, ssm_forward(): pl.pallas_call(ssm_fwd_kernel, grid_spec=pltpu.PrefetchScalarGridSpec(num...  32.1 us
  transfers between devices with their start and end apart: 8, of which 1 were waited for; matrix products, arithmetic and copies ran while one was open for 11% of the time, Pallas kernels for 39%

profile of v5, /device:TPU:0, one launch (start us, length us, event | category | flops | bytes accessed | tf_op | source)
XLA Modules:
  0.0 946.5 jit_solution(1565738238265839640)
XLA Ops:
  23.8 91.5 %shard_map.257 = (s32[2,2,2,2,2,17,128]{6,5,4,3,2,1,0:T(8,128)}, bf16[2,2,2,4,1040,256]{5,4,3,2,1,0:T(8,128)(2,1)}, bf16[2,2,6,256,256]{4,3,2,1,0:T(8,128)(2,1)}) custom-call(s32[17,128]{1,0:T(8,128)} %bitcast.198, bf16[4,1040,256]{2,1,0:T(8,128)(2,1)} %bitcast.156, bf16[6,256,256]{2,1,0:T(8,128)(2,1)} %convert_element_type.97.w_ref), custom_call_target="tpu_custom_call" | custom-call | flops 1048576 | bytes 34078720 | tf_op jit(solution)/shard_map/pallas_call | solution.py:1501
  116.6 25.1 %gather_fusion = bf16[4096,256]{1,0:T(8,128)(2,1)} fusion(bf16[33280,256]{1,0:T(8,128)(2,1)} %bitcast.157, s32[4096]{0:T(1024)S(1)} %broadcast_clamp_fusion), kind=kCustom, calls=%fused_computation | custom fusion | bytes 4210688 | tf_op jit(solution)/shard_map/jit(_take)/gather | solution.py:1802
  155.4 112.7 %shard_map.259 = bf16[4,2,2,2,6,256,256]{6,5,4,3,2,1,0:T(8,128)(2,1)} custom-call(bf16[4,6,256,256]{3,2,1,0:T(8,128)(2,1)} %bitcast.163), custom_call_target="tpu_custom_call" | custom-call | flops 1048576 | bytes 50331648 | tf_op jit(solution)/shard_map/pallas_call | solution.py:1578
  284.4 15.1 %shard_map.260.proj_ref.q_ref.k_ref.v_ref = f32[1024,4096]{1,0:T(8,128)} custom-call(s32[48]{0:T(128)} %own_ref.23, bf16[1024,1024]{1,0:T(8,128)(2,1)} %get-tuple-element.96.x_ref.l_ref, bf16[4,48,256,256]{3,2,1,0:T(8,128)(2,1)} %bitcast.123, bf16[4,48,256,256]{3,2,1,0:T(8,128)(2,1)} %bitcast.124, bf16[4,48,256,256]{3,2,1,0:T(8,128)(2,1)} %bitcast.125, ...), custom_call_target="tpu_custom_call" | custom-call | flops 8589934592 | bytes 18874368 | tf_op jit(solution)/shard_map/pallas_call | solution.py:110
  299.4 8.6 shard_map.262
  308.1 32.1 %shard_map.261 = (f32[1024,1536]{1,0:T(8,128)}, f32[8,128,1536]{2,1,0:T(8,128)}, f32[1024,1792]{1,0:T(8,128)}, f32[1024,1792]{1,0:T(8,128)}, bf16[1024,1536]{1,0:T(8,128)(2,1)}) custom-call(s32[8]{0:T(128)} %bitcast.210, f32[1024,4096]{1,0:T(8,128)} %shard_map.260.proj_ref.q_ref.k_ref.v_ref, f32[1024,8]{1,0:T(8,128)} %convert_element_type.99.near_ref, ...), custom_call_target="tpu_custom_call" | custom-call | flops 1610612736 | bytes 62914560 | tf_op jit(solution)/shard_map/pallas_call | solution.py:839
  361.0 13.7 %shard_map.266 = bf16[2,2,2,2,32,1024]{5,4,3,2,1,0:T(8,128)(2,1)} custom-call(bf16[2,32,1024]{2,1,0:T(8,128)(2,1)} %bitcast.181), custom_call_target="tpu_custom_call" | custom-call | flops 1024 | bytes 2097152 | tf_op jit(solution)/shard_map/pallas_call | solution.py:1641
  374.7 8.5 fusion.69
  396.0 10.7 %convolution_convert_fusion = bf16[4160,1024]{1,0:T(8,128)(2,1)} fusion(bf16[512,1024]{1,0:T(8,128)(2,1)S(1)} %bitcast.172, f32[512,4160]{0,1:T(8,128)} %copy-done.1, f32[512]{0:T(512)S(1)} %get-tuple-element.166, f32[512]{0:T(512)S(1)} %get-tuple-element.128, s32[512]{0:T(512)S(1)} %copy-done.33, pred[4160]{0:T(1024)(128)(4,1)S(1)} %iota_compare_fusion.15), kind=kOutput, calls=%fused_computation.1 | convolution fusion | flops 4381245440 | bytes 18098240 | tf_op jit(solution)/shard_map/rv,rd->vd/dot_general | solution.py:1905
  406.6 12.1 %fusion.62 = f32[512,1024]{1,0:T(8,128)} fusion(bf16[4160,1024]{1,0:T(8,128)(2,1)} %all-gather.3.cloned.1.call-done, f32[512,4160]{0,1:T(8,128)} %copy-done.1, f32[512]{0:T(512)S(1)} %get-tuple-element.166, f32[512]{0:T(512)S(1)} %get-tuple-element.128, s32[512]{0:T(512)S(1)} %copy-done.33, pred[4160]{0:T(1024)(128)(4,1)S(1)} %iota_compare_fusion.15), kind=kOutput, calls=%fused_computation.161 | convolution fusion | flops 4376985600 | bytes 19146816 | tf_op jit(solution)/shard_map/rv,vd->rd/dot_general | solution.py:1904
  420.8 18.8 %shard_map.268 = f32[2,32,1024]{2,1,0:T(8,128)} custom-call(f32[2,2,2,2,32,1024]{5,4,3,2,1,0:T(8,128)} %bitcast.165), custom_call_target="tpu_custom_call" | custom-call | flops 524288 | bytes 4194304 | tf_op jit(solution)/shard_map/pallas_call | solution.py:1699
  448.6 7.7 shard_map.270
  466.2 50.6 %shard_map.272 = (bf16[1024,4096]{1,0:T(8,128)(2,1)}, f32[1024,256]{1,0:T(8,128)}, f32[8,8,128]{2,1,0:T(8,128)}, f32[8,1792]{1,0:T(8,128)}) custom-call(s32[8]{0:T(128)} %bitcast.211, f32[1024,4096]{1,0:T(8,128)} %shard_map.260.proj_ref.q_ref.k_ref.v_ref, f32[1024,8]{1,0:T(8,128)} %convert_element_type.99.near_ref, f32[4,1792]{1,0:T(4,128)} %reshape.270.cw_ref, ...), custom_call_target="tpu_custom_call" | custom-call | flops 4831838208 | bytes 94371840 | tf_op jit(solution)/shard_map/pallas_call | solution.py:891
  520.2 13.6 %shard_map.273 = bf16[1024,4096]{1,0:T(8,128)(2,1)} custom-call(s32[64]{0:T(128)} %bitcast.185, f32[1024,4096]{1,0:T(8,128)} %shard_map.260.proj_ref.q_ref.k_ref.v_ref, f32[1024,4096]{1,0:T(8,128)} %shard_map.260.proj_ref.q_ref.k_ref.v_ref, f32[1024,4096]{1,0:T(8,128)} %shard_map.260.proj_ref.q_ref.k_ref.v_ref, ...), custom_call_target="tpu_custom_call", output_to_operand_aliasing={{}: (11, {})} | custom-call | flops 335544320 | bytes 10485760 | tf_op jit(solution)/shard_map/pallas_call | solution.py:570
  541.6 21.0 %shard_map.274 = (f32[1024,1024]{1,0:T(8,128)}, bf16[1024,1024]{1,0:T(8,128)(2,1)}, f32[1,1024]{1,0:T(1,128)}) custom-call(s32[48]{0:T(128)} %own_ref.23, bf16[1,1024,4096]{2,1,0:T(8,128)(2,1)} %bitcast.154, bf16[4,48,256,256]{3,2,1,0:T(8,128)(2,1)} %bitcast.149, bf16[4,48,256,256]{3,2,1,0:T(8,128)(2,1)} %bitcast.150, bf16[4,48,256,256]{3,2,1,0:T(8,128)(2,1)} %bitcast.151, ...), custom_call_target="tpu_custom_call" | custom-call | flops 8589934592 | bytes 16777216 | tf_op jit(solution)/shard_map/pallas_call | solution.py:279
  593.8 12.0 %shard_map.276.rest_0_ = bf16[4,48,256,256]{3,2,1,0:T(8,128)(2,1)} custom-call(s32[48]{0:T(128)} %own_ref.23, bf16[64,1024]{1,0:T(8,128)(2,1)} %get-tuple-element.98.x_ref.l_ref, bf16[2,64,2048]{2,1,0:T(8,128)(2,1)} %shard_map.269.rest_0_.rest_1_.r_ref, bf16[4,48,256,256]{3,2,1,0:T(8,128)(2,1)} %shard_map.275.rest_0_), custom_call_target="tpu_custom_call", output_to_operand_aliasing={{}: (3, {})} | custom-call | flops 536870912 | bytes 8912896 | tf_op jit(solution)/shard_map/pallas_call | solution.py:337
  612.7 19.4 %shard_map.278 = bf16[4,48,256,256]{3,2,1,0:T(8,128)(2,1)} custom-call(s32[48]{0:T(128)} %own_ref.23, bf16[1024,1024]{1,0:T(8,128)(2,1)} %get-tuple-element.96.x_ref.l_ref, bf16[1,1024,4096]{2,1,0:T(8,128)(2,1)} %bitcast.155, bf16[4,48,256,256]{3,2,1,0:T(8,128)(2,1)} %shard_map.277.rest_0_), custom_call_target="tpu_custom_call", output_to_operand_aliasing={{}: (3, {})} | custom-call | flops 8589934592 | bytes 16777216 | tf_op jit(solution)/shard_map/pallas_call | solution.py:337
  633.3 176.9 %shard_map.279 = (bf16[2,2,6,256,256]{4,3,2,1,0:T(8,128)(2,1)}, bf16[2,2,2,2,1536,256]{5,4,3,2,1,0:T(8,128)(2,1)}, f32[304,128]{1,0:T(8,128)}) custom-call(bf16[2,2,2,2,2,6,256,256]{7,6,5,4,3,2,1,0:T(8,128)(2,1)} %bitcast.153, bf16[2,1536,256]{2,1,0:T(8,128)(2,1)} %bitcast.160, f32[304,128]{1,0:T(8,128)} %pad_bitcast_fusion.v_ref), custom_call_target="tpu_custom_call" | custom-call | flops 12582912 | bytes 75497472 | tf_op jit(solution)/shard_map/pallas_call | solution.py:1360
  813.9 22.4 %shard_map.280 = f32[4098,256]{1,0:T(8,128)} custom-call(s32[32]{0:T(128)} %reduce_sum.212.lo_ref, s32[32]{0:T(128)} %reduce_sum.213.hi_ref, s32[32768]{0:T(1024)} %copy-done.11, bf16[8192,256]{1,0:T(8,128)(2,1)} %all-gather.5.cloned.1.call-done.rest_0_, bf16[24576,256]{1,0:T(8,128)(2,1)} %bitcast.158), custom_call_target="tpu_custom_call" | custom-call | flops 268435456 | bytes 16777216 | tf_op jit(solution)/shard_map/pallas_call | solution.py:1012
  842.0 10.7 %shard_map.281 = f32[8,128]{1,0:T(8,128)} custom-call(f32[8,128]{1,0:T(8,128)} %broadcast_in_dim.127.x_ref), custom_call_target="tpu_custom_call" | custom-call | flops 32768 | bytes 131072 | tf_op jit(solution)/shard_map/pallas_call | solution.py:1143
  855.3 8.7 shard_map.282.rot_ref
  864.6 10.4 %shard_map.283 = (f32[6,256,256]{2,1,0:T(8,128)}, f32[6,256,256]{2,1,0:T(8,128)}, bf16[6,1024,256]{2,1,0:T(8,128)(2,1)}) custom-call(f32[3]{0:T(128)} %pad_maximum_fusion.4.scale_ref, f32[6,256,256]{2,1,0:T(8,128)} %shard_map.282.rot_ref, f32[6,256,256]{2,1,0:T(8,128)} %m_ref.1, f32[6,256,256]{2,1,0:T(8,128)} %v_ref.1, f32[6,256,1024]{2,1,0:T(8,128)} %l_ref.3, ...), custom_call_target="tpu_custom_call" | custom-call | flops 2415919104 | bytes 11010048 | tf_op jit(solution)/shard_map/pallas_call | solution.py:1074
  877.1 12.5 %multiply_subtract_fusion = (f32[4098,256]{1,0:T(8,128)}, f32[4098,256]{1,0:T(8,128)}, f32[4098,256]{1,0:T(8,128)}) fusion(f32[4098,256]{1,0:T(8,128)} %param.30, f32[]{:T(128)} %bitcast.53, f32[]{:T(128)} %bitcast.52, f32[]{:T(128)} %min.3, f32[4098,256]{1,0:T(8,128)} %shard_map.280, bf16[4160,256]{1,0:T(8,128)(2,1)S(1)} %copy-done.4, ...), kind=kLoop, calls=%fused_computation.10 | loop fusion | flops 18883584 | bytes 31472652 | tf_op jit(solution)/shard_map/sub | solution.py:1743
  889.6 45.0 %reduce-scatter.5.cloned.1.call-done = bf16[6,256,256]{2,1,0:T(8,128)(2,1)} async-done(((bf16[6,1024,256]{2,1,0:T(8,128)(2,1)}), bf16[6,256,256]{2,1,0:T(8,128)(2,1)}) %reduce-scatter.5.cloned.1.call-update) | async-done | bytes 786448 | tf_op jit(solution)/shard_map/reduce_scatter | solution.py:2029
  (231 shorter events, 165.2 us)
Async XLA Ops:
  7.2 367.5 %all-gather.3.cloned.1.call-start = ((), (), s32[]{:S(2)}) async-start(), calls=%async_computation.3 | async-start | bytes 10649600 | tf_op jit(solution)/shard_map/all_gather | solution.py:1799
  21.6 93.7 %copy-start.30 = (s32[1024]{0:T(1024)}, s32[1024]{0:T(1024)S(1)}, u32[]{:S(2)}) copy-start(s32[1024]{0:T(1024)S(1)} %get-tuple-element.64) | copy-start | bytes 12292
  116.4 37.6 %copy-start.13 = (s32[4,8,2176]{2,1,0:T(8,128)}, s32[4,8,2176]{2,1,0:T(8,128)S(1)}, u32[]{:S(2)}) copy-start(s32[4,8,2176]{2,1,0:T(8,128)S(1)} %reshape.266) | copy-start | bytes 835588
  116.6 28.9 %copy-start.15 = (f32[38216]{0:T(1024)S(1)}, f32[38216]{0:T(1024)}, u32[]{:S(2)}) copy-start(f32[38216]{0:T(1024)} %param.33) | copy-start | bytes 458596
  141.7 131.4 %all-to-all-start = ((bf16[4,1024,256]{2,1,0:T(8,128)(2,1)}), bf16[4,1024,256]{2,1,0:T(8,128)(2,1)S(1)}, u32[]{:S(2)}, u32[]{:S(2)}) async-start(bf16[4,1024,256]{2,1,0:T(8,128)(2,1)} %bitcast.159), calls=%async_computation | async-start | bytes 4194304 | tf_op jit(solution)/shard_map/all_to_all | solution.py:1806
  145.5 422.3 %reduce-scatter.3.cloned.1.call-start = ((), (), s32[]{:S(2)}) async-start(), calls=%async_computation.4 | async-start | bytes 10649600 | tf_op jit(solution)/shard_map/reduce_scatter | solution.py:1908
  150.7 128.3 %copy-start.5 = (bf16[1024,24]{1,0:T(8,128)(2,1)}, bf16[1024,24]{1,0:T(8,128)(2,1)S(1)}, u32[]{:S(2)}) copy-start(bf16[1024,24]{1,0:T(8,128)(2,1)S(1)} %convert_element_type.100) | copy-start | bytes 147460
  272.5 26.9 %copy-start.34 = (f32[24]{0:T(128)}, f32[24]{0:T(128)S(1)}, u32[]{:S(2)}) copy-start(f32[24]{0:T(128)S(1)} %get-tuple-element.148) | copy-start | bytes 292
  283.3 16.1 %copy-start.10 = (f32[8,3,8,128]{3,2,0,1:T(8,128)}, f32[8,3,8,128]{3,2,0,1:T(8,128)S(1)}, u32[]{:S(2)}) copy-start(f32[8,3,8,128]{3,2,0,1:T(8,128)S(1)} %copy.131) | copy-start | bytes 294916
  308.0 32.1 %copy-start.23 = (s32[1,64]{1,0:T(1,128)S(1)}, s32[1,64]{1,0:T(1,128)}, u32[]{:S(2)}) copy-start(s32[1,64]{1,0:T(1,128)} %param.20) | copy-start | bytes 772
  308.1 34.8 %copy-start.18 = (bf16[64,512]{1,0:T(8,128)(2,1)S(1)}, bf16[64,512]{1,0:T(8,128)(2,1)}, u32[]{:S(2)}) copy-start(bf16[64,512]{1,0:T(8,128)(2,1)} %shard_map.262) | copy-start | bytes 196612
  418.7 20.9 %copy-start.25 = (f32[1024]{0:T(1024)S(1)}, f32[1024]{0:T(1024)}, u32[]{:S(2)}) copy-start(f32[1024]{0:T(1024)} %get-tuple-element.144) | copy-start | bytes 12292
  418.8 214.6 %all-gather.5.cloned.1.call-start = ((), (), s32[]{:S(2)}) async-start(), calls=%async_computation.5 | async-start | bytes 4718592 | tf_op jit(solution)/shard_map/all_gather | solution.py:1984
  520.1 13.7 %copy-start.7 = (f32[1024,256]{1,0:T(8,128)S(1)}, f32[1024,256]{1,0:T(8,128)}, u32[]{:S(2)}) copy-start(f32[1024,256]{1,0:T(8,128)} %get-tuple-element.90) | copy-start | bytes 3145732
  520.1 13.7 %copy-start.9 = (f32[1024,24]{1,0:T(8,128)S(1)}, f32[1024,24]{1,0:T(8,128)}, u32[]{:S(2)}) copy-start(f32[1024,24]{1,0:T(8,128)} %get-tuple-element.170) | copy-start | bytes 294916
  520.2 13.7 %copy-start.35 = (f32[24]{0:T(128)S(1)}, f32[24]{0:T(128)}, u32[]{:S(2)}) copy-start(f32[24]{0:T(128)} %copy-done.34) | copy-start | bytes 292
  520.2 14.7 %copy-start.19 = (f32[64,1024]{1,0:T(8,128)S(1)}, f32[64,1024]{1,0:T(8,128)}, u32[]{:S(2)}) copy-start(f32[64,1024]{1,0:T(8,128)} %get-tuple-element.92) | copy-start | bytes 786436
  520.2 14.7 %copy-start.24 = (s32[1,64]{1,0:T(1,128)S(1)}, s32[1,64]{1,0:T(1,128)}, u32[]{:S(2)}) copy-start(s32[1,64]{1,0:T(1,128)} %param.20) | copy-start | bytes 772
  570.7 363.8 %reduce-scatter.5.cloned.1.call-start = ((), (), s32[]{:S(2)}) async-start(), calls=%async_computation.6 | async-start | bytes 3932160 | tf_op jit(solution)/shard_map/reduce_scatter | solution.py:2029
  571.9 21.9 %copy-start.11 = (s32[32768]{0:T(1024)}, s32[32768]{0:T(1024)S(1)}, u32[]{:S(2)}) copy-start(s32[32768]{0:T(1024)S(1)} %get-tuple-element.126.ids_ref) | copy-start | bytes 393220
  581.2 50.9 %collective-permute-start = (bf16[1024,256]{1,0:T(8,128)(2,1)}, bf16[1024,256]{1,0:T(8,128)(2,1)S(1)}, u32[]{:S(2)}, u32[]{:S(2)}) collective-permute-start(bf16[1024,256]{1,0:T(8,128)(2,1)} %get-tuple-element.133), channel_id=1, source_target_pairs={{0,8},{8,16},{16,24},{24,0},{1,9},{9,17},{17,25},{25,1},{2,10},{10... | collective-permute-start | bytes 1572872 | tf_op jit(solution)/shard_map/ppermute | solution.py:1729
  582.9 49.2 %collective-permute-start.2 = (bf16[1024,256]{1,0:T(8,128)(2,1)}, bf16[1024,256]{1,0:T(8,128)(2,1)S(1)}, u32[]{:S(2)}, u32[]{:S(2)}) collective-permute-start(bf16[1024,256]{1,0:T(8,128)(2,1)} %get-tuple-element.134), channel_id=1, source_target_pairs={{0,16},{8,24},{16,0},{24,8},{1,17},{9,25},{17,1},{25,9},{2,18},{10... | collective-permute-start | bytes 1572872 | tf_op jit(solution)/shard_map/ppermute | solution.py:1729
  585.2 46.9 %collective-permute-start.1 = (bf16[1024,256]{1,0:T(8,128)(2,1)S(1)}, bf16[1024,256]{1,0:T(8,128)(2,1)S(1)}, u32[]{:S(2)}, u32[]{:S(2)}) collective-permute-start(bf16[1024,256]{1,0:T(8,128)(2,1)S(1)} %get-tuple-element.135), channel_id=1, source_target_pairs={{0,24},{8,0},{16,8},{24,16},{1,25},{9,1},{17,9},{25,17},{2,26},{10... | collective-permute-start | bytes 1572872 | tf_op jit(solution)/shard_map/ppermute | solution.py:1729
  813.9 22.4 %copy-start.4 = (bf16[4160,256]{1,0:T(8,128)(2,1)S(1)}, bf16[4160,256]{1,0:T(8,128)(2,1)}, u32[]{:S(2)}) copy-start(bf16[4160,256]{1,0:T(8,128)(2,1)} %reduce-scatter.3.cloned.1.call-done) | copy-start | bytes 6389764
  (27 other events, 175.6 us)
Sparse Core Ops, SparseCore 0:
  115.5 195.9 all-gather.2
  418.9 146.7 reduce-scatter.2
  570.9 36.8 all-gather.4
  875.1 59.4 reduce-scatter.4

commit v6 on v5

--- a/solution.py
+++ b/solution.py
@@ -23,7 +23,7 @@
 QROWS = 256
 LANES = 128
 NO_TOKEN = 1 << 30
-LISTS = 4
+LISTS = 8
 TABLE_PARTS = 4
 PAD_ROWS = 16 * TABLE_PARTS
 GROUP = 4
@@ -143,7 +143,7 @@
 
 
 def sigmoid(values):
-    return 1.0 / (1.0 + jnp.exp(-values))
+    return 0.5 + 0.5 * jnp.tanh(0.5 * values)
 
 
 def gate_up_kernel(own_ref, x_ref, *rest):

time: 957 us -> 958 us (level)
  no operation moved by 1% of the time
where the time goes in v6:
time: 958 us; the launch traced here: 946 us
  Pallas kernels  696 us (73%)
  other arithmetic  62.9 us (7%)
  matrix products  60.8 us (6%)
  local copies, waits for them, and re-layouts  50.2 us (5%)
  waiting for transfers between devices  45.1 us (5%)
  between operations  21.9 us (2%)
    pallas_call x1, Pallas kernels, tail_exchange(): pl.pallas_call(functools.partial(tail_kernel, rows, cols, slots), in_spec...  177 us
    pallas_call x1, Pallas kernels, gather_weights(): pl.pallas_call(functools.partial(weights_kernel, rows, cols), in_specs=[p...  113 us
    pallas_call x1, Pallas kernels, front_exchange(): pl.pallas_call(functools.partial(front_kernel, rows, cols), in_specs=[pl....  91.5 us
    pallas_call x1, Pallas kernels, ssm_backward(): pl.pallas_call(ssm_bwd_kernel, grid_spec=pltpu.PrefetchScalarGridSpec(num...  50.3 us
    pallas_call x4, Pallas kernels, weight_grad(): pl.pallas_call(wgrad_kernel, grid_spec=pltpu.PrefetchScalarGridSpec(num_s...  45.4 us
    reduce_scatter x1, waiting for transfers between devices, body(): lax.psum_scatter(partial_update, 'row', scatter_dimension=1, tiled=True)  45 us
    pallas_call x6, Pallas kernels, slot_call(): pl.pallas_call(kernel, grid_spec=pltpu.PrefetchScalarGridSpec(num_scalar_...  40.7 us
    pallas_call x1, Pallas kernels, ssm_forward(): pl.pallas_call(ssm_fwd_kernel, grid_spec=pltpu.PrefetchScalarGridSpec(num...  31.7 us
  transfers between devices with their start and end apart: 8, of which 1 were waited for; matrix products, arithmetic and copies ran while one was open for 11% of the time, Pallas kernels for 39%

profile of v6, /device:TPU:0, one launch (start us, length us, event | category | flops | bytes accessed | tf_op | source)
XLA Modules:
  0.0 946.5 jit_solution(16495805890498849431)
XLA Ops:
  23.8 91.5 %shard_map.257 = (s32[2,2,2,2,2,17,128]{6,5,4,3,2,1,0:T(8,128)}, bf16[2,2,2,4,1040,256]{5,4,3,2,1,0:T(8,128)(2,1)}, bf16[2,2,6,256,256]{4,3,2,1,0:T(8,128)(2,1)}) custom-call(s32[17,128]{1,0:T(8,128)} %bitcast.198, bf16[4,1040,256]{2,1,0:T(8,128)(2,1)} %bitcast.156, bf16[6,256,256]{2,1,0:T(8,128)(2,1)} %convert_element_type.97.w_ref), custom_call_target="tpu_custom_call" | custom-call | flops 1048576 | bytes 34078720 | tf_op jit(solution)/shard_map/pallas_call | solution.py:1501
  116.6 25.1 %gather_fusion = bf16[4096,256]{1,0:T(8,128)(2,1)} fusion(bf16[33280,256]{1,0:T(8,128)(2,1)} %bitcast.157, s32[4096]{0:T(1024)S(1)} %broadcast_clamp_fusion), kind=kCustom, calls=%fused_computation | custom fusion | bytes 4210688 | tf_op jit(solution)/shard_map/jit(_take)/gather | solution.py:1802
  155.4 112.7 %shard_map.259 = bf16[4,2,2,2,6,256,256]{6,5,4,3,2,1,0:T(8,128)(2,1)} custom-call(bf16[4,6,256,256]{3,2,1,0:T(8,128)(2,1)} %bitcast.163), custom_call_target="tpu_custom_call" | custom-call | flops 1048576 | bytes 50331648 | tf_op jit(solution)/shard_map/pallas_call | solution.py:1578
  284.4 15.1 %shard_map.260.proj_ref.q_ref.k_ref.v_ref = f32[1024,4096]{1,0:T(8,128)} custom-call(s32[48]{0:T(128)} %own_ref.23, bf16[1024,1024]{1,0:T(8,128)(2,1)} %get-tuple-element.96.x_ref.l_ref, bf16[4,48,256,256]{3,2,1,0:T(8,128)(2,1)} %bitcast.123, bf16[4,48,256,256]{3,2,1,0:T(8,128)(2,1)} %bitcast.124, bf16[4,48,256,256]{3,2,1,0:T(8,128)(2,1)} %bitcast.125, ...), custom_call_target="tpu_custom_call" | custom-call | flops 8589934592 | bytes 18874368 | tf_op jit(solution)/shard_map/pallas_call | solution.py:110
  299.4 8.6 shard_map.262
  308.1 31.7 %shard_map.261 = (f32[1024,1536]{1,0:T(8,128)}, f32[8,128,1536]{2,1,0:T(8,128)}, f32[1024,1792]{1,0:T(8,128)}, f32[1024,1792]{1,0:T(8,128)}, bf16[1024,1536]{1,0:T(8,128)(2,1)}) custom-call(s32[8]{0:T(128)} %bitcast.210, f32[1024,4096]{1,0:T(8,128)} %shard_map.260.proj_ref.q_ref.k_ref.v_ref, f32[1024,8]{1,0:T(8,128)} %convert_element_type.99.near_ref, ...), custom_call_target="tpu_custom_call" | custom-call | flops 1610612736 | bytes 62914560 | tf_op jit(solution)/shard_map/pallas_call | solution.py:839
  360.6 13.7 %shard_map.266 = bf16[2,2,2,2,32,1024]{5,4,3,2,1,0:T(8,128)(2,1)} custom-call(bf16[2,32,1024]{2,1,0:T(8,128)(2,1)} %bitcast.181), custom_call_target="tpu_custom_call" | custom-call | flops 1024 | bytes 2097152 | tf_op jit(solution)/shard_map/pallas_call | solution.py:1641
  374.3 8.5 fusion.69
  395.6 10.7 %convolution_convert_fusion = bf16[4160,1024]{1,0:T(8,128)(2,1)} fusion(bf16[512,1024]{1,0:T(8,128)(2,1)S(1)} %bitcast.172, f32[512,4160]{0,1:T(8,128)} %copy-done.1, f32[512]{0:T(512)S(1)} %get-tuple-element.166, f32[512]{0:T(512)S(1)} %get-tuple-element.128, s32[512]{0:T(512)S(1)} %copy-done.33, pred[4160]{0:T(1024)(128)(4,1)S(1)} %iota_compare_fusion.15), kind=kOutput, calls=%fused_computation.1 | convolution fusion | flops 4381245440 | bytes 18098240 | tf_op jit(solution)/shard_map/rv,rd->vd/dot_general | solution.py:1905
  406.2 12.1 %fusion.62 = f32[512,1024]{1,0:T(8,128)} fusion(bf16[4160,1024]{1,0:T(8,128)(2,1)} %all-gather.3.cloned.1.call-done, f32[512,4160]{0,1:T(8,128)} %copy-done.1, f32[512]{0:T(512)S(1)} %get-tuple-element.166, f32[512]{0:T(512)S(1)} %get-tuple-element.128, s32[512]{0:T(512)S(1)} %copy-done.33, pred[4160]{0:T(1024)(128)(4,1)S(1)} %iota_compare_fusion.15), kind=kOutput, calls=%fused_computation.161 | convolution fusion | flops 4376985600 | bytes 19146816 | tf_op jit(solution)/shard_map/rv,vd->rd/dot_general | solution.py:1904
  420.4 18.8 %shard_map.268 = f32[2,32,1024]{2,1,0:T(8,128)} custom-call(f32[2,2,2,2,32,1024]{5,4,3,2,1,0:T(8,128)} %bitcast.165), custom_call_target="tpu_custom_call" | custom-call | flops 524288 | bytes 4194304 | tf_op jit(solution)/shard_map/pallas_call | solution.py:1699
  448.2 7.7 shard_map.270
  465.8 50.3 %shard_map.272 = (bf16[1024,4096]{1,0:T(8,128)(2,1)}, f32[1024,256]{1,0:T(8,128)}, f32[8,8,128]{2,1,0:T(8,128)}, f32[8,1792]{1,0:T(8,128)}) custom-call(s32[8]{0:T(128)} %bitcast.211, f32[1024,4096]{1,0:T(8,128)} %shard_map.260.proj_ref.q_ref.k_ref.v_ref, f32[1024,8]{1,0:T(8,128)} %convert_element_type.99.near_ref, f32[4,1792]{1,0:T(4,128)} %reshape.270.cw_ref, ...), custom_call_target="tpu_custom_call" | custom-call | flops 4831838208 | bytes 94371840 | tf_op jit(solution)/shard_map/pallas_call | solution.py:891
  519.5 13.6 %shard_map.273 = bf16[1024,4096]{1,0:T(8,128)(2,1)} custom-call(s32[64]{0:T(128)} %bitcast.185, f32[1024,4096]{1,0:T(8,128)} %shard_map.260.proj_ref.q_ref.k_ref.v_ref, f32[1024,4096]{1,0:T(8,128)} %shard_map.260.proj_ref.q_ref.k_ref.v_ref, f32[1024,4096]{1,0:T(8,128)} %shard_map.260.proj_ref.q_ref.k_ref.v_ref, ...), custom_call_target="tpu_custom_call", output_to_operand_aliasing={{}: (11, {})} | custom-call | flops 335544320 | bytes 10485760 | tf_op jit(solution)/shard_map/pallas_call | solution.py:570
  540.9 21.0 %shard_map.274 = (f32[1024,1024]{1,0:T(8,128)}, bf16[1024,1024]{1,0:T(8,128)(2,1)}, f32[1,1024]{1,0:T(1,128)}) custom-call(s32[48]{0:T(128)} %own_ref.23, bf16[1,1024,4096]{2,1,0:T(8,128)(2,1)} %bitcast.154, bf16[4,48,256,256]{3,2,1,0:T(8,128)(2,1)} %bitcast.149, bf16[4,48,256,256]{3,2,1,0:T(8,128)(2,1)} %bitcast.150, bf16[4,48,256,256]{3,2,1,0:T(8,128)(2,1)} %bitcast.151, ...), custom_call_target="tpu_custom_call" | custom-call | flops 8589934592 | bytes 16777216 | tf_op jit(solution)/shard_map/pallas_call | solution.py:279
  593.0 12.0 %shard_map.276.rest_0_ = bf16[4,48,256,256]{3,2,1,0:T(8,128)(2,1)} custom-call(s32[48]{0:T(128)} %own_ref.23, bf16[64,1024]{1,0:T(8,128)(2,1)} %get-tuple-element.98.x_ref.l_ref, bf16[2,64,2048]{2,1,0:T(8,128)(2,1)} %shard_map.269.rest_0_.rest_1_.r_ref, bf16[4,48,256,256]{3,2,1,0:T(8,128)(2,1)} %shard_map.275.rest_0_), custom_call_target="tpu_custom_call", output_to_operand_aliasing={{}: (3, {})} | custom-call | flops 536870912 | bytes 8912896 | tf_op jit(solution)/shard_map/pallas_call | solution.py:337
  612.0 19.4 %shard_map.278 = bf16[4,48,256,256]{3,2,1,0:T(8,128)(2,1)} custom-call(s32[48]{0:T(128)} %own_ref.23, bf16[1024,1024]{1,0:T(8,128)(2,1)} %get-tuple-element.96.x_ref.l_ref, bf16[1,1024,4096]{2,1,0:T(8,128)(2,1)} %bitcast.155, bf16[4,48,256,256]{3,2,1,0:T(8,128)(2,1)} %shard_map.277.rest_0_), custom_call_target="tpu_custom_call", output_to_operand_aliasing={{}: (3, {})} | custom-call | flops 8589934592 | bytes 16777216 | tf_op jit(solution)/shard_map/pallas_call | solution.py:337
  632.6 176.5 %shard_map.279 = (bf16[2,2,6,256,256]{4,3,2,1,0:T(8,128)(2,1)}, bf16[2,2,2,2,1536,256]{5,4,3,2,1,0:T(8,128)(2,1)}, f32[304,128]{1,0:T(8,128)}) custom-call(bf16[2,2,2,2,2,6,256,256]{7,6,5,4,3,2,1,0:T(8,128)(2,1)} %bitcast.153, bf16[2,1536,256]{2,1,0:T(8,128)(2,1)} %bitcast.160, f32[304,128]{1,0:T(8,128)} %pad_bitcast_fusion.v_ref), custom_call_target="tpu_custom_call" | custom-call | flops 12582912 | bytes 75497472 | tf_op jit(solution)/shard_map/pallas_call | solution.py:1360
  812.8 23.4 %shard_map.280 = f32[4098,256]{1,0:T(8,128)} custom-call(s32[32]{0:T(128)} %reduce_sum.212.lo_ref, s32[32]{0:T(128)} %reduce_sum.213.hi_ref, s32[32768]{0:T(1024)} %copy-done.11, bf16[8192,256]{1,0:T(8,128)(2,1)} %all-gather.5.cloned.1.call-done.rest_0_, bf16[24576,256]{1,0:T(8,128)(2,1)} %bitcast.158), custom_call_target="tpu_custom_call" | custom-call | flops 134217728 | bytes 8388608 | tf_op jit(solution)/shard_map/pallas_call | solution.py:1012
  842.0 10.7 %shard_map.281 = f32[8,128]{1,0:T(8,128)} custom-call(f32[8,128]{1,0:T(8,128)} %broadcast_in_dim.127.x_ref), custom_call_target="tpu_custom_call" | custom-call | flops 32768 | bytes 131072 | tf_op jit(solution)/shard_map/pallas_call | solution.py:1143
  855.2 8.7 shard_map.282.rot_ref
  864.5 10.4 %shard_map.283 = (f32[6,256,256]{2,1,0:T(8,128)}, f32[6,256,256]{2,1,0:T(8,128)}, bf16[6,1024,256]{2,1,0:T(8,128)(2,1)}) custom-call(f32[3]{0:T(128)} %pad_maximum_fusion.4.scale_ref, f32[6,256,256]{2,1,0:T(8,128)} %shard_map.282.rot_ref, f32[6,256,256]{2,1,0:T(8,128)} %m_ref.1, f32[6,256,256]{2,1,0:T(8,128)} %v_ref.1, f32[6,256,1024]{2,1,0:T(8,128)} %l_ref.3, ...), custom_call_target="tpu_custom_call" | custom-call | flops 2415919104 | bytes 11010048 | tf_op jit(solution)/shard_map/pallas_call | solution.py:1074
  877.0 12.5 %multiply_subtract_fusion = (f32[4098,256]{1,0:T(8,128)}, f32[4098,256]{1,0:T(8,128)}, f32[4098,256]{1,0:T(8,128)}) fusion(f32[4098,256]{1,0:T(8,128)} %param.30, f32[]{:T(128)} %bitcast.53, f32[]{:T(128)} %bitcast.52, f32[]{:T(128)} %min.3, f32[4098,256]{1,0:T(8,128)} %shard_map.280, bf16[4160,256]{1,0:T(8,128)(2,1)S(1)} %copy-done.4, ...), kind=kLoop, calls=%fused_computation.10 | loop fusion | flops 18883584 | bytes 31472652 | tf_op jit(solution)/shard_map/sub | solution.py:1743
  889.5 45.0 %reduce-scatter.5.cloned.1.call-done = bf16[6,256,256]{2,1,0:T(8,128)(2,1)} async-done(((bf16[6,1024,256]{2,1,0:T(8,128)(2,1)}), bf16[6,256,256]{2,1,0:T(8,128)(2,1)}) %reduce-scatter.5.cloned.1.call-update) | async-done | bytes 786448 | tf_op jit(solution)/shard_map/reduce_scatter | solution.py:2029
  (231 shorter events, 165.2 us)
Async XLA Ops:
  7.2 367.1 %all-gather.3.cloned.1.call-start = ((), (), s32[]{:S(2)}) async-start(), calls=%async_computation.3 | async-start | bytes 10649600 | tf_op jit(solution)/shard_map/all_gather | solution.py:1799
  21.6 93.7 %copy-start.30 = (s32[1024]{0:T(1024)}, s32[1024]{0:T(1024)S(1)}, u32[]{:S(2)}) copy-start(s32[1024]{0:T(1024)S(1)} %get-tuple-element.64) | copy-start | bytes 12292
  116.4 37.6 %copy-start.13 = (s32[4,8,2176]{2,1,0:T(8,128)}, s32[4,8,2176]{2,1,0:T(8,128)S(1)}, u32[]{:S(2)}) copy-start(s32[4,8,2176]{2,1,0:T(8,128)S(1)} %reshape.266) | copy-start | bytes 835588
  116.6 28.9 %copy-start.15 = (f32[38216]{0:T(1024)S(1)}, f32[38216]{0:T(1024)}, u32[]{:S(2)}) copy-start(f32[38216]{0:T(1024)} %param.33) | copy-start | bytes 458596
  141.7 131.4 %all-to-all-start = ((bf16[4,1024,256]{2,1,0:T(8,128)(2,1)}), bf16[4,1024,256]{2,1,0:T(8,128)(2,1)S(1)}, u32[]{:S(2)}, u32[]{:S(2)}) async-start(bf16[4,1024,256]{2,1,0:T(8,128)(2,1)} %bitcast.159), calls=%async_computation | async-start | bytes 4194304 | tf_op jit(solution)/shard_map/all_to_all | solution.py:1806
  145.5 421.7 %reduce-scatter.3.cloned.1.call-start = ((), (), s32[]{:S(2)}) async-start(), calls=%async_computation.4 | async-start | bytes 10649600 | tf_op jit(solution)/shard_map/reduce_scatter | solution.py:1908
  150.7 128.3 %copy-start.5 = (bf16[1024,24]{1,0:T(8,128)(2,1)}, bf16[1024,24]{1,0:T(8,128)(2,1)S(1)}, u32[]{:S(2)}) copy-start(bf16[1024,24]{1,0:T(8,128)(2,1)S(1)} %convert_element_type.100) | copy-start | bytes 147460
  272.5 26.9 %copy-start.34 = (f32[24]{0:T(128)}, f32[24]{0:T(128)S(1)}, u32[]{:S(2)}) copy-start(f32[24]{0:T(128)S(1)} %get-tuple-element.148) | copy-start | bytes 292
  283.3 16.1 %copy-start.10 = (f32[8,3,8,128]{3,2,0,1:T(8,128)}, f32[8,3,8,128]{3,2,0,1:T(8,128)S(1)}, u32[]{:S(2)}) copy-start(f32[8,3,8,128]{3,2,0,1:T(8,128)S(1)} %copy.131) | copy-start | bytes 294916
  308.1 31.7 %copy-start.23 = (s32[1,64]{1,0:T(1,128)S(1)}, s32[1,64]{1,0:T(1,128)}, u32[]{:S(2)}) copy-start(s32[1,64]{1,0:T(1,128)} %param.20) | copy-start | bytes 772
  308.1 34.4 %copy-start.18 = (bf16[64,512]{1,0:T(8,128)(2,1)S(1)}, bf16[64,512]{1,0:T(8,128)(2,1)}, u32[]{:S(2)}) copy-start(bf16[64,512]{1,0:T(8,128)(2,1)} %shard_map.262) | copy-start | bytes 196612
  418.4 20.9 %copy-start.25 = (f32[1024]{0:T(1024)S(1)}, f32[1024]{0:T(1024)}, u32[]{:S(2)}) copy-start(f32[1024]{0:T(1024)} %get-tuple-element.144) | copy-start | bytes 12292
  418.4 214.2 %all-gather.5.cloned.1.call-start = ((), (), s32[]{:S(2)}) async-start(), calls=%async_computation.5 | async-start | bytes 4718592 | tf_op jit(solution)/shard_map/all_gather | solution.py:1984
  519.4 13.7 %copy-start.7 = (f32[1024,256]{1,0:T(8,128)S(1)}, f32[1024,256]{1,0:T(8,128)}, u32[]{:S(2)}) copy-start(f32[1024,256]{1,0:T(8,128)} %get-tuple-element.90) | copy-start | bytes 3145732
  519.4 13.7 %copy-start.9 = (f32[1024,24]{1,0:T(8,128)S(1)}, f32[1024,24]{1,0:T(8,128)}, u32[]{:S(2)}) copy-start(f32[1024,24]{1,0:T(8,128)} %get-tuple-element.170) | copy-start | bytes 294916
  519.5 13.7 %copy-start.35 = (f32[24]{0:T(128)S(1)}, f32[24]{0:T(128)}, u32[]{:S(2)}) copy-start(f32[24]{0:T(128)} %copy-done.34) | copy-start | bytes 292
  519.5 14.8 %copy-start.19 = (f32[64,1024]{1,0:T(8,128)S(1)}, f32[64,1024]{1,0:T(8,128)}, u32[]{:S(2)}) copy-start(f32[64,1024]{1,0:T(8,128)} %get-tuple-element.92) | copy-start | bytes 786436
  519.5 14.7 %copy-start.24 = (s32[1,64]{1,0:T(1,128)S(1)}, s32[1,64]{1,0:T(1,128)}, u32[]{:S(2)}) copy-start(s32[1,64]{1,0:T(1,128)} %param.20) | copy-start | bytes 772
  570.1 364.4 %reduce-scatter.5.cloned.1.call-start = ((), (), s32[]{:S(2)}) async-start(), calls=%async_computation.6 | async-start | bytes 3932160 | tf_op jit(solution)/shard_map/reduce_scatter | solution.py:2029
  571.2 21.8 %copy-start.11 = (s32[32768]{0:T(1024)}, s32[32768]{0:T(1024)S(1)}, u32[]{:S(2)}) copy-start(s32[32768]{0:T(1024)S(1)} %get-tuple-element.126.ids_ref) | copy-start | bytes 393220
  580.5 50.8 %collective-permute-start = (bf16[1024,256]{1,0:T(8,128)(2,1)}, bf16[1024,256]{1,0:T(8,128)(2,1)S(1)}, u32[]{:S(2)}, u32[]{:S(2)}) collective-permute-start(bf16[1024,256]{1,0:T(8,128)(2,1)} %get-tuple-element.133), channel_id=1, source_target_pairs={{0,8},{8,16},{16,24},{24,0},{1,9},{9,17},{17,25},{25,1},{2,10},{10... | collective-permute-start | bytes 1572872 | tf_op jit(solution)/shard_map/ppermute | solution.py:1729
  582.1 49.2 %collective-permute-start.2 = (bf16[1024,256]{1,0:T(8,128)(2,1)}, bf16[1024,256]{1,0:T(8,128)(2,1)S(1)}, u32[]{:S(2)}, u32[]{:S(2)}) collective-permute-start(bf16[1024,256]{1,0:T(8,128)(2,1)} %get-tuple-element.134), channel_id=1, source_target_pairs={{0,16},{8,24},{16,0},{24,8},{1,17},{9,25},{17,1},{25,9},{2,18},{10... | collective-permute-start | bytes 1572872 | tf_op jit(solution)/shard_map/ppermute | solution.py:1729
  584.4 46.9 %collective-permute-start.1 = (bf16[1024,256]{1,0:T(8,128)(2,1)S(1)}, bf16[1024,256]{1,0:T(8,128)(2,1)S(1)}, u32[]{:S(2)}, u32[]{:S(2)}) collective-permute-start(bf16[1024,256]{1,0:T(8,128)(2,1)S(1)} %get-tuple-element.135), channel_id=1, source_target_pairs={{0,24},{8,0},{16,8},{24,16},{1,25},{9,1},{17,9},{25,17},{2,26},{10... | collective-permute-start | bytes 1572872 | tf_op jit(solution)/shard_map/ppermute | solution.py:1729
  812.8 23.4 %copy-start.4 = (bf16[4160,256]{1,0:T(8,128)(2,1)S(1)}, bf16[4160,256]{1,0:T(8,128)(2,1)}, u32[]{:S(2)}) copy-start(bf16[4160,256]{1,0:T(8,128)(2,1)} %reduce-scatter.3.cloned.1.call-done) | copy-start | bytes 6389764
  (27 other events, 175.6 us)
Sparse Core Ops, SparseCore 0:
  115.5 195.9 all-gather.2
  418.5 146.8 reduce-scatter.2
  570.2 36.7 all-gather.4
  875.0 59.4 reduce-scatter.4
